TPU v7x, 32 devices: a whole 2x2x4 slice. The times are simulated.
32 devices in a mesh: grp: 2 (over x), kb: 8 (over z, y), slab: 2 (over core).
Axes of the slice: x: 2, y: 2, z: 4, core: 2. Of those that a mesh axis runs over, the one named last changes fastest.
Arguments:
- orbitals: float32 [2, 16, 32, 1024], P(None, ('grp', 'kb'), 'slab'), parts along dimension 1, may hold values from -6 to 6
- kernel: float32 [8, 32, 1024], P(None, None, 'slab'), may hold values from 0.05 to 2
- q_index: int32 [8, 8], replicated, may hold values from 0 to 7, as said below
- owner: int32 [8], replicated, may hold values from 0 to 7, each once
Outputs:
- applied: float32 [2, 16, 32, 1024], P(None, ('grp', 'kb'), 'slab'), parts along dimension 1
- gram: float32 [2, 16, 1], P(None, ('grp', 'kb')), parts along dimension 1
There are 2 independent parts, one for each index of `grp`. A program takes and returns all parts, laid end to end along the dimension named above; an argument that names none is the same for every part. Nothing has to cross between parts.
Inputs may be any that keep to these rules, and one draw needn't show every extreme that they name: q_index[a, b] numbers the difference of k-points a and b among the 8 q vectors of the mesh: the table is symmetric, constant on its diagonal, and each row names every q once. `owner`: each block number appears once.
All inputs are finite; a program needn't handle non-finite values.
Results may differ from a plain program's by a relative error of at most 0.0003.
Values sent between devices are 32-bit elements; how exact they have to be, the bound alone decides.
No kernel may reach another device: no remote copies, remote signals or barrier semaphores. Data moves between devices by JAX's collectives and lax.ppermute only.
A program may use at most 128 MiB of HBM per device.

v0:
```python
import math

import jax
import jax.numpy as jnp
from jax import lax
from jax.sharding import PartitionSpec as P

NK = 8


highest = lax.Precision.HIGHEST


def dft_table(length):
    rows_idx = lax.broadcasted_iota(jnp.int32, (length, length), 0)
    cols_idx = lax.broadcasted_iota(jnp.int32, (length, length), 1)
    phase = (rows_idx * cols_idx % length).astype(jnp.float32) * (2.0 * math.pi / length)
    return (jnp.cos(phase), jnp.sin(phase))


def first_axis(real_part, imag_part, forward):
    length = real_part.shape[1]
    cosine, sine_table = dft_table(length)
    pattern = "nak,aw->nwk"
    real_cos = jnp.einsum(pattern, real_part, cosine, precision=highest)
    real_sin = jnp.einsum(pattern, real_part, sine_table, precision=highest)
    imag_cos = jnp.einsum(pattern, imag_part, cosine, precision=highest)
    imag_sin = jnp.einsum(pattern, imag_part, sine_table, precision=highest)
    if forward:
        return (real_cos + imag_sin, imag_cos - real_sin)
    return ((real_cos - imag_sin) / length, (imag_cos + real_sin) / length)


def plane_tables(side):
    total = side * side
    rows_idx = lax.broadcasted_iota(jnp.int32, (total, total), 0)
    cols_idx = lax.broadcasted_iota(jnp.int32, (total, total), 1)
    product = rows_idx // side * (cols_idx // side) + rows_idx % side * (cols_idx % side)
    phase = (product % side).astype(jnp.float32) * (2.0 * math.pi / side)
    cosine = jnp.cos(phase)
    sine_table = jnp.sin(phase)
    return (cosine, cosine - sine_table, cosine + sine_table)


def plane_transform(real_part, imag_part, tables, forward):
    cosine, minus_table, plus_table = tables
    total = cosine.shape[0]
    shape_kept = real_part.shape
    flat_re = real_part.reshape(-1, total)
    flat_im = imag_part.reshape(-1, total)
    common = jnp.dot(flat_re + flat_im, cosine, precision=highest)
    if forward:
        out_re = common - jnp.dot(flat_im, minus_table, precision=highest)
        out_im = common - jnp.dot(flat_re, plus_table, precision=highest)
    else:
        out_re = (common - jnp.dot(flat_im, plus_table, precision=highest)) / total
        out_im = (common - jnp.dot(flat_re, minus_table, precision=highest)) / total
    return (out_re.reshape(shape_kept), out_im.reshape(shape_kept))


def pair_densities(targets, partners):
    target_re = targets[0][:, None]
    target_im = targets[1][:, None]
    partner_re = partners[0][None]
    partner_im = partners[1][None]
    density_re = partner_re * target_re + partner_im * target_im
    density_im = partner_re * target_im - partner_im * target_re
    flat_shape = (-1,) + density_re.shape[2:]
    return (density_re.reshape(flat_shape), density_im.reshape(flat_shape))


def kernel_rows(kernel, kernel_choice):
    one_hot = (kernel_choice[:, None] == jnp.arange(kernel.shape[0], dtype=jnp.int32)[None]).astype(
        jnp.float32
    )
    return jnp.einsum("pq,qab->pab", one_hot, kernel, precision=highest)


def apply_partners(partners, potential_re, potential_im, target_count):
    block_shape = (target_count, partners.shape[1]) + partners.shape[2:]
    potential_re = potential_re.reshape(block_shape)
    potential_im = potential_im.reshape(block_shape)
    partner_re = partners[0][None]
    partner_im = partners[1][None]
    sum_re = jnp.sum(partner_re * potential_re - partner_im * potential_im, axis=1)
    sum_im = jnp.sum(partner_re * potential_im + partner_im * potential_re, axis=1)
    return jnp.stack([-sum_re / NK, -sum_im / NK])


def on_device(orbitals, kernel, q_index, owner):
    target_count = orbitals.shape[1]
    grid_side = kernel.shape[1]
    blocks_per_k = lax.axis_size("kb") // NK
    partners = lax.all_gather(orbitals, "kb", axis=1, tiled=True)
    partner_count = partners.shape[1]
    band_block = jnp.repeat(owner, target_count)
    band_kpoint = band_block // blocks_per_k
    own_kpoint = owner[lax.axis_index("kb")] // blocks_per_k
    difference_row = q_index[own_kpoint]
    kpoint_match = band_kpoint[:, None] == jnp.arange(NK, dtype=jnp.int32)[None]
    q_partner = jnp.sum(jnp.where(kpoint_match, difference_row[None], 0), axis=1)
    tables = plane_tables(grid_side)
    halves = lax.all_to_all(partners, "slab", split_axis=1, concat_axis=2, tiled=True)
    whole_targets, whole_kernel = (
        lax.all_gather(orbitals, "slab", axis=2, tiled=True),
        lax.all_gather(kernel, "slab", axis=2, tiled=True),
    )
    half_count = halves.shape[1]
    q_half = lax.dynamic_slice_in_dim(q_partner, lax.axis_index("slab") * half_count, half_count)
    density_re, density_im = pair_densities(whole_targets, halves)
    spec_re, spec_im = first_axis(density_re, density_im, True)
    spec_re, spec_im = plane_transform(spec_re, spec_im, tables, True)
    weights = kernel_rows(whole_kernel, jnp.tile(q_half, target_count))
    back_re, back_im = plane_transform(spec_re * weights, spec_im * weights, tables, False)
    back_re, back_im = first_axis(back_re, back_im, False)
    partial_terms = apply_partners(halves, back_re, back_im, target_count)
    applied = lax.psum_scatter(partial_terms, "slab", scatter_dimension=2, tiled=True)
    partner_re = partners[0]
    partner_im = partners[1]
    applied_re = applied[0]
    applied_im = applied[1]
    correlation_re = jnp.einsum(
        "pxa,txa->tp", partner_re, applied_re, precision=highest
    ) + jnp.einsum("pxa,txa->tp", partner_im, applied_im, precision=highest)
    correlation_im = jnp.einsum(
        "pxa,txa->tp", partner_re, applied_im, precision=highest
    ) - jnp.einsum("pxa,txa->tp", partner_im, applied_re, precision=highest)
    cells = grid_side * grid_side * grid_side
    correlation_sums = lax.psum((correlation_re / cells, correlation_im / cells), "slab")
    column_count = target_count * blocks_per_k
    band_column = (
        band_block % blocks_per_k * target_count
        + jnp.arange(partner_count, dtype=jnp.int32) % target_count
    )
    selected = (band_kpoint == own_kpoint)[:, None] & (
        band_column[:, None] == jnp.arange(column_count, dtype=jnp.int32)[None]
    )
    selector = jnp.where(selected, 1.0, 0.0).astype(jnp.float32)
    gram_re = jnp.dot(correlation_sums[0], selector, precision=highest)
    gram_im = jnp.dot(correlation_sums[1], selector, precision=highest)
    return (applied, jnp.stack([gram_re, gram_im]))


def solution(mesh):
    in_specs = (P(None, ("grp", "kb"), "slab", None), P(None, None, "slab"), P(), P())
    out_specs = (P(None, ("grp", "kb"), "slab", None), P(None, ("grp", "kb"), None))
    return jax.shard_map(
        on_device, mesh=mesh, in_specs=in_specs, out_specs=out_specs, check_vma=False
    )
```

profile of v0, /device:TPU:0, one launch (start us, length us, event | category | flops | bytes accessed | tf_op | source)
XLA Modules:
  0.0 222.6 jit_solution(2163058669979089143)
XLA Ops:
  7.2 0.0 copy-start
  7.2 0.0 copy-start.2
  7.2 0.0 copy-start.3
  7.2 0.0 all-gather.5.cloned.1.call-start
  7.2 2.1 copy.39
  9.4 0.0 all-gather.5.cloned.1.call-update
  9.4 0.0 all-gather.3.cloned.1.call-start
  9.5 0.7 all-gather.3.cloned.1.call-update
  10.2 0.0 reduce-scatter.2.cloned.1.call-start
  10.2 0.0 copy-done.3
  10.2 0.6 dynamic_slice.9
  12.8 0.2 select_reduce_fusion
  13.0 0.1 dynamic_slice.11
  13.1 2.1 all_gather.10
  15.2 6.2 %all-gather.5.cloned.1.call-done = f32[8,32,1024]{2,0,1:T(8,128)} async-done(((f32[8,32,512]{2,0,1:T(8,128)}), f32[8,32,1024]{2,0,1:T(8,128)}) %all-gather.5.cloned.1.call-update) | async-done | bytes 1048592 | tf_op jit(solution)/shard_map/all_gather | solution.py:106
  21.4 1.8 fusion.90
  23.2 41.6 %all-gather.3.cloned.1.call-done = f32[2,8,16,1024]{3,2,0,1:T(8,128)} async-done(((f32[2,1,16,1024]{3,2,0,1:T(8,128)}), f32[2,8,16,1024]{3,2,0,1:T(8,128)}) %all-gather.3.cloned.1.call-update) | async-done | bytes 1048592 | tf_op jit(solution)/shard_map/all_gather | solution.py:94
  64.8 5.7 %all_to_all.15 = f32[2,8,16,1024]{3,2,0,1:T(8,128)S(1)} all-to-all(f32[2,8,16,1024]{3,2,0,1:T(8,128)} %all-gather.3.cloned.1.call-done), channel_id=1, replica_groups=mesh['grp'=2,'kb'=8,'slab'=2] {'slab'}, dimensions={1} | all-to-all | bytes 2097152 | tf_op jit(solution)/shard_map/all_to_all | solution.py:103
  70.5 0.1 copy.69
  70.6 0.1 fusion.149
  70.7 0.7 fusion.52
  71.4 0.7 fusion.51
  72.0 0.7 convolution_subtract_fusion.1
  72.7 0.7 convolution_add_fusion.1
  73.4 19.1 %fusion.9 = f32[128,1024]{1,0:T(8,128)S(1)} fusion(s32[1024]{0:T(1024)S(1)} %get-tuple-element.19, s32[1024]{0:T(1024)S(1)} %get-tuple-element.20, pred[1024]{0:T(1024)(128)(4,1)S(1)} %get-tuple-element.22, s32[1024]{0:T(1024)S(1)} %get-tuple-element.18, s32[1024]{0:T(1024)S(1)} %get-tuple-element.21, pred[1024]{0:T(1024)(128)(4,1)S(1)} %get-tuple-element.23, ...), kind=kOutput, calls=%fused_computation.11 | convolution fusion | flops 1631715328 | bytes 1591296 | tf_op jit(solution)/shard_map/dot_general | solution.py:51
  92.6 20.3 %fusion.23 = f32[128,1024]{1,0:T(8,128)S(1)} fusion(f32[128,1024]{1,0:T(8,128)S(1)} %fusion.9, f32[128,1024]{1,0:T(8,128)S(1)} %bitcast.122, s32[1024]{0:T(1024)S(1)} %get-tuple-element.19, s32[1024]{0:T(1024)S(1)} %get-tuple-element.20, pred[1024]{0:T(1024)(128)(4,1)S(1)} %get-tuple-element.22, s32[1024]{0:T(1024)S(1)} %get-tuple-element.18, ...), kind=kOutput, calls=%fused_computation.24 | convolution fusion | flops 1632763904 | bytes 1591296 | tf_op jit(solution)/shard_map/dot_general | solution.py:54
  112.8 20.3 %fusion.32 = f32[128,1024]{1,0:T(8,128)S(1)} fusion(f32[128,1024]{1,0:T(8,128)S(1)} %fusion.9, f32[128,1024]{1,0:T(8,128)S(1)} %bitcast.120, s32[1024]{0:T(1024)S(1)} %get-tuple-element.19, s32[1024]{0:T(1024)S(1)} %get-tuple-element.20, pred[1024]{0:T(1024)(128)(4,1)S(1)} %get-tuple-element.22, s32[1024]{0:T(1024)S(1)} %get-tuple-element.18, ...), kind=kOutput, calls=%fused_computation.27 | convolution fusion | flops 1632763904 | bytes 1591296 | tf_op jit(solution)/shard_map/dot_general | solution.py:53
  133.1 0.4 copy_multiply_fusion
  133.5 19.0 %fusion.5 = f32[128,1024]{1,0:T(8,128)S(1)} fusion(s32[1024]{0:T(1024)S(1)} %get-tuple-element.19, s32[1024]{0:T(1024)S(1)} %get-tuple-element.20, pred[1024]{0:T(1024)(128)(4,1)S(1)} %get-tuple-element.22, s32[1024]{0:T(1024)S(1)} %get-tuple-element.18, s32[1024]{0:T(1024)S(1)} %get-tuple-element.21, pred[1024]{0:T(1024)(128)(4,1)S(1)} %get-tuple-element.23, ...), kind=kOutput, calls=%fused_computation.8 | convolution fusion | flops 1631715328 | bytes 1591296 | tf_op jit(solution)/shard_map/dot_general | solution.py:51
  152.5 20.3 %fusion.38 = f32[128,1024]{1,0:T(8,128)S(1)} fusion(f32[128,1024]{1,0:T(8,128)S(1)} %fusion.5, f32[128,1024]{1,0:T(8,128)S(1)} %bitcast.117, s32[1024]{0:T(1024)S(1)} %get-tuple-element.19, s32[1024]{0:T(1024)S(1)} %get-tuple-element.20, pred[1024]{0:T(1024)(128)(4,1)S(1)} %get-tuple-element.22, s32[1024]{0:T(1024)S(1)} %get-tuple-element.18, ...), kind=kOutput, calls=%fused_computation.29 | convolution fusion | flops 1632894976 | bytes 1591296 | tf_op jit(solution)/shard_map/dot_general | solution.py:57
  172.8 20.6 %fusion.29 = f32[128,1024]{1,0:T(8,128)S(1)} fusion(f32[128,1024]{1,0:T(8,128)S(1)} %fusion.5, f32[128,1024]{1,0:T(8,128)S(1)} %bitcast.113, s32[1024]{0:T(1024)S(1)} %get-tuple-element.19, s32[1024]{0:T(1024)S(1)} %get-tuple-element.20, pred[1024]{0:T(1024)(128)(4,1)S(1)} %get-tuple-element.22, s32[1024]{0:T(1024)S(1)} %get-tuple-element.18, ...), kind=kOutput, calls=%fused_computation.26 | convolution fusion | flops 1632894976 | bytes 1591296 | tf_op jit(solution)/shard_map/dot_general | solution.py:56
  193.3 0.7 fusion.64
  194.0 0.7 fusion.66
  194.7 0.7 fusion.22
  195.3 0.9 subtract_reduce_fusion
  196.2 0.7 pad_maximum_fusion
  197.0 0.0 reduce-scatter.2.cloned.1.call-update
  197.0 0.5 copy-done.1
  197.5 0.1 slice_bitcast_fusion.1
  197.6 5.9 %reduce-scatter.2.cloned.1.call-done = f32[2,1,16,1024]{3,2,1,0:T(8,128)} async-done(((f32[2,1,32,1024]{3,2,1,0:T(8,128)}), f32[2,1,16,1024]{3,2,1,0:T(8,128)}) %reduce-scatter.2.cloned.1.call-update) | async-done | bytes 131088 | tf_op jit(solution)/shard_map/reduce_scatter | solution.py:117
  203.6 0.9 slice_bitcast_fusion.5
  204.4 1.4 convolution_bitcast_fusion
  205.9 1.4 convolution_bitcast_fusion.2
  207.3 1.4 fusion.44
  208.7 1.5 fusion.42
  210.2 2.5 %all-reduce = (f32[8]{0:T(128)S(1)}, f32[8]{0:T(128)S(1)}) all-reduce(f32[8]{0:T(128)S(1)} %fusion.42, f32[8]{0:T(128)S(1)} %fusion.44), channel_id=1, replica_groups=mesh['grp'=2,'kb'=8,'slab'=2] {'slab'}, use_global_device_ids=true, to_apply=%region_4.5 | all-reduce | flops 16 | bytes 128 | tf_op jit(solution)/shard_map/psum | solution.py:129
  212.7 1.3 multiply_reduce_fusion.1
  213.9 1.8 pad_maximum_fusion.1
  (10 shorter events, 0.1 us)
Async XLA Ops:
  7.2 5.6 %copy-start = (s32[8,8]{1,0:T(8,128)S(1)}, s32[8,8]{1,0:T(8,128)}, u32[]{:S(2)}) copy-start(s32[8,8]{1,0:T(8,128)} %param.6) | copy-start | bytes 772
  7.2 5.9 %copy-start.2 = (f32[2,1,16,1024]{3,2,1,0:T(8,128)S(1)}, f32[2,1,16,1024]{3,2,1,0:T(8,128)}, u32[]{:S(2)}) copy-start(f32[2,1,16,1024]{3,2,1,0:T(8,128)} %param.4) | copy-start | bytes 393220
  7.2 3.0 %copy-start.3 = (s32[8]{0:T(128)S(1)}, s32[8]{0:T(128)}, u32[]{:S(2)}) copy-start(s32[8]{0:T(128)} %param.7) | copy-start | bytes 100
  7.2 14.2 %all-gather.5.cloned.1.call-start = ((), (), s32[]{:S(2)}) async-start(), calls=%async_computation.3 | async-start | bytes 1572864 | tf_op jit(solution)/shard_map/all_gather | solution.py:106
  9.4 55.4 %all-gather.3.cloned.1.call-start = ((), (), s32[]{:S(2)}) async-start(), calls=%async_computation.2 | async-start | bytes 1179648 | tf_op jit(solution)/shard_map/all_gather | solution.py:94
  10.2 193.4 %reduce-scatter.2.cloned.1.call-start = ((), (), s32[]{:S(2)}) async-start(), calls=%async_computation.4 | async-start | bytes 393216 | tf_op jit(solution)/shard_map/reduce_scatter | solution.py:117
  196.2 1.3 copy-start.1
Sparse Core Ops, SparseCore 0:
  9.6 11.7 all-gather.4
  23.5 41.3 all-gather.2
  197.1 6.4 reduce-scatter.1
where the time goes:
time: 227 us; the launch traced here: 223 us
  matrix products  133 us (59%)
  waiting for transfers between devices  54.5 us (24%)
  between operations  16.2 us (7%)
  blocking collectives  10.2 us (4%)
  local copies, waits for them, and re-layouts  4.54 us (2%)
  other arithmetic  4.38 us (2%)
    all_gather x1, waiting for transfers between devices, on_device(): partners = lax.all_gather(orbitals, 'kb', axis=1, tiled=True)  41.6 us
    dot_general x2, matrix products, plane_transform(): common = jnp.dot(flat_re + flat_im, cosine, precision=highest)  38.1 us
    dot_general x1, matrix products, plane_transform(): out_re = (common - jnp.dot(flat_im, plus_table, precision=highest)) / total  20.6 us
    dot_general x1, matrix products, plane_transform(): out_re = common - jnp.dot(flat_im, minus_table, precision=highest)  20.3 us
    dot_general x1, matrix products, plane_transform(): out_im = (common - jnp.dot(flat_re, minus_table, precision=highest)) / total  20.3 us
    dot_general x1, matrix products, plane_transform(): out_im = common - jnp.dot(flat_re, plus_table, precision=highest)  20.3 us
    all_gather x1, waiting for transfers between devices, on_device(): lax.all_gather(kernel, 'slab', axis=2, tiled=True)  6.19 us
    reduce_scatter x1, waiting for transfers between devices, on_device(): lax.psum_scatter(partial_terms, 'slab', scatter_dimension=2, tiled=True)  5.94 us
  transfers between devices with their start and end apart: 3, of which 3 were waited for; matrix products, arithmetic and copies ran while one was open for 1% of the time, Pallas kernels for 0%

commit v1 on v0

v1 whole, which is shorter than its diff:
```python
import functools
import math

import jax
import jax.numpy as jnp
import numpy as np
from jax import lax
from jax.experimental import pallas as pl
from jax.experimental.pallas import tpu as pltpu
from jax.sharding import PartitionSpec as P

NK = 8
LANES = 128
F32 = jnp.float32
BF16 = jnp.bfloat16


def bf16_parts(table):
    high = table.astype(np.float32).astype(BF16)
    low = (table - high.astype(np.float64)).astype(np.float32).astype(BF16)
    return np.stack([high, low])


def lane_table(side):
    lows = LANES // side
    index = np.arange(LANES)
    low, z = index // side, index % side
    phase = 2.0 * math.pi * (np.outer(low, low) / lows + np.outer(z, z) / side)
    real, imag = np.cos(phase), -np.sin(phase)
    return np.block([[real, imag], [-imag, real]])


def sublane_table(side, count):
    index = np.arange(side)
    phase = 2.0 * math.pi * (np.outer(index, index) % side) / side
    unit = np.eye(count)
    cosine, sine = np.kron(unit, np.cos(phase)), np.kron(unit, np.sin(phase))
    return np.block([[cosine, sine], [-sine, cosine]])


def twist_table(side, rows):
    tiles = side * side // LANES
    phase = 2.0 * math.pi * np.outer(np.arange(tiles), np.arange(LANES) // side) / side
    both = np.stack([np.cos(phase), np.sin(phase)], 1).astype(np.float32)
    return np.ascontiguousarray(np.broadcast_to(both[:, :, None], (tiles, 2, rows, LANES)))


def split(value):
    high = value.astype(BF16)
    return high, (value - high.astype(F32)).astype(BF16)


def dot_parts(left, right):
    dot = functools.partial(jnp.dot, preferred_element_type=F32)
    return dot(left[0], right[0]) + (dot(left[1], right[0]) + dot(left[0], right[1]))


def dft_list(values, sign):
    count = len(values)
    if count == 1:
        return values
    even, odd = dft_list(values[0::2], sign), dft_list(values[1::2], sign)
    first, second = [], []
    for k in range(count // 2):
        re, im = odd[k]
        eighth = 8 * k // count if 8 * k % count == 0 else None
        if eighth == 0:
            pass
        elif eighth == 2:
            re, im = (-im, re) if sign > 0 else (im, -re)
        elif eighth == 1:
            root = math.sqrt(0.5)
            re, im = (
                ((re - im) * root, (re + im) * root)
                if sign > 0
                else ((re + im) * root, (im - re) * root)
            )
        elif eighth == 3:
            root = math.sqrt(0.5)
            re, im = (
                ((-re - im) * root, (re - im) * root)
                if sign > 0
                else ((im - re) * root, (-re - im) * root)
            )
        else:
            angle = 2.0 * math.pi * k / count
            cosine, sine = math.cos(angle), sign * math.sin(angle)
            re, im = re * cosine - im * sine, re * sine + im * cosine
        first.append((even[k][0] + re, even[k][1] + im))
        second.append((even[k][0] - re, even[k][1] - im))
    return first + second


def lane_slice(tile):
    return pl.ds(tile * LANES, LANES)


def choose_kernel(side, choice_ref, core_ref, mine_ref, other_ref, out_ref):
    tiles = side * side // LANES
    lows = LANES // side
    scale = -1.0 / (NK * side**3)
    first_core = core_ref[0] == 0
    lane = lax.broadcasted_iota(jnp.int32, (side, LANES), 1) // side
    for pair in range(out_ref.shape[0]):
        q = choice_ref[pair]
        mine, other = mine_ref[q], other_ref[q]
        low_half = jnp.where(first_core, mine, other) * scale
        high_half = jnp.where(first_core, other, mine) * scale
        for b in range(tiles):
            total = None
            for a in range(lows):
                row = a * tiles + b
                source, chunk = row // lows, row % lows
                half = low_half if source < tiles // 2 else high_half
                at = source % (tiles // 2) * LANES
                piece = half[:, at : at + LANES]
                shift = (a - chunk) % lows * side
                if shift:
                    piece = pltpu.roll(piece, shift, 1)
                total = piece if total is None else jnp.where(lane == a, piece, total)
            out_ref[pair, :, lane_slice(b)] = total


def pair_kernel(
    side, count, has_sum, *refs
):
    refs = list(refs)
    take = lambda n: [refs.pop(0) for _ in range(n)]
    target = take(2)
    partners = [take(2) for _ in range(count)]
    (weight_ref,) = take(1)
    lane_f, lane_b, rows_f, rows_b, twist = take(5)
    sums = take(2) if has_sum else None
    outs = take(2)
    a_high, a_low, y_ref, f_high, f_low, g_ref = take(6)

    tiles = side * side // LANES
    half = side // 2
    rows = side * count

    def parts(ref):
        return ref[0], ref[1]

    for p in range(count):
        for h in range(2):
            row = p * side + h * half
            values = []
            for t in range(tiles):
                t_re, t_im = target[h][0, 0, :, lane_slice(t)], target[h][1, 0, :, lane_slice(t)]
                p_re = partners[p][h][0, 0, :, lane_slice(t)]
                p_im = partners[p][h][1, 0, :, lane_slice(t)]
                values.append((p_re * t_re + p_im * t_im, p_re * t_im - p_im * t_re))
            for b, (re, im) in enumerate(dft_list(values, -1)):
                if b:
                    cosine, sine = twist[b, 0], twist[b, 1]
                    re, im = re * cosine + im * sine, im * cosine - re * sine
                at = pl.ds(b * rows + row, half)
                for k, part in enumerate((re, im)):
                    high, low = split(part)
                    a_high[at, lane_slice(k)] = high
                    a_low[at, lane_slice(k)] = low
    y_ref[...] = dot_parts((a_high[...], a_low[...]), parts(lane_f))
    for n in range(tiles // 2):
        blocks = []
        for k in range(2):
            blocks.append(
                jnp.concatenate(
                    [y_ref[pl.ds((2 * n + j) * rows, rows), lane_slice(k)] for j in range(2)], 1
                )
            )
        spectrum = dot_parts(parts(rows_f), split(jnp.concatenate(blocks, 0)))
        weights = weight_ref[:, :, pl.ds(n * 2 * LANES, 2 * LANES)].reshape(rows, 2 * LANES)
        weighted = spectrum * jnp.concatenate([weights, weights], 0)
        back = dot_parts(parts(rows_b), split(weighted))
        high, low = split(back)
        for j in range(2):
            for k in range(2):
                at = (pl.ds((2 * n + j) * rows, rows), lane_slice(k))
                f_high[at] = high[k * rows : (k + 1) * rows, j * LANES : (j + 1) * LANES]
                f_low[at] = low[k * rows : (k + 1) * rows, j * LANES : (j + 1) * LANES]
    g_ref[...] = dot_parts((f_high[...], f_low[...]), parts(lane_b))
    gram_re = jnp.zeros((half, LANES), F32)
    gram_im = jnp.zeros((half, LANES), F32)
    for h in range(2):
        total = [[0.0, 0.0] for _ in range(tiles)]
        if has_sum:
            for t in range(tiles):
                total[t] = [sums[h][pl.ds((k * tiles + t) * half, half), :] for k in range(2)]
        for p in range(count):
            row = p * side + h * half
            values = []
            for b in range(tiles):
                at = pl.ds(b * rows + row, half)
                re, im = g_ref[at, lane_slice(0)], g_ref[at, lane_slice(1)]
                if b:
                    cosine, sine = twist[b, 0], twist[b, 1]
                    re, im = re * cosine - im * sine, im * cosine + re * sine
                values.append((re, im))
            for t, (re, im) in enumerate(dft_list(values, 1)):
                p_re = partners[p][h][0, 0, :, lane_slice(t)]
                p_im = partners[p][h][1, 0, :, lane_slice(t)]
                total[t][0] = total[t][0] + (p_re * re - p_im * im)
                total[t][1] = total[t][1] + (p_re * im + p_im * re)
        for t in range(tiles):
            re, im = total[t]
            t_re, t_im = target[h][0, 0, :, lane_slice(t)], target[h][1, 0, :, lane_slice(t)]
            gram_re += t_re * re + t_im * im
            gram_im += t_re * im - t_im * re
            outs[h][pl.ds(t * half, half), :] = re
            outs[h][pl.ds((tiles + t) * half, half), :] = im
    end = 2 * tiles * half
    scale = 1.0 / side**3
    sums_row = jnp.concatenate(
        [
            jnp.full((4, LANES), jnp.sum(gram_re) * scale, F32),
            jnp.full((4, LANES), jnp.sum(gram_im) * scale, F32),
        ],
        0,
    )
    for h in range(2):
        outs[h][pl.ds(end, 8), :] = sums_row


def join_kernel(flag_ref, mine_ref, near_ref, away_mine_ref, away_near_ref, applied_ref, gram_ref):
    half = applied_ref.shape[2]
    tiles = applied_ref.shape[3] // LANES
    own = flag_ref[0] == 1
    for k in range(2):
        for t in range(tiles):
            at = pl.ds((k * tiles + t) * half, half)
            applied_ref[k, 0, :, lane_slice(t)] = jnp.where(
                own, mine_ref[at, :], near_ref[at, :]
            ) + jnp.where(own, away_mine_ref[at, :], away_near_ref[at, :])
    end = 2 * tiles * half
    at = pl.ds(end, 8)
    sums = jnp.where(own, mine_ref[at, :], near_ref[at, :]) + jnp.where(
        own, away_mine_ref[at, :], away_near_ref[at, :]
    )
    gram_ref[0, 0, 0] = jnp.max(sums[0:1, :])
    gram_ref[1, 0, 0] = jnp.max(sums[4:5, :])


VMEM = pl.BlockSpec(memory_space=pltpu.VMEM)
SMEM = pl.BlockSpec(memory_space=pltpu.SMEM)


def params():
    return pltpu.CompilerParams(vmem_limit_bytes=48 * 2**20)


def choose(choice, core, mine, other, side):
    return pl.pallas_call(
        functools.partial(choose_kernel, side),
        out_shape=jax.ShapeDtypeStruct((choice.shape[0], side, side * side), F32),
        in_specs=[SMEM, SMEM, VMEM, VMEM],
        out_specs=VMEM,
        compiler_params=params(),
        name="choose",
    )(choice, core, mine, other)


def apply_pairs(target, partners, weights, side, sums=None):
    count = len(partners)
    half = side // 2
    tiles = side * side // LANES
    rows = side * count
    lane = lane_table(side)
    across = sublane_table(side, count)
    tables = [
        jnp.asarray(bf16_parts(lane)),
        jnp.asarray(bf16_parts(lane.T)),
        jnp.asarray(bf16_parts(across)),
        jnp.asarray(bf16_parts(across.T)),
        jnp.asarray(twist_table(side, half)),
    ]
    operands = list(target) + [x for pair in partners for x in pair] + [weights] + tables
    operands += list(sums) if sums is not None else []
    message = jax.ShapeDtypeStruct((2 * tiles * half + 8, LANES), F32)
    return pl.pallas_call(
        functools.partial(pair_kernel, side, count, sums is not None),
        out_shape=(message, message),
        in_specs=[VMEM] * len(operands),
        out_specs=(VMEM, VMEM),
        scratch_shapes=[
            pltpu.VMEM((tiles * rows, 2 * LANES), BF16),
            pltpu.VMEM((tiles * rows, 2 * LANES), BF16),
            pltpu.VMEM((tiles * rows, 2 * LANES), F32),
            pltpu.VMEM((tiles * rows, 2 * LANES), BF16),
            pltpu.VMEM((tiles * rows, 2 * LANES), BF16),
            pltpu.VMEM((tiles * rows, 2 * LANES), F32),
        ],
        compiler_params=params(),
        name="pairs",
    )(*operands)


def join(flag, parts, shape):
    return pl.pallas_call(
        join_kernel,
        out_shape=(jax.ShapeDtypeStruct(shape, F32), jax.ShapeDtypeStruct((2, 1, 1), F32)),
        in_specs=[SMEM, VMEM, VMEM, VMEM, VMEM],
        out_specs=(VMEM, SMEM),
        compiler_params=params(),
        name="join",
    )(flag, *parts)


def block_gram(orbitals, applied, owner, blocks_per_k, cells):
    highest = lax.Precision.HIGHEST
    partners = lax.all_gather(orbitals, "kb", axis=1, tiled=True)
    re = jnp.einsum("pxa,txa->tp", partners[0], applied[0], precision=highest)
    re += jnp.einsum("pxa,txa->tp", partners[1], applied[1], precision=highest)
    im = jnp.einsum("pxa,txa->tp", partners[0], applied[1], precision=highest)
    im -= jnp.einsum("pxa,txa->tp", partners[1], applied[0], precision=highest)
    sums = lax.psum(jnp.stack([re, im]) / cells, "slab")
    own = owner[lax.axis_index("kb")] // blocks_per_k
    wanted = own * blocks_per_k + jnp.arange(blocks_per_k, dtype=jnp.int32)
    selector = jnp.where(owner[:, None] == wanted[None], 1.0, 0.0).astype(F32)
    return jnp.einsum("ktp,pc->ktc", sums, selector, precision=highest)


def on_device(orbitals, kernel, q_index, owner):
    side = kernel.shape[1]
    n_kb = lax.axis_size("kb")
    lines = n_kb // 2
    blocks_per_k = n_kb // NK
    place, core = lax.axis_index("kb"), lax.axis_index("slab")
    column, line = place % 2, place // 2

    def swap(x):
        return lax.ppermute(x, "slab", [(0, 1), (1, 0)])

    def from_line(x, d):
        return lax.ppermute(
            x, "kb", [(2 * a + c, 2 * (a ^ d) + c) for a in range(lines) for c in range(2)]
        )

    beside = lax.ppermute(orbitals, "kb", [(a, a ^ 1) for a in range(n_kb)])
    mine = [orbitals] + [from_line(orbitals, d) for d in range(1, lines)]
    partners = [(x, swap(x)) for x in mine]
    home = core == column
    target_mine = jnp.where(home, orbitals, beside)
    target_sent = jnp.where(home, beside, orbitals)
    target = (target_mine, swap(target_sent))

    k_of = owner // blocks_per_k
    target_k = k_of[2 * line + core]
    partner_at = 2 * (line ^ jnp.arange(lines, dtype=jnp.int32)) + column
    choice = q_index[target_k][k_of[partner_at]]
    weights = choose(choice, core[None].astype(jnp.int32), kernel, swap(kernel), side)

    sums = None
    step = min(4, lines)
    for at in range(0, lines, step):
        sums = apply_pairs(target, partners[at : at + step], weights[at : at + step], side, sums)
    own_part, other_part = sums

    def index(line_at, column_at, core_at):
        return (2 * line_at + column_at) * 2 + core_at

    both = ("kb", "slab")
    away_mine = lax.ppermute(
        own_part,
        both,
        [(index(m, y, 1 - y), index(m, 1 - y, 1 - y)) for m in range(lines) for y in range(2)],
    )
    away_near = lax.ppermute(
        other_part,
        both,
        [(index(m, y, 1 - y), index(m, 1 - y, y)) for m in range(lines) for y in range(2)],
    )
    near = lax.ppermute(
        other_part,
        both,
        [(index(m, y, y), index(m, y, 1 - y)) for m in range(lines) for y in range(2)],
    )
    applied, gram = join(
        home[None].astype(jnp.int32), (own_part, near, away_mine, away_near), orbitals.shape
    )
    if blocks_per_k > 1:
        gram = block_gram(orbitals, applied, owner, blocks_per_k, side**3)
    return applied, gram


def solution(mesh):
    in_specs = (P(None, ("grp", "kb"), "slab", None), P(None, None, "slab"), P(), P())
    out_specs = (P(None, ("grp", "kb"), "slab", None), P(None, ("grp", "kb"), None))
    return jax.shard_map(
        on_device, mesh=mesh, in_specs=in_specs, out_specs=out_specs, check_vma=False
    )
```

time: 227 us -> 36.3 us (0.16)
  the two profiles are of different devices: /device:TPU:0 before, /device:TPU:1 now
where the time goes in v1:
time: 36.3 us; the launch traced here: 36.1 us
  starting transfers between devices  21.9 us (60%)
  Pallas kernels  5.29 us (15%)
  local copies, waits for them, and re-layouts  3.24 us (9%)
  between operations  2.86 us (8%)
  waiting for transfers between devices  2.69 us (7%)
    ppermute x6, starting transfers between devices, swap(): return lax.ppermute(x, 'slab', [(0, 1), (1, 0)])  8.32 us
    ppermute x1, starting transfers between devices, on_device(): lax.ppermute(other_part, both, [(index(m, y, 1 - y), index(m, 1 - y, y))...  3.76 us
    ppermute x3, starting transfers between devices, from_line(): lax.ppermute(x, 'kb', [(2 * a + c, 2 * (a ^ d) + c) for a in range(lines)...  3.61 us
    pallas_call x1, Pallas kernels, apply_pairs(): pl.pallas_call(functools.partial(pair_kernel, side, count, sums is not No...  3.54 us
    ppermute x1, starting transfers between devices, on_device(): lax.ppermute(own_part, both, [(index(m, y, 1 - y), index(m, 1 - y, 1 - y)...  2.82 us
    ppermute x1, waiting for transfers between devices, on_device(): lax.ppermute(other_part, both, [(index(m, y, 1 - y), index(m, 1 - y, y))...  2.66 us
    ppermute x1, starting transfers between devices, on_device(): beside = lax.ppermute(orbitals, 'kb', [(a, a ^ 1) for a in range(n_kb)])  2.13 us
    ppermute x1, starting transfers between devices, on_device(): lax.ppermute(other_part, both, [(index(m, y, y), index(m, y, 1 - y)) for...  1.29 us
  transfers between devices with their start and end apart: 13, of which 1 were waited for; matrix products, arithmetic and copies ran while one was open for 5% of the time, Pallas kernels for 3%

profile of v1, /device:TPU:1, one launch (start us, length us, event | category | flops | bytes accessed | tf_op | source)
XLA Modules:
  0.0 36.1 jit_solution(7847936151181132157)
XLA Ops:
  0.6 0.0 copy-start
  0.6 2.1 %collective-permute-start = (f32[2,1,16,1024]{3,2,1,0:T(8,128)}, f32[2,1,16,1024]{3,2,1,0:T(8,128)S(1)}, u32[]{:S(2)}, u32[]{:S(2)}) collective-permute-start(f32[2,1,16,1024]{3,2,1,0:T(8,128)} %refs_2_.1), channel_id=1, source_target_pairs={{0,2},{2,0},{4,6},{6,4},{8,10},{10,8},{12,14},{14,12},{1,3},{3,1},... | collective-permute-start | bytes 393224 | tf_op jit(solution)/shard_map/ppermute | solution.py:338
  2.8 1.3 %collective-permute-start.3 = (f32[2,1,16,1024]{3,2,1,0:T(8,128)}, f32[2,1,16,1024]{3,2,1,0:T(8,128)S(1)}, u32[]{:S(2)}, u32[]{:S(2)}) collective-permute-start(f32[2,1,16,1024]{3,2,1,0:T(8,128)} %refs_2_.1), channel_id=1, source_target_pairs={{0,4},{2,6},{4,0},{6,2},{8,12},{10,14},{12,8},{14,10},{1,5},{3,7},... | collective-permute-start | bytes 393224 | tf_op jit(solution)/shard_map/ppermute | solution.py:334
  4.1 2.3 %collective-permute-start.5 = (f32[2,1,16,1024]{3,2,1,0:T(8,128)}, f32[2,1,16,1024]{3,2,1,0:T(8,128)S(1)}, u32[]{:S(2)}, u32[]{:S(2)}) collective-permute-start(f32[2,1,16,1024]{3,2,1,0:T(8,128)} %refs_2_.1), channel_id=1, source_target_pairs={{0,8},{2,10},{4,12},{6,14},{8,0},{10,2},{12,4},{14,6},{1,9},{3,11}... | collective-permute-start | bytes 393224 | tf_op jit(solution)/shard_map/ppermute | solution.py:334
  6.4 0.0 collective-permute-start.7
  6.4 1.7 %collective-permute-start.9 = (f32[8,32,512]{2,1,0:T(8,128)}, f32[8,32,512]{2,1,0:T(8,128)S(1)}, u32[]{:S(2)}, u32[]{:S(2)}) collective-permute-start(f32[8,32,512]{2,1,0:T(8,128)} %mine_ref.1), channel_id=1, source_target_pairs={{0,1},{1,0},{2,3},{3,2},{4,5},{5,4},{6,7},{7,6},{8,9},{9,8},{10,11... | collective-permute-start | bytes 1572872 | tf_op jit(solution)/shard_map/ppermute | solution.py:331
  8.1 0.7 %copy-done.8 = s32[8]{0:T(128)S(1)} copy-done((s32[8]{0:T(128)S(1)}, s32[8]{0:T(128)}, u32[]{:S(2)}) %copy-start.8) | copy-done | bytes 56
  8.8 0.6 %dynamic_slice.6 = s32[1]{0:T(128)} dynamic-slice(s32[8]{0:T(128)S(1)} %copy-done.8, s32[]{:T(128)S(6)} %select_n.57), dynamic_slice_sizes={1} | dynamic-slice | bytes 12 | tf_op jit(solution)/shard_map/dynamic_slice | solution.py:347
  10.7 0.0 copy-start.1
  10.7 0.6 %gather_fusion = s32[4]{0:T(128)S(1)} fusion(s32[8]{0:T(128)S(1)} %copy-done.8, s32[1024]{0:T(1024)S(1)} %pad_clamp_fusion.1), kind=kCustom, calls=%fused_computation | custom fusion | bytes 48 | tf_op jit(solution)/shard_map/gather | solution.py:349
  12.0 0.0 copy-start.2
  12.0 0.0 collective-permute-done
  12.0 0.0 copy-done.1
  12.1 0.1 collective-permute-start.2
  12.2 0.0 collective-permute-done.3.refs_4_
  12.2 0.6 %collective-permute-start.1 = (f32[2,1,16,1024]{3,2,1,0:T(8,128)S(1)}, f32[2,1,16,1024]{3,2,1,0:T(8,128)S(1)}, u32[]{:S(2)}, u32[]{:S(2)}) collective-permute-start(f32[2,1,16,1024]{3,2,1,0:T(8,128)S(1)} %get-tuple-element.10), channel_id=1, source_target_pairs={{0,1},{1,0},{2,3},{3,2},{4,5},{5,4},{6,7},{7,6},{8,9},{9,8},{10,11... | collective-permute-start | bytes 393224 | tf_op jit(solution)/shard_map/ppermute | solution.py:331
  12.7 0.0 collective-permute-done.5.refs_6_
  12.7 5.5 %collective-permute-start.4 = (f32[2,1,16,1024]{3,2,1,0:T(8,128)S(1)}, f32[2,1,16,1024]{3,2,1,0:T(8,128)S(1)}, u32[]{:S(2)}, u32[]{:S(2)}) collective-permute-start(f32[2,1,16,1024]{3,2,1,0:T(8,128)S(1)} %collective-permute-done.3.refs_4_), channel_id=1, source_target_pairs={{0,1},{1,0},{2,3},{3,2},{4,5},{5,4},{6,7},{7,6},{8,9},{9,8},{10,11... | collective-permute-start | bytes 393224 | tf_op jit(solution)/shard_map/ppermute | solution.py:331
  18.2 0.0 collective-permute-done.7.refs_8_
  18.2 0.0 collective-permute-start.6
  18.2 0.0 collective-permute-done.9.other_ref
  18.2 0.5 %collective-permute-start.8 = (f32[2,1,16,1024]{3,2,1,0:T(8,128)S(1)}, f32[2,1,16,1024]{3,2,1,0:T(8,128)S(1)}, u32[]{:S(2)}, u32[]{:S(2)}) collective-permute-start(f32[2,1,16,1024]{3,2,1,0:T(8,128)S(1)} %collective-permute-done.7.refs_8_), channel_id=1, source_target_pairs={{0,1},{1,0},{2,3},{3,2},{4,5},{5,4},{6,7},{7,6},{8,9},{9,8},{10,11... | collective-permute-start | bytes 393224 | tf_op jit(solution)/shard_map/ppermute | solution.py:331
  18.7 0.0 copy-done
  18.7 0.6 %gather_fusion.1 = s32[4]{0:T(128)S(1)} fusion(s32[8]{0:T(128)S(1)} %dynamic-slice_bitcast_fusion, s32[1024]{0:T(1024)S(1)} %pad_clamp_fusion), kind=kCustom, calls=%fused_computation.1 | custom fusion | bytes 48 | tf_op jit(solution)/shard_map/gather | solution.py:349
  19.4 0.0 copy-done.2
  19.4 0.0 copy-start.5
  19.4 0.0 copy-start.6
  19.4 0.0 copy-start.7
  19.4 1.0 %choose.1.refs_10_ = f32[4,32,1024]{2,1,0:T(8,128)S(1)} custom-call(s32[4]{0:T(128)S(1)} %gather_fusion.1, s32[1]{0:T(128)} %bitcast.6.core_ref, f32[8,32,512]{2,1,0:T(8,128)S(1)} %copy-done.2, f32[8,32,512]{2,1,0:T(8,128)S(1)} %collective-permute-done.9.other_ref), custom_call_target="tpu_custom_call" | custom-call | tf_op jit(solution)/shard_map/choose/pallas_call | solution.py:252
  20.4 0.0 collective-permute-done.2.refs_3_
  20.4 0.0 collective-permute-done.1.refs_1_
  20.5 0.0 collective-permute-done.4.refs_5_
  20.5 0.0 collective-permute-done.6.refs_7_
  20.5 0.0 collective-permute-done.8.refs_9_
  20.5 0.0 copy-done.3
  20.5 0.0 copy-done.4
  20.5 0.0 copy-done.5
  20.5 0.0 copy-done.6
  20.6 0.0 copy-done.7
  20.6 3.5 %pairs.1 = (f32[264,128]{1,0:T(8,128)S(1)}, f32[264,128]{1,0:T(8,128)S(1)}) custom-call(f32[2,1,16,1024]{3,2,1,0:T(8,128)S(1)} %get-tuple-element.11.refs_0_, f32[2,1,16,1024]{3,2,1,0:T(8,128)S(1)} %collective-permute-done.1.refs_1_, f32[2,1,16,1024]{3,2,1,0:T(8,128)S(1)} %copy-done.1, f32[2,1,16,1024]{3,2,1,0:T(8,128)S(1)} %collective-permute-done.2.refs_3_, ...), custom_call_target="tpu_custom_call" | custom-call | tf_op jit(solution)/shard_map/pairs/pallas_call | solution.py:279
  24.1 1.3 %collective-permute-start.10 = (f32[264,128]{1,0:T(8,128)S(1)}, f32[264,128]{1,0:T(8,128)S(1)}, u32[]{:S(2)}, u32[]{:S(2)}) collective-permute-start(f32[264,128]{1,0:T(8,128)S(1)} %get-tuple-element.5), channel_id=1, source_target_pairs={{0,1},{3,2},{4,5},{7,6},{8,9},{11,10},{12,13},{15,14},{16,17},{19,... | collective-permute-start | bytes 405512 | tf_op jit(solution)/shard_map/ppermute | solution.py:372
  25.4 2.8 %collective-permute-start.11 = (f32[264,128]{1,0:T(8,128)S(1)}, f32[264,128]{1,0:T(8,128)S(1)}, u32[]{:S(2)}, u32[]{:S(2)}) collective-permute-start(f32[264,128]{1,0:T(8,128)S(1)} %get-tuple-element.4.mine_ref), channel_id=1, source_target_pairs={{1,3},{2,0},{5,7},{6,4},{9,11},{10,8},{13,15},{14,12},{17,19},{18,... | collective-permute-start | bytes 405512 | tf_op jit(solution)/shard_map/ppermute | solution.py:362
  28.3 3.8 %collective-permute-start.12 = (f32[264,128]{1,0:T(8,128)S(1)}, f32[264,128]{1,0:T(8,128)S(1)}, u32[]{:S(2)}, u32[]{:S(2)}) collective-permute-start(f32[264,128]{1,0:T(8,128)S(1)} %get-tuple-element.5), channel_id=1, source_target_pairs={{1,2},{2,1},{5,6},{6,5},{9,10},{10,9},{13,14},{14,13},{17,18},{18,... | collective-permute-start | bytes 405512 | tf_op jit(solution)/shard_map/ppermute | solution.py:367
  32.0 0.0 collective-permute-done.10.near_ref
  32.1 0.0 collective-permute-done.11.away_mine_ref
  32.1 2.7 %collective-permute-done.12.away_near_ref = f32[264,128]{1,0:T(8,128)S(1)} collective-permute-done((f32[264,128]{1,0:T(8,128)S(1)}, f32[264,128]{1,0:T(8,128)S(1)}, u32[]{:S(2)}, u32[]{:S(2)}) %collective-permute-start.12) | collective-permute-done | bytes 135200 | tf_op jit(solution)/shard_map/ppermute | solution.py:367
  34.7 0.7 %join.1 = (f32[2,1,16,1024]{3,2,1,0:T(8,128)}, f32[2,1,1]{2,1,0:T(1,128)S(1)}) custom-call(s32[1]{0:T(128)} %bitcast.flag_ref, f32[264,128]{1,0:T(8,128)S(1)} %get-tuple-element.4.mine_ref, f32[264,128]{1,0:T(8,128)S(1)} %collective-permute-done.10.near_ref, f32[264,128]{1,0:T(8,128)S(1)} %collective-permute-done.11.away_mine_ref, ...), custom_call_target="tpu_custom_call" | custom-call | tf_op jit(solution)/shard_map/join/pallas_call | solution.py:298
  35.5 0.6 %copy.12 = f32[2,1,1]{0,2,1:T(1,128)} copy(f32[2,1,1]{2,1,0:T(1,128)S(1)} %get-tuple-element.9) | data formatting | bytes 16 | tf_op jit(solution)/shard_map/join/pallas_call | solution.py:298
  (9 shorter events, 0.1 us)
Async XLA Ops:
  0.6 18.1 %copy-start = (s32[8,8]{1,0:T(8,128)S(1)}, s32[8,8]{1,0:T(8,128)}, u32[]{:S(2)}) copy-start(s32[8,8]{1,0:T(8,128)} %param.11) | copy-start | bytes 772
  0.6 11.4 %collective-permute-start = (f32[2,1,16,1024]{3,2,1,0:T(8,128)}, f32[2,1,16,1024]{3,2,1,0:T(8,128)S(1)}, u32[]{:S(2)}, u32[]{:S(2)}) collective-permute-start(f32[2,1,16,1024]{3,2,1,0:T(8,128)} %refs_2_.1), channel_id=1, source_target_pairs={{0,2},{2,0},{4,6},{6,4},{8,10},{10,8},{12,14},{14,12},{1,3},{3,1},... | collective-permute-start | bytes 393224 | tf_op jit(solution)/shard_map/ppermute | solution.py:338
  2.8 9.4 %collective-permute-start.3 = (f32[2,1,16,1024]{3,2,1,0:T(8,128)}, f32[2,1,16,1024]{3,2,1,0:T(8,128)S(1)}, u32[]{:S(2)}, u32[]{:S(2)}) collective-permute-start(f32[2,1,16,1024]{3,2,1,0:T(8,128)} %refs_2_.1), channel_id=1, source_target_pairs={{0,4},{2,6},{4,0},{6,2},{8,12},{10,14},{12,8},{14,10},{1,5},{3,7},... | collective-permute-start | bytes 393224 | tf_op jit(solution)/shard_map/ppermute | solution.py:334
  4.1 8.7 %collective-permute-start.5 = (f32[2,1,16,1024]{3,2,1,0:T(8,128)}, f32[2,1,16,1024]{3,2,1,0:T(8,128)S(1)}, u32[]{:S(2)}, u32[]{:S(2)}) collective-permute-start(f32[2,1,16,1024]{3,2,1,0:T(8,128)} %refs_2_.1), channel_id=1, source_target_pairs={{0,8},{2,10},{4,12},{6,14},{8,0},{10,2},{12,4},{14,6},{1,9},{3,11}... | collective-permute-start | bytes 393224 | tf_op jit(solution)/shard_map/ppermute | solution.py:334
  6.4 11.8 %collective-permute-start.7 = (f32[2,1,16,1024]{3,2,1,0:T(8,128)}, f32[2,1,16,1024]{3,2,1,0:T(8,128)S(1)}, u32[]{:S(2)}, u32[]{:S(2)}) collective-permute-start(f32[2,1,16,1024]{3,2,1,0:T(8,128)} %refs_2_.1), channel_id=1, source_target_pairs={{0,12},{2,14},{4,8},{6,10},{8,4},{10,6},{12,0},{14,2},{1,13},{3,15... | collective-permute-start | bytes 393224 | tf_op jit(solution)/shard_map/ppermute | solution.py:334
  6.4 11.8 %collective-permute-start.9 = (f32[8,32,512]{2,1,0:T(8,128)}, f32[8,32,512]{2,1,0:T(8,128)S(1)}, u32[]{:S(2)}, u32[]{:S(2)}) collective-permute-start(f32[8,32,512]{2,1,0:T(8,128)} %mine_ref.1), channel_id=1, source_target_pairs={{0,1},{1,0},{2,3},{3,2},{4,5},{5,4},{6,7},{7,6},{8,9},{9,8},{10,11... | collective-permute-start | bytes 1572872 | tf_op jit(solution)/shard_map/ppermute | solution.py:331
  8.1 0.7 %copy-start.8 = (s32[8]{0:T(128)S(1)}, s32[8]{0:T(128)}, u32[]{:S(2)}) copy-start(s32[8]{0:T(128)} %param.12) | copy-start | bytes 100
  10.7 1.3 %copy-start.1 = (f32[2,1,16,1024]{3,2,1,0:T(8,128)S(1)}, f32[2,1,16,1024]{3,2,1,0:T(8,128)}, u32[]{:S(2)}) copy-start(f32[2,1,16,1024]{3,2,1,0:T(8,128)} %refs_2_.1) | copy-start | bytes 393220
  12.0 7.3 %copy-start.2 = (f32[8,32,512]{2,1,0:T(8,128)S(1)}, f32[8,32,512]{2,1,0:T(8,128)}, u32[]{:S(2)}) copy-start(f32[8,32,512]{2,1,0:T(8,128)} %mine_ref.1) | copy-start | bytes 1572868
  12.1 8.4 %collective-permute-start.2 = (f32[2,1,16,1024]{3,2,1,0:T(8,128)S(1)}, f32[2,1,16,1024]{3,2,1,0:T(8,128)S(1)}, u32[]{:S(2)}, u32[]{:S(2)}) collective-permute-start(f32[2,1,16,1024]{3,2,1,0:T(8,128)S(1)} %copy-done.1), channel_id=1, source_target_pairs={{0,1},{1,0},{2,3},{3,2},{4,5},{5,4},{6,7},{7,6},{8,9},{9,8},{10,11... | collective-permute-start | bytes 393224 | tf_op jit(solution)/shard_map/ppermute | solution.py:331
  12.2 8.3 %collective-permute-start.1 = (f32[2,1,16,1024]{3,2,1,0:T(8,128)S(1)}, f32[2,1,16,1024]{3,2,1,0:T(8,128)S(1)}, u32[]{:S(2)}, u32[]{:S(2)}) collective-permute-start(f32[2,1,16,1024]{3,2,1,0:T(8,128)S(1)} %get-tuple-element.10), channel_id=1, source_target_pairs={{0,1},{1,0},{2,3},{3,2},{4,5},{5,4},{6,7},{7,6},{8,9},{9,8},{10,11... | collective-permute-start | bytes 393224 | tf_op jit(solution)/shard_map/ppermute | solution.py:331
  12.7 7.7 %collective-permute-start.4 = (f32[2,1,16,1024]{3,2,1,0:T(8,128)S(1)}, f32[2,1,16,1024]{3,2,1,0:T(8,128)S(1)}, u32[]{:S(2)}, u32[]{:S(2)}) collective-permute-start(f32[2,1,16,1024]{3,2,1,0:T(8,128)S(1)} %collective-permute-done.3.refs_4_), channel_id=1, source_target_pairs={{0,1},{1,0},{2,3},{3,2},{4,5},{5,4},{6,7},{7,6},{8,9},{9,8},{10,11... | collective-permute-start | bytes 393224 | tf_op jit(solution)/shard_map/ppermute | solution.py:331
  18.2 2.3 %collective-permute-start.6 = (f32[2,1,16,1024]{3,2,1,0:T(8,128)S(1)}, f32[2,1,16,1024]{3,2,1,0:T(8,128)S(1)}, u32[]{:S(2)}, u32[]{:S(2)}) collective-permute-start(f32[2,1,16,1024]{3,2,1,0:T(8,128)S(1)} %collective-permute-done.5.refs_6_), channel_id=1, source_target_pairs={{0,1},{1,0},{2,3},{3,2},{4,5},{5,4},{6,7},{7,6},{8,9},{9,8},{10,11... | collective-permute-start | bytes 393224 | tf_op jit(solution)/shard_map/ppermute | solution.py:331
  18.2 2.3 %collective-permute-start.8 = (f32[2,1,16,1024]{3,2,1,0:T(8,128)S(1)}, f32[2,1,16,1024]{3,2,1,0:T(8,128)S(1)}, u32[]{:S(2)}, u32[]{:S(2)}) collective-permute-start(f32[2,1,16,1024]{3,2,1,0:T(8,128)S(1)} %collective-permute-done.7.refs_8_), channel_id=1, source_target_pairs={{0,1},{1,0},{2,3},{3,2},{4,5},{5,4},{6,7},{7,6},{8,9},{9,8},{10,11... | collective-permute-start | bytes 393224 | tf_op jit(solution)/shard_map/ppermute | solution.py:331
  19.4 1.1 %copy-start.3 = (bf16[2,256,256]{2,1,0:T(8,128)(2,1)S(1)}, bf16[2,256,256]{2,1,0:T(8,128)(2,1)}, u32[]{:S(2)}) copy-start(bf16[2,256,256]{2,1,0:T(8,128)(2,1)} %constant.59.clone.refs_11_) | copy-start | bytes 786436
  19.4 1.1 %copy-start.4 = (bf16[2,256,256]{2,1,0:T(8,128)(2,1)S(1)}, bf16[2,256,256]{2,1,0:T(8,128)(2,1)}, u32[]{:S(2)}) copy-start(bf16[2,256,256]{2,1,0:T(8,128)(2,1)} %constant.60.clone.refs_12_) | copy-start | bytes 786436
  19.4 1.1 %copy-start.5 = (bf16[2,256,256]{2,1,0:T(8,128)(2,1)S(1)}, bf16[2,256,256]{2,1,0:T(8,128)(2,1)}, u32[]{:S(2)}) copy-start(bf16[2,256,256]{2,1,0:T(8,128)(2,1)} %constant.61.clone.refs_13_) | copy-start | bytes 786436
  19.4 1.2 %copy-start.6 = (bf16[2,256,256]{2,1,0:T(8,128)(2,1)S(1)}, bf16[2,256,256]{2,1,0:T(8,128)(2,1)}, u32[]{:S(2)}) copy-start(bf16[2,256,256]{2,1,0:T(8,128)(2,1)} %constant.62.clone.refs_14_) | copy-start | bytes 786436
  19.4 1.2 %copy-start.7 = (f32[8,2,16,128]{3,2,1,0:T(8,128)S(1)}, f32[8,2,16,128]{3,2,1,0:T(8,128)}, u32[]{:S(2)}) copy-start(f32[8,2,16,128]{3,2,1,0:T(8,128)} %constant.63.clone.refs_15_) | copy-start | bytes 393220
  24.1 7.9 %collective-permute-start.10 = (f32[264,128]{1,0:T(8,128)S(1)}, f32[264,128]{1,0:T(8,128)S(1)}, u32[]{:S(2)}, u32[]{:S(2)}) collective-permute-start(f32[264,128]{1,0:T(8,128)S(1)} %get-tuple-element.5), channel_id=1, source_target_pairs={{0,1},{3,2},{4,5},{7,6},{8,9},{11,10},{12,13},{15,14},{16,17},{19,... | collective-permute-start | bytes 405512 | tf_op jit(solution)/shard_map/ppermute | solution.py:372
  25.4 6.6 %collective-permute-start.11 = (f32[264,128]{1,0:T(8,128)S(1)}, f32[264,128]{1,0:T(8,128)S(1)}, u32[]{:S(2)}, u32[]{:S(2)}) collective-permute-start(f32[264,128]{1,0:T(8,128)S(1)} %get-tuple-element.4.mine_ref), channel_id=1, source_target_pairs={{1,3},{2,0},{5,7},{6,4},{9,11},{10,8},{13,15},{14,12},{17,19},{18,... | collective-permute-start | bytes 405512 | tf_op jit(solution)/shard_map/ppermute | solution.py:362
  28.3 6.4 %collective-permute-start.12 = (f32[264,128]{1,0:T(8,128)S(1)}, f32[264,128]{1,0:T(8,128)S(1)}, u32[]{:S(2)}, u32[]{:S(2)}) collective-permute-start(f32[264,128]{1,0:T(8,128)S(1)} %get-tuple-element.5), channel_id=1, source_target_pairs={{1,2},{2,1},{5,6},{6,5},{9,10},{10,9},{13,14},{14,13},{17,18},{18,... | collective-permute-start | bytes 405512 | tf_op jit(solution)/shard_map/ppermute | solution.py:367

commit v2 on v1

--- a/solution.py
+++ b/solution.py
@@ -95,14 +95,17 @@
     return pl.ds(tile * LANES, LANES)
 
 
-def choose_kernel(side, choice_ref, core_ref, mine_ref, other_ref, out_ref):
+def weight_kernel(side, blocks_per_k, order, q_ref, owner_ref, mine_ref, other_ref, weight_ref):
     tiles = side * side // LANES
     lows = LANES // side
     scale = -1.0 / (NK * side**3)
-    first_core = core_ref[0] == 0
+    place, core = lax.axis_index("kb"), lax.axis_index("slab")
+    line, column = place // 2, place % 2
+    first_core = core == 0
+    target_k = owner_ref[2 * line + core] // blocks_per_k
     lane = lax.broadcasted_iota(jnp.int32, (side, LANES), 1) // side
-    for pair in range(out_ref.shape[0]):
-        q = choice_ref[pair]
+    for pair, d in enumerate(order):
+        q = q_ref[target_k, owner_ref[2 * (line ^ d) + column] // blocks_per_k]
         mine, other = mine_ref[q], other_ref[q]
         low_half = jnp.where(first_core, mine, other) * scale
         high_half = jnp.where(first_core, other, mine) * scale
@@ -118,21 +121,19 @@
                 if shift:
                     piece = pltpu.roll(piece, shift, 1)
                 total = piece if total is None else jnp.where(lane == a, piece, total)
-            out_ref[pair, :, lane_slice(b)] = total
-
-
-def pair_kernel(
-    side, count, has_sum, *refs
-):
+            weight_ref[pair, :, lane_slice(b)] = total
+
+
+def pair_kernel(side, count, first, has_sum, *refs):
     refs = list(refs)
     take = lambda n: [refs.pop(0) for _ in range(n)]
-    target = take(2)
+    own, beside = take(2), take(2)
     partners = [take(2) for _ in range(count)]
     (weight_ref,) = take(1)
     lane_f, lane_b, rows_f, rows_b, twist = take(5)
     sums = take(2) if has_sum else None
     outs = take(2)
-    a_high, a_low, y_ref, f_high, f_low, g_ref = take(6)
+    target, a_high, a_low, y_ref, f_high, f_low, g_ref = take(7)
 
     tiles = side * side // LANES
     half = side // 2
@@ -141,12 +142,15 @@
     def parts(ref):
         return ref[0], ref[1]
 
+    home = lax.axis_index("kb") % 2 == lax.axis_index("slab")
+    for h in range(2):
+        target[h] = jnp.where(home, own[h][:, 0], beside[h][:, 0])
     for p in range(count):
         for h in range(2):
             row = p * side + h * half
             values = []
             for t in range(tiles):
-                t_re, t_im = target[h][0, 0, :, lane_slice(t)], target[h][1, 0, :, lane_slice(t)]
+                t_re, t_im = target[h, 0, :, lane_slice(t)], target[h, 1, :, lane_slice(t)]
                 p_re = partners[p][h][0, 0, :, lane_slice(t)]
                 p_im = partners[p][h][1, 0, :, lane_slice(t)]
                 values.append((p_re * t_re + p_im * t_im, p_re * t_im - p_im * t_re))
@@ -169,7 +173,8 @@
                 )
             )
         spectrum = dot_parts(parts(rows_f), split(jnp.concatenate(blocks, 0)))
-        weights = weight_ref[:, :, pl.ds(n * 2 * LANES, 2 * LANES)].reshape(rows, 2 * LANES)
+        weights = weight_ref[first : first + count, :, pl.ds(n * 2 * LANES, 2 * LANES)]
+        weights = weights.reshape(rows, 2 * LANES)
         weighted = spectrum * jnp.concatenate([weights, weights], 0)
         back = dot_parts(parts(rows_b), split(weighted))
         high, low = split(back)
@@ -203,7 +208,7 @@
                 total[t][1] = total[t][1] + (p_re * im + p_im * re)
         for t in range(tiles):
             re, im = total[t]
-            t_re, t_im = target[h][0, 0, :, lane_slice(t)], target[h][1, 0, :, lane_slice(t)]
+            t_re, t_im = target[h, 0, :, lane_slice(t)], target[h, 1, :, lane_slice(t)]
             gram_re += t_re * re + t_im * im
             gram_im += t_re * im - t_im * re
             outs[h][pl.ds(t * half, half), :] = re
@@ -221,45 +226,46 @@
         outs[h][pl.ds(end, 8), :] = sums_row
 
 
-def join_kernel(flag_ref, mine_ref, near_ref, away_mine_ref, away_near_ref, applied_ref, gram_ref):
+def join_kernel(own_ref, near_ref, away_ref, applied_ref, gram_ref):
     half = applied_ref.shape[2]
     tiles = applied_ref.shape[3] // LANES
-    own = flag_ref[0] == 1
+    home = lax.axis_index("kb") % 2 == lax.axis_index("slab")
     for k in range(2):
         for t in range(tiles):
             at = pl.ds((k * tiles + t) * half, half)
-            applied_ref[k, 0, :, lane_slice(t)] = jnp.where(
-                own, mine_ref[at, :], near_ref[at, :]
-            ) + jnp.where(own, away_mine_ref[at, :], away_near_ref[at, :])
-    end = 2 * tiles * half
-    at = pl.ds(end, 8)
-    sums = jnp.where(own, mine_ref[at, :], near_ref[at, :]) + jnp.where(
-        own, away_mine_ref[at, :], away_near_ref[at, :]
-    )
+            applied_ref[k, 0, :, lane_slice(t)] = (
+                jnp.where(home, own_ref[at, :], near_ref[at, :]) + away_ref[at, :]
+            )
+    at = pl.ds(2 * tiles * half, 8)
+    sums = jnp.where(home, own_ref[at, :], near_ref[at, :]) + away_ref[at, :]
     gram_ref[0, 0, 0] = jnp.max(sums[0:1, :])
-    gram_ref[1, 0, 0] = jnp.max(sums[4:5, :])
+    gram_ref[0, 0, 1] = jnp.max(sums[4:5, :])
 
 
 VMEM = pl.BlockSpec(memory_space=pltpu.VMEM)
 SMEM = pl.BlockSpec(memory_space=pltpu.SMEM)
 
 
+COST = pl.CostEstimate(flops=2*10**10, bytes_accessed=10**8, transcendentals=0)
+
+
 def params():
     return pltpu.CompilerParams(vmem_limit_bytes=48 * 2**20)
 
 
-def choose(choice, core, mine, other, side):
+def choose_weights(q_index, owner, kernels, order, side, blocks_per_k):
     return pl.pallas_call(
-        functools.partial(choose_kernel, side),
-        out_shape=jax.ShapeDtypeStruct((choice.shape[0], side, side * side), F32),
+        functools.partial(weight_kernel, side, blocks_per_k, order),
+        out_shape=jax.ShapeDtypeStruct((len(order), side, side * side), F32),
         in_specs=[SMEM, SMEM, VMEM, VMEM],
         out_specs=VMEM,
         compiler_params=params(),
-        name="choose",
-    )(choice, core, mine, other)
-
-
-def apply_pairs(target, partners, weights, side, sums=None):
+        cost_estimate=COST,
+        name="weights",
+    )(q_index, owner, *kernels)
+
+
+def apply_pairs(own, beside, partners, weights, first, side, sums=None):
     count = len(partners)
     half = side // 2
     tiles = side * side // LANES
@@ -273,15 +279,16 @@
         jnp.asarray(bf16_parts(across.T)),
         jnp.asarray(twist_table(side, half)),
     ]
-    operands = list(target) + [x for pair in partners for x in pair] + [weights] + tables
+    operands = [*own, *beside] + [x for pair in partners for x in pair] + [weights] + tables
     operands += list(sums) if sums is not None else []
     message = jax.ShapeDtypeStruct((2 * tiles * half + 8, LANES), F32)
     return pl.pallas_call(
-        functools.partial(pair_kernel, side, count, sums is not None),
+        functools.partial(pair_kernel, side, count, first, sums is not None),
         out_shape=(message, message),
         in_specs=[VMEM] * len(operands),
         out_specs=(VMEM, VMEM),
         scratch_shapes=[
+            pltpu.VMEM((2, 2, half, side * side), F32),
             pltpu.VMEM((tiles * rows, 2 * LANES), BF16),
             pltpu.VMEM((tiles * rows, 2 * LANES), BF16),
             pltpu.VMEM((tiles * rows, 2 * LANES), F32),
@@ -290,19 +297,22 @@
             pltpu.VMEM((tiles * rows, 2 * LANES), F32),
         ],
         compiler_params=params(),
+        cost_estimate=COST,
         name="pairs",
     )(*operands)
 
 
-def join(flag, parts, shape):
-    return pl.pallas_call(
+def join(own, near, away, shape):
+    applied, gram = pl.pallas_call(
         join_kernel,
-        out_shape=(jax.ShapeDtypeStruct(shape, F32), jax.ShapeDtypeStruct((2, 1, 1), F32)),
-        in_specs=[SMEM, VMEM, VMEM, VMEM, VMEM],
+        out_shape=(jax.ShapeDtypeStruct(shape, F32), jax.ShapeDtypeStruct((1, 1, 2), F32)),
+        in_specs=[VMEM, VMEM, VMEM],
         out_specs=(VMEM, SMEM),
         compiler_params=params(),
+        cost_estimate=COST,
         name="join",
-    )(flag, *parts)
+    )(own, near, away)
+    return applied, gram.transpose(2, 0, 1)
 
 
 def block_gram(orbitals, applied, owner, blocks_per_k, cells):
@@ -325,7 +335,8 @@
     lines = n_kb // 2
     blocks_per_k = n_kb // NK
     place, core = lax.axis_index("kb"), lax.axis_index("slab")
-    column, line = place % 2, place // 2
+    column = place % 2
+    across = [(a, a ^ 1) for a in range(n_kb)]
 
     def swap(x):
         return lax.ppermute(x, "slab", [(0, 1), (1, 0)])
@@ -335,48 +346,25 @@
             x, "kb", [(2 * a + c, 2 * (a ^ d) + c) for a in range(lines) for c in range(2)]
         )
 
-    beside = lax.ppermute(orbitals, "kb", [(a, a ^ 1) for a in range(n_kb)])
-    mine = [orbitals] + [from_line(orbitals, d) for d in range(1, lines)]
-    partners = [(x, swap(x)) for x in mine]
-    home = core == column
-    target_mine = jnp.where(home, orbitals, beside)
-    target_sent = jnp.where(home, beside, orbitals)
-    target = (target_mine, swap(target_sent))
-
-    k_of = owner // blocks_per_k
-    target_k = k_of[2 * line + core]
-    partner_at = 2 * (line ^ jnp.arange(lines, dtype=jnp.int32)) + column
-    choice = q_index[target_k][k_of[partner_at]]
-    weights = choose(choice, core[None].astype(jnp.int32), kernel, swap(kernel), side)
-
+    order = list(range(lines))
+    arrived = {d: from_line(orbitals, d) for d in [*order[2:], 1]}
+    beside = lax.ppermute(orbitals, "kb", across)
+    far_kernel = swap(kernel)
+    weights = choose_weights(
+        q_index, owner, (kernel, far_kernel), tuple(order), side, blocks_per_k
+    )
+    own = (orbitals, swap(lax.optimization_barrier((orbitals, far_kernel))[0]))
+    arrived[2], weights = lax.optimization_barrier((arrived[2], weights))
+    arrived[1], beside, arrived[2] = lax.optimization_barrier((arrived[1], beside, arrived[2]))
+    beside = (beside, swap(beside))
+    partners = [own] + [(arrived[d], swap(arrived[d])) for d in order[1:]]
     sums = None
-    step = min(4, lines)
-    for at in range(0, lines, step):
-        sums = apply_pairs(target, partners[at : at + step], weights[at : at + step], side, sums)
-    own_part, other_part = sums
-
-    def index(line_at, column_at, core_at):
-        return (2 * line_at + column_at) * 2 + core_at
-
-    both = ("kb", "slab")
-    away_mine = lax.ppermute(
-        own_part,
-        both,
-        [(index(m, y, 1 - y), index(m, 1 - y, 1 - y)) for m in range(lines) for y in range(2)],
-    )
-    away_near = lax.ppermute(
-        other_part,
-        both,
-        [(index(m, y, 1 - y), index(m, 1 - y, y)) for m in range(lines) for y in range(2)],
-    )
-    near = lax.ppermute(
-        other_part,
-        both,
-        [(index(m, y, y), index(m, y, 1 - y)) for m in range(lines) for y in range(2)],
-    )
-    applied, gram = join(
-        home[None].astype(jnp.int32), (own_part, near, away_mine, away_near), orbitals.shape
-    )
+    for at in range(0, lines, 4):
+        sums = apply_pairs(own, beside, partners[at : at + 4], weights, at, side, sums)
+    mine, far = sums
+    near = swap(far)
+    away = lax.ppermute(jnp.where(core == column, near, mine), "kb", across)
+    applied, gram = join(mine, near, away, orbitals.shape)
     if blocks_per_k > 1:
         gram = block_gram(orbitals, applied, owner, blocks_per_k, side**3)
     return applied, gram

time: 36.3 us -> 31.3 us (0.86)
  the two profiles are of different devices: /device:TPU:1 before, /device:TPU:0 now
where the time goes in v2:
time: 31.3 us; the launch traced here: 31.1 us
  waiting for transfers between devices  12.1 us (39%)
  starting transfers between devices  10.4 us (33%)
  Pallas kernels  5.34 us (17%)
  local copies, waits for them, and re-layouts  2.41 us (8%)
  between operations  0.72 us (2%)
    ppermute x3, waiting for transfers between devices, from_line(): lax.ppermute(x, 'kb', [(2 * a + c, 2 * (a ^ d) + c) for a in range(lines)...  5.55 us
    ppermute x3, starting transfers between devices, from_line(): lax.ppermute(x, 'kb', [(2 * a + c, 2 * (a ^ d) + c) for a in range(lines)...  5.46 us
    ppermute x1, waiting for transfers between devices, on_device(): away = lax.ppermute(jnp.where(core == column, near, mine), 'kb', across)  4.15 us
    pallas_call x1, Pallas kernels, apply_pairs(): pl.pallas_call(functools.partial(pair_kernel, side, count, first, sums is...  3.54 us
    ppermute x7, waiting for transfers between devices, swap(): return lax.ppermute(x, 'slab', [(0, 1), (1, 0)])  2.45 us
    unnamed x18, local copies, waits for them, and re-layouts  2.41 us
    ppermute x7, starting transfers between devices, swap(): return lax.ppermute(x, 'slab', [(0, 1), (1, 0)])  1.86 us
    ppermute x1, starting transfers between devices, on_device(): away = lax.ppermute(jnp.where(core == column, near, mine), 'kb', across)  1.58 us
  transfers between devices with their start and end apart: 12, of which 7 were waited for; matrix products, arithmetic and copies ran while one was open for 0% of the time, Pallas kernels for 4%

profile of v2, /device:TPU:0, one launch (start us, length us, event | category | flops | bytes accessed | tf_op | source)
XLA Modules:
  0.0 31.1 jit_solution(4497678360812840567)
XLA Ops:
  0.6 0.5 %collective-permute-start = (f32[8,32,512]{2,1,0:T(8,128)}, f32[8,32,512]{2,1,0:T(8,128)S(1)}, u32[]{:S(2)}, u32[]{:S(2)}) collective-permute-start(f32[8,32,512]{2,1,0:T(8,128)} %mine_ref.1), channel_id=1, source_target_pairs={{0,1},{1,0},{2,3},{3,2},{4,5},{5,4},{6,7},{7,6},{8,9},{9,8},{10,11... | collective-permute-start | bytes 1572872 | tf_op jit(solution)/shard_map/ppermute | solution.py:342
  1.1 4.7 %collective-permute-start.8 = (f32[2,1,16,1024]{3,2,1,0:T(8,128)}, f32[2,1,16,1024]{3,2,1,0:T(8,128)S(1)}, u32[]{:S(2)}, u32[]{:S(2)}) collective-permute-start(f32[2,1,16,1024]{3,2,1,0:T(8,128)} %refs_4_.1), channel_id=1, source_target_pairs={{0,12},{2,14},{4,8},{6,10},{8,4},{10,6},{12,0},{14,2},{1,13},{3,15... | collective-permute-start | bytes 393224 | tf_op jit(solution)/shard_map/ppermute | solution.py:345
  5.8 0.0 collective-permute-start.2
  5.8 1.5 %collective-permute-start.3 = (f32[2,1,16,1024]{3,2,1,0:T(8,128)}, f32[2,1,16,1024]{3,2,1,0:T(8,128)S(1)}, u32[]{:S(2)}, u32[]{:S(2)}) collective-permute-start(f32[2,1,16,1024]{3,2,1,0:T(8,128)} %refs_4_.1), channel_id=1, source_target_pairs={{0,2},{2,0},{4,6},{6,4},{8,10},{10,8},{12,14},{14,12},{1,3},{3,1},... | collective-permute-start | bytes 393224 | tf_op jit(solution)/shard_map/ppermute | solution.py:351
  7.3 0.8 %collective-permute-start.4 = (f32[2,1,16,1024]{3,2,1,0:T(8,128)}, f32[2,1,16,1024]{3,2,1,0:T(8,128)S(1)}, u32[]{:S(2)}, u32[]{:S(2)}) collective-permute-start(f32[2,1,16,1024]{3,2,1,0:T(8,128)} %refs_4_.1), channel_id=1, source_target_pairs={{0,8},{2,10},{4,12},{6,14},{8,0},{10,2},{12,4},{14,6},{1,9},{3,11}... | collective-permute-start | bytes 393224 | tf_op jit(solution)/shard_map/ppermute | solution.py:345
  8.1 2.3 %collective-permute-done.8.refs_10_ = f32[2,1,16,1024]{3,2,1,0:T(8,128)S(1)} collective-permute-done((f32[2,1,16,1024]{3,2,1,0:T(8,128)}, f32[2,1,16,1024]{3,2,1,0:T(8,128)S(1)}, u32[]{:S(2)}, u32[]{:S(2)}) %collective-permute-start.8) | collective-permute-done | bytes 131104 | tf_op jit(solution)/shard_map/ppermute | solution.py:345
  10.4 0.0 collective-permute-start.9
  10.4 0.0 collective-permute-done.other_ref
  10.4 0.5 %collective-permute-start.1 = (f32[2,1,16,1024]{3,2,1,0:T(8,128)}, f32[2,1,16,1024]{3,2,1,0:T(8,128)S(1)}, u32[]{:S(2)}, u32[]{:S(2)}) collective-permute-start(f32[2,1,16,1024]{3,2,1,0:T(8,128)} %refs_4_.1), channel_id=1, source_target_pairs={{0,1},{1,0},{2,3},{3,2},{4,5},{5,4},{6,7},{7,6},{8,9},{9,8},{10,11... | collective-permute-start | bytes 393224 | tf_op jit(solution)/shard_map/ppermute | solution.py:342
  10.9 0.0 copy-start
  10.9 1.0 %copy-done = f32[8,32,512]{2,1,0:T(8,128)S(1)} copy-done((f32[8,32,512]{2,1,0:T(8,128)S(1)}, f32[8,32,512]{2,1,0:T(8,128)}, u32[]{:S(2)}) %copy-start) | copy-done | bytes 524312
  12.0 0.0 copy-start.2
  12.0 0.7 %copy-done.2 = s32[8,8]{1,0:T(8,128)S(1)} copy-done((s32[8,8]{1,0:T(8,128)S(1)}, s32[8,8]{1,0:T(8,128)}, u32[]{:S(2)}) %copy-start.2) | copy-done | bytes 280
  12.7 0.0 copy-start.3
  12.7 0.7 %copy-done.3 = s32[8]{0:T(128)S(1)} copy-done((s32[8]{0:T(128)S(1)}, s32[8]{0:T(128)}, u32[]{:S(2)}) %copy-start.3) | copy-done | bytes 56
  13.3 0.0 copy-start.1
  13.3 0.0 copy-start.4
  13.3 0.0 copy-start.5
  13.3 0.0 copy-start.6
  13.3 0.0 copy-start.7
  13.4 0.0 copy-start.8
  13.4 1.1 %weights.1.refs_12_ = f32[4,32,1024]{2,1,0:T(8,128)S(1)} custom-call(s32[8,8]{1,0:T(8,128)S(1)} %copy-done.2, s32[8]{0:T(128)S(1)} %copy-done.3, f32[8,32,512]{2,1,0:T(8,128)S(1)} %copy-done, f32[8,32,512]{2,1,0:T(8,128)S(1)} %collective-permute-done.other_ref), custom_call_target="tpu_custom_call" | custom-call | flops 20000000000 | bytes 100000000 | tf_op jit(solution)/shard_map/weights/pallas_call | solution.py:257
  14.5 3.2 %collective-permute-done.4.refs_8_ = f32[2,1,16,1024]{3,2,1,0:T(8,128)S(1)} collective-permute-done((f32[2,1,16,1024]{3,2,1,0:T(8,128)}, f32[2,1,16,1024]{3,2,1,0:T(8,128)S(1)}, u32[]{:S(2)}, u32[]{:S(2)}) %collective-permute-start.4) | collective-permute-done | bytes 131104 | tf_op jit(solution)/shard_map/ppermute | solution.py:345
  17.7 0.0 collective-permute-done.2.refs_6_
  17.7 0.0 collective-permute-done.3.refs_2_
  17.7 0.0 collective-permute-start.5
  17.7 0.5 %collective-permute-start.6 = (f32[2,1,16,1024]{3,2,1,0:T(8,128)S(1)}, f32[2,1,16,1024]{3,2,1,0:T(8,128)S(1)}, u32[]{:S(2)}, u32[]{:S(2)}) collective-permute-start(f32[2,1,16,1024]{3,2,1,0:T(8,128)S(1)} %collective-permute-done.2.refs_6_), channel_id=1, source_target_pairs={{0,1},{1,0},{2,3},{3,2},{4,5},{5,4},{6,7},{7,6},{8,9},{9,8},{10,11... | collective-permute-start | bytes 393224 | tf_op jit(solution)/shard_map/ppermute | solution.py:342
  18.2 0.1 collective-permute-start.7
  18.3 0.0 collective-permute-done.9.refs_11_
  18.3 0.0 collective-permute-done.1.refs_1_.refs_5_
  18.3 0.8 %collective-permute-done.5.refs_3_ = f32[2,1,16,1024]{3,2,1,0:T(8,128)S(1)} collective-permute-done((f32[2,1,16,1024]{3,2,1,0:T(8,128)S(1)}, f32[2,1,16,1024]{3,2,1,0:T(8,128)S(1)}, u32[]{:S(2)}, u32[]{:S(2)}) %collective-permute-start.5) | collective-permute-done | bytes 131104 | tf_op jit(solution)/shard_map/ppermute | solution.py:342
  19.1 0.2 collective-permute-done.6.refs_7_
  19.3 0.3 %collective-permute-done.7.refs_9_ = f32[2,1,16,1024]{3,2,1,0:T(8,128)S(1)} collective-permute-done((f32[2,1,16,1024]{3,2,1,0:T(8,128)S(1)}, f32[2,1,16,1024]{3,2,1,0:T(8,128)S(1)}, u32[]{:S(2)}, u32[]{:S(2)}) %collective-permute-start.7) | collective-permute-done | bytes 131104 | tf_op jit(solution)/shard_map/ppermute | solution.py:342
  19.6 0.0 copy-done.1
  19.6 0.0 copy-done.4
  19.6 0.0 copy-done.5
  19.6 0.0 copy-done.6
  19.6 0.0 copy-done.7
  19.6 0.0 copy-done.8
  19.6 3.5 %pairs.1 = (f32[264,128]{1,0:T(8,128)S(1)}, f32[264,128]{1,0:T(8,128)S(1)}) custom-call(f32[2,1,16,1024]{3,2,1,0:T(8,128)S(1)} %copy-done.1, f32[2,1,16,1024]{3,2,1,0:T(8,128)S(1)} %collective-permute-done.1.refs_1_.refs_5_, f32[2,1,16,1024]{3,2,1,0:T(8,128)S(1)} %collective-permute-done.3.refs_2_, f32[2,1,16,1024]{3,2,1,0:T(8,128)S(1)} %collective-permute-done.5.refs_3_, ...), custom_call_target="tpu_custom_call" | custom-call | flops 20000000000 | bytes 100000000 | tf_op jit(solution)/shard_map/pairs/pallas_call | solution.py:285
  23.2 0.2 collective-permute-start.10
  23.4 1.2 %collective-permute-done.10.near_ref = f32[264,128]{1,0:T(8,128)S(1)} collective-permute-done((f32[264,128]{1,0:T(8,128)S(1)}, f32[264,128]{1,0:T(8,128)S(1)}, u32[]{:S(2)}, u32[]{:S(2)}) %collective-permute-start.10) | collective-permute-done | bytes 135200 | tf_op jit(solution)/shard_map/ppermute | solution.py:342
  24.6 1.6 %collective-permute-start.11 = (f32[264,128]{1,0:T(8,128)S(1)}, f32[264,128]{1,0:T(8,128)S(1)}, u32[]{:S(2)}, u32[]{:S(2)}) collective-permute-start(f32[264,128]{1,0:T(8,128)S(1)} %broadcast_select_fusion), channel_id=1, source_target_pairs={{0,2},{2,0},{4,6},{6,4},{8,10},{10,8},{12,14},{14,12},{1,3},{3,1},... | collective-permute-start | bytes 405512 | tf_op jit(solution)/shard_map/ppermute | solution.py:366
  26.2 4.2 %collective-permute-done.11.away_ref = f32[264,128]{1,0:T(8,128)S(1)} collective-permute-done((f32[264,128]{1,0:T(8,128)S(1)}, f32[264,128]{1,0:T(8,128)S(1)}, u32[]{:S(2)}, u32[]{:S(2)}) %collective-permute-start.11) | collective-permute-done | bytes 135200 | tf_op jit(solution)/shard_map/ppermute | solution.py:366
  30.4 0.7 %join.1 = (f32[2,1,16,1024]{3,2,1,0:T(8,128)}, f32[1,1,2]{2,1,0:T(1,128)}) custom-call(f32[264,128]{1,0:T(8,128)S(1)} %get-tuple-element.18.own_ref, f32[264,128]{1,0:T(8,128)S(1)} %collective-permute-done.10.near_ref, f32[264,128]{1,0:T(8,128)S(1)} %collective-permute-done.11.away_ref), custom_call_target="tpu_custom_call" | custom-call | flops 20000000000 | bytes 100000000 | tf_op jit(solution)/shard_map/join/pallas_call | solution.py:306
  (1 shorter events, 0.0 us)
Async XLA Ops:
  0.6 9.8 %collective-permute-start = (f32[8,32,512]{2,1,0:T(8,128)}, f32[8,32,512]{2,1,0:T(8,128)S(1)}, u32[]{:S(2)}, u32[]{:S(2)}) collective-permute-start(f32[8,32,512]{2,1,0:T(8,128)} %mine_ref.1), channel_id=1, source_target_pairs={{0,1},{1,0},{2,3},{3,2},{4,5},{5,4},{6,7},{7,6},{8,9},{9,8},{10,11... | collective-permute-start | bytes 1572872 | tf_op jit(solution)/shard_map/ppermute | solution.py:342
  1.1 9.3 %collective-permute-start.8 = (f32[2,1,16,1024]{3,2,1,0:T(8,128)}, f32[2,1,16,1024]{3,2,1,0:T(8,128)S(1)}, u32[]{:S(2)}, u32[]{:S(2)}) collective-permute-start(f32[2,1,16,1024]{3,2,1,0:T(8,128)} %refs_4_.1), channel_id=1, source_target_pairs={{0,12},{2,14},{4,8},{6,10},{8,4},{10,6},{12,0},{14,2},{1,13},{3,15... | collective-permute-start | bytes 393224 | tf_op jit(solution)/shard_map/ppermute | solution.py:345
  5.8 11.9 %collective-permute-start.2 = (f32[2,1,16,1024]{3,2,1,0:T(8,128)}, f32[2,1,16,1024]{3,2,1,0:T(8,128)S(1)}, u32[]{:S(2)}, u32[]{:S(2)}) collective-permute-start(f32[2,1,16,1024]{3,2,1,0:T(8,128)} %refs_4_.1), channel_id=1, source_target_pairs={{0,4},{2,6},{4,0},{6,2},{8,12},{10,14},{12,8},{14,10},{1,5},{3,7},... | collective-permute-start | bytes 393224 | tf_op jit(solution)/shard_map/ppermute | solution.py:345
  5.8 11.9 %collective-permute-start.3 = (f32[2,1,16,1024]{3,2,1,0:T(8,128)}, f32[2,1,16,1024]{3,2,1,0:T(8,128)S(1)}, u32[]{:S(2)}, u32[]{:S(2)}) collective-permute-start(f32[2,1,16,1024]{3,2,1,0:T(8,128)} %refs_4_.1), channel_id=1, source_target_pairs={{0,2},{2,0},{4,6},{6,4},{8,10},{10,8},{12,14},{14,12},{1,3},{3,1},... | collective-permute-start | bytes 393224 | tf_op jit(solution)/shard_map/ppermute | solution.py:351
  7.3 10.4 %collective-permute-start.4 = (f32[2,1,16,1024]{3,2,1,0:T(8,128)}, f32[2,1,16,1024]{3,2,1,0:T(8,128)S(1)}, u32[]{:S(2)}, u32[]{:S(2)}) collective-permute-start(f32[2,1,16,1024]{3,2,1,0:T(8,128)} %refs_4_.1), channel_id=1, source_target_pairs={{0,8},{2,10},{4,12},{6,14},{8,0},{10,2},{12,4},{14,6},{1,9},{3,11}... | collective-permute-start | bytes 393224 | tf_op jit(solution)/shard_map/ppermute | solution.py:345
  10.4 7.9 %collective-permute-start.9 = (f32[2,1,16,1024]{3,2,1,0:T(8,128)S(1)}, f32[2,1,16,1024]{3,2,1,0:T(8,128)S(1)}, u32[]{:S(2)}, u32[]{:S(2)}) collective-permute-start(f32[2,1,16,1024]{3,2,1,0:T(8,128)S(1)} %collective-permute-done.8.refs_10_), channel_id=1, source_target_pairs={{0,1},{1,0},{2,3},{3,2},{4,5},{5,4},{6,7},{7,6},{8,9},{9,8},{10,11... | collective-permute-start | bytes 393224 | tf_op jit(solution)/shard_map/ppermute | solution.py:342
  10.4 7.9 %collective-permute-start.1 = (f32[2,1,16,1024]{3,2,1,0:T(8,128)}, f32[2,1,16,1024]{3,2,1,0:T(8,128)S(1)}, u32[]{:S(2)}, u32[]{:S(2)}) collective-permute-start(f32[2,1,16,1024]{3,2,1,0:T(8,128)} %refs_4_.1), channel_id=1, source_target_pairs={{0,1},{1,0},{2,3},{3,2},{4,5},{5,4},{6,7},{7,6},{8,9},{9,8},{10,11... | collective-permute-start | bytes 393224 | tf_op jit(solution)/shard_map/ppermute | solution.py:342
  10.9 1.0 %copy-start = (f32[8,32,512]{2,1,0:T(8,128)S(1)}, f32[8,32,512]{2,1,0:T(8,128)}, u32[]{:S(2)}) copy-start(f32[8,32,512]{2,1,0:T(8,128)} %mine_ref.1) | copy-start | bytes 1572868
  12.0 0.7 %copy-start.2 = (s32[8,8]{1,0:T(8,128)S(1)}, s32[8,8]{1,0:T(8,128)}, u32[]{:S(2)}) copy-start(s32[8,8]{1,0:T(8,128)} %q_ref.1) | copy-start | bytes 772
  12.7 0.7 %copy-start.3 = (s32[8]{0:T(128)S(1)}, s32[8]{0:T(128)}, u32[]{:S(2)}) copy-start(s32[8]{0:T(128)} %owner_ref.1) | copy-start | bytes 100
  13.3 6.3 %copy-start.1 = (f32[2,1,16,1024]{3,2,1,0:T(8,128)S(1)}, f32[2,1,16,1024]{3,2,1,0:T(8,128)}, u32[]{:S(2)}) copy-start(f32[2,1,16,1024]{3,2,1,0:T(8,128)} %refs_4_.1) | copy-start | bytes 393220
  13.3 6.3 %copy-start.4 = (bf16[2,256,256]{2,1,0:T(8,128)(2,1)S(1)}, bf16[2,256,256]{2,1,0:T(8,128)(2,1)}, u32[]{:S(2)}) copy-start(bf16[2,256,256]{2,1,0:T(8,128)(2,1)} %constant.31.clone.refs_13_) | copy-start | bytes 786436
  13.3 6.3 %copy-start.5 = (bf16[2,256,256]{2,1,0:T(8,128)(2,1)S(1)}, bf16[2,256,256]{2,1,0:T(8,128)(2,1)}, u32[]{:S(2)}) copy-start(bf16[2,256,256]{2,1,0:T(8,128)(2,1)} %constant.32.clone.refs_14_) | copy-start | bytes 786436
  13.3 6.3 %copy-start.6 = (bf16[2,256,256]{2,1,0:T(8,128)(2,1)S(1)}, bf16[2,256,256]{2,1,0:T(8,128)(2,1)}, u32[]{:S(2)}) copy-start(bf16[2,256,256]{2,1,0:T(8,128)(2,1)} %constant.33.clone.refs_15_) | copy-start | bytes 786436
  13.3 6.3 %copy-start.7 = (bf16[2,256,256]{2,1,0:T(8,128)(2,1)S(1)}, bf16[2,256,256]{2,1,0:T(8,128)(2,1)}, u32[]{:S(2)}) copy-start(bf16[2,256,256]{2,1,0:T(8,128)(2,1)} %constant.34.clone.refs_16_) | copy-start | bytes 786436
  13.4 6.3 %copy-start.8 = (f32[8,2,16,128]{3,2,1,0:T(8,128)S(1)}, f32[8,2,16,128]{3,2,1,0:T(8,128)}, u32[]{:S(2)}) copy-start(f32[8,2,16,128]{3,2,1,0:T(8,128)} %constant.35.clone.refs_17_) | copy-start | bytes 393220
  17.7 1.4 %collective-permute-start.5 = (f32[2,1,16,1024]{3,2,1,0:T(8,128)S(1)}, f32[2,1,16,1024]{3,2,1,0:T(8,128)S(1)}, u32[]{:S(2)}, u32[]{:S(2)}) collective-permute-start(f32[2,1,16,1024]{3,2,1,0:T(8,128)S(1)} %collective-permute-done.3.refs_2_), channel_id=1, source_target_pairs={{0,1},{1,0},{2,3},{3,2},{4,5},{5,4},{6,7},{7,6},{8,9},{9,8},{10,11... | collective-permute-start | bytes 393224 | tf_op jit(solution)/shard_map/ppermute | solution.py:342
  17.7 1.5 %collective-permute-start.6 = (f32[2,1,16,1024]{3,2,1,0:T(8,128)S(1)}, f32[2,1,16,1024]{3,2,1,0:T(8,128)S(1)}, u32[]{:S(2)}, u32[]{:S(2)}) collective-permute-start(f32[2,1,16,1024]{3,2,1,0:T(8,128)S(1)} %collective-permute-done.2.refs_6_), channel_id=1, source_target_pairs={{0,1},{1,0},{2,3},{3,2},{4,5},{5,4},{6,7},{7,6},{8,9},{9,8},{10,11... | collective-permute-start | bytes 393224 | tf_op jit(solution)/shard_map/ppermute | solution.py:342
  18.2 1.3 %collective-permute-start.7 = (f32[2,1,16,1024]{3,2,1,0:T(8,128)S(1)}, f32[2,1,16,1024]{3,2,1,0:T(8,128)S(1)}, u32[]{:S(2)}, u32[]{:S(2)}) collective-permute-start(f32[2,1,16,1024]{3,2,1,0:T(8,128)S(1)} %collective-permute-done.4.refs_8_), channel_id=1, source_target_pairs={{0,1},{1,0},{2,3},{3,2},{4,5},{5,4},{6,7},{7,6},{8,9},{9,8},{10,11... | collective-permute-start | bytes 393224 | tf_op jit(solution)/shard_map/ppermute | solution.py:342
  23.2 1.4 %collective-permute-start.10 = (f32[264,128]{1,0:T(8,128)S(1)}, f32[264,128]{1,0:T(8,128)S(1)}, u32[]{:S(2)}, u32[]{:S(2)}) collective-permute-start(f32[264,128]{1,0:T(8,128)S(1)} %get-tuple-element.19), channel_id=1, source_target_pairs={{0,1},{1,0},{2,3},{3,2},{4,5},{5,4},{6,7},{7,6},{8,9},{9,8},{10,11... | collective-permute-start | bytes 405512 | tf_op jit(solution)/shard_map/ppermute | solution.py:342
  24.6 5.7 %collective-permute-start.11 = (f32[264,128]{1,0:T(8,128)S(1)}, f32[264,128]{1,0:T(8,128)S(1)}, u32[]{:S(2)}, u32[]{:S(2)}) collective-permute-start(f32[264,128]{1,0:T(8,128)S(1)} %broadcast_select_fusion), channel_id=1, source_target_pairs={{0,2},{2,0},{4,6},{6,4},{8,10},{10,8},{12,14},{14,12},{1,3},{3,1},... | collective-permute-start | bytes 405512 | tf_op jit(solution)/shard_map/ppermute | solution.py:366

commit v3 on v2

--- a/solution.py
+++ b/solution.py
@@ -10,6 +10,7 @@
 from jax.sharding import PartitionSpec as P
 
 NK = 8
+GROUP = 4
 LANES = 128
 F32 = jnp.float32
 BF16 = jnp.bfloat16
@@ -30,12 +31,10 @@
     return np.block([[real, imag], [-imag, real]])
 
 
-def sublane_table(side, count):
-    index = np.arange(side)
-    phase = 2.0 * math.pi * (np.outer(index, index) % side) / side
-    unit = np.eye(count)
-    cosine, sine = np.kron(unit, np.cos(phase)), np.kron(unit, np.sin(phase))
-    return np.block([[cosine, sine], [-sine, cosine]])
+def turn_table(side):
+    phase = 2.0 * math.pi * np.outer(np.arange(side // 2), np.arange(2 * GROUP) // GROUP) / side
+    both = np.stack([np.cos(phase), np.sin(phase)], 1).astype(np.float32)
+    return np.ascontiguousarray(np.broadcast_to(both[..., None], (*both.shape, LANES)))
 
 
 def twist_table(side, rows):
@@ -121,33 +120,40 @@
                 if shift:
                     piece = pltpu.roll(piece, shift, 1)
                 total = piece if total is None else jnp.where(lane == a, piece, total)
-            weight_ref[pair, :, lane_slice(b)] = total
-
-
-def pair_kernel(side, count, first, has_sum, *refs):
+            at = pl.ds(b * GROUP * side + pair % GROUP, side, stride=GROUP)
+            weight_ref[pair // GROUP, at, :] = total
+
+
+def pair_kernel(side, at_group, has_sum, *refs):
     refs = list(refs)
     take = lambda n: [refs.pop(0) for _ in range(n)]
+    partners = [take(2) for _ in range(GROUP)]
     own, beside = take(2), take(2)
-    partners = [take(2) for _ in range(count)]
     (weight_ref,) = take(1)
-    lane_f, lane_b, rows_f, rows_b, twist = take(5)
+    lane_f, lane_b, twist, turn = take(4)
     sums = take(2) if has_sum else None
     outs = take(2)
-    target, a_high, a_low, y_ref, f_high, f_low, g_ref = take(7)
+    target, x_re, x_im, high_ref, low_ref, g_ref = take(6)
 
     tiles = side * side // LANES
     half = side // 2
-    rows = side * count
+    subs = 2 * GROUP
+    rows = half * subs
 
     def parts(ref):
         return ref[0], ref[1]
+
+    sign = jnp.where(lax.broadcasted_iota(jnp.int32, (subs, LANES), 0) < GROUP, 1.0, -1.0)
+
+    def halves(value):
+        return pltpu.roll(value, GROUP, 0) + value * sign
 
     home = lax.axis_index("kb") % 2 == lax.axis_index("slab")
     for h in range(2):
         target[h] = jnp.where(home, own[h][:, 0], beside[h][:, 0])
-    for p in range(count):
+
+    for p in range(GROUP):
         for h in range(2):
-            row = p * side + h * half
             values = []
             for t in range(tiles):
                 t_re, t_im = target[h, 0, :, lane_slice(t)], target[h, 1, :, lane_slice(t)]
@@ -158,32 +164,50 @@
                 if b:
                     cosine, sine = twist[b, 0], twist[b, 1]
                     re, im = re * cosine + im * sine, im * cosine - re * sine
-                at = pl.ds(b * rows + row, half)
-                for k, part in enumerate((re, im)):
-                    high, low = split(part)
-                    a_high[at, lane_slice(k)] = high
-                    a_low[at, lane_slice(k)] = low
-    y_ref[...] = dot_parts((a_high[...], a_low[...]), parts(lane_f))
-    for n in range(tiles // 2):
-        blocks = []
-        for k in range(2):
-            blocks.append(
-                jnp.concatenate(
-                    [y_ref[pl.ds((2 * n + j) * rows, rows), lane_slice(k)] for j in range(2)], 1
-                )
-            )
-        spectrum = dot_parts(parts(rows_f), split(jnp.concatenate(blocks, 0)))
-        weights = weight_ref[first : first + count, :, pl.ds(n * 2 * LANES, 2 * LANES)]
-        weights = weights.reshape(rows, 2 * LANES)
-        weighted = spectrum * jnp.concatenate([weights, weights], 0)
-        back = dot_parts(parts(rows_b), split(weighted))
-        high, low = split(back)
-        for j in range(2):
+                at = pl.ds(b * rows + h * GROUP + p, half, stride=subs)
+                x_re[at, :] = re
+                x_im[at, :] = im
+    def forward(b):
+        values = []
+        for x in range(half):
+            at = pl.ds(b * rows + x * subs, subs)
+            re, im = halves(x_re[at, :]), halves(x_im[at, :])
+            if x:
+                cosine, sine = turn[x, 0], turn[x, 1]
+                re, im = re * cosine + im * sine, im * cosine - re * sine
+            values.append((re, im))
+        values = dft_list(values, -1)
+        for x in range(0, half, 2):
+            at = pl.ds(b * rows + x * subs, 2 * subs)
             for k in range(2):
-                at = (pl.ds((2 * n + j) * rows, rows), lane_slice(k))
-                f_high[at] = high[k * rows : (k + 1) * rows, j * LANES : (j + 1) * LANES]
-                f_low[at] = low[k * rows : (k + 1) * rows, j * LANES : (j + 1) * LANES]
-    g_ref[...] = dot_parts((f_high[...], f_low[...]), parts(lane_b))
+                high, low = split(jnp.concatenate([values[x][k], values[x + 1][k]], 0))
+                high_ref[at, lane_slice(k)] = high
+                low_ref[at, lane_slice(k)] = low
+
+    def middle(b):
+        at = pl.ds(b * rows, rows)
+        spectrum = dot_parts((high_ref[at, :], low_ref[at, :]), parts(lane_f))
+        weights = weight_ref[at_group, at, :]
+        weighted = split(spectrum * jnp.concatenate([weights, weights], 1))
+        g_ref[at, :] = dot_parts(weighted, parts(lane_b))
+
+    def backward(b):
+        values = []
+        for x in range(half):
+            at = pl.ds(b * rows + x * subs, subs)
+            values.append((g_ref[at, lane_slice(0)], g_ref[at, lane_slice(1)]))
+        for x, (re, im) in enumerate(dft_list(values, 1)):
+            if x:
+                cosine, sine = turn[x, 0], turn[x, 1]
+                re, im = re * cosine - im * sine, im * cosine + re * sine
+            at = pl.ds(b * rows + x * subs, subs)
+            x_re[at, :] = halves(re)
+            x_im[at, :] = halves(im)
+
+    for b in range(tiles):
+        forward(b)
+        middle(b)
+        backward(b)
     gram_re = jnp.zeros((half, LANES), F32)
     gram_im = jnp.zeros((half, LANES), F32)
     for h in range(2):
@@ -191,12 +215,11 @@
         if has_sum:
             for t in range(tiles):
                 total[t] = [sums[h][pl.ds((k * tiles + t) * half, half), :] for k in range(2)]
-        for p in range(count):
-            row = p * side + h * half
+        for p in range(GROUP):
             values = []
             for b in range(tiles):
-                at = pl.ds(b * rows + row, half)
-                re, im = g_ref[at, lane_slice(0)], g_ref[at, lane_slice(1)]
+                at = pl.ds(b * rows + h * GROUP + p, half, stride=subs)
+                re, im = x_re[at, :], x_im[at, :]
                 if b:
                     cosine, sine = twist[b, 0], twist[b, 1]
                     re, im = re * cosine - im * sine, im * cosine + re * sine
@@ -256,7 +279,7 @@
 def choose_weights(q_index, owner, kernels, order, side, blocks_per_k):
     return pl.pallas_call(
         functools.partial(weight_kernel, side, blocks_per_k, order),
-        out_shape=jax.ShapeDtypeStruct((len(order), side, side * side), F32),
+        out_shape=jax.ShapeDtypeStruct((len(order) // GROUP, GROUP * side**3 // LANES, LANES), F32),
         in_specs=[SMEM, SMEM, VMEM, VMEM],
         out_specs=VMEM,
         compiler_params=params(),
@@ -265,36 +288,32 @@
     )(q_index, owner, *kernels)
 
 
-def apply_pairs(own, beside, partners, weights, first, side, sums=None):
-    count = len(partners)
+def apply_pairs(own, beside, partners, weights, at_group, side, sums=None):
     half = side // 2
     tiles = side * side // LANES
-    rows = side * count
+    rows = tiles * half * 2 * GROUP
     lane = lane_table(side)
-    across = sublane_table(side, count)
     tables = [
         jnp.asarray(bf16_parts(lane)),
         jnp.asarray(bf16_parts(lane.T)),
-        jnp.asarray(bf16_parts(across)),
-        jnp.asarray(bf16_parts(across.T)),
         jnp.asarray(twist_table(side, half)),
+        jnp.asarray(turn_table(side)),
     ]
-    operands = [*own, *beside] + [x for pair in partners for x in pair] + [weights] + tables
+    operands = [x for pair in partners for x in pair] + [*own, *beside, weights] + tables
     operands += list(sums) if sums is not None else []
     message = jax.ShapeDtypeStruct((2 * tiles * half + 8, LANES), F32)
     return pl.pallas_call(
-        functools.partial(pair_kernel, side, count, first, sums is not None),
+        functools.partial(pair_kernel, side, at_group, sums is not None),
         out_shape=(message, message),
         in_specs=[VMEM] * len(operands),
         out_specs=(VMEM, VMEM),
         scratch_shapes=[
             pltpu.VMEM((2, 2, half, side * side), F32),
-            pltpu.VMEM((tiles * rows, 2 * LANES), BF16),
-            pltpu.VMEM((tiles * rows, 2 * LANES), BF16),
-            pltpu.VMEM((tiles * rows, 2 * LANES), F32),
-            pltpu.VMEM((tiles * rows, 2 * LANES), BF16),
-            pltpu.VMEM((tiles * rows, 2 * LANES), BF16),
-            pltpu.VMEM((tiles * rows, 2 * LANES), F32),
+            pltpu.VMEM((rows, LANES), F32),
+            pltpu.VMEM((rows, LANES), F32),
+            pltpu.VMEM((rows, 2 * LANES), BF16),
+            pltpu.VMEM((rows, 2 * LANES), BF16),
+            pltpu.VMEM((rows, 2 * LANES), F32),
         ],
         compiler_params=params(),
         cost_estimate=COST,
@@ -346,21 +365,24 @@
             x, "kb", [(2 * a + c, 2 * (a ^ d) + c) for a in range(lines) for c in range(2)]
         )
 
-    order = list(range(lines))
-    arrived = {d: from_line(orbitals, d) for d in [*order[2:], 1]}
+    order = [*range(2, lines), 1, 0]
+    arrived = {d: from_line(orbitals, d) for d in order[:-1]}
     beside = lax.ppermute(orbitals, "kb", across)
     far_kernel = swap(kernel)
     weights = choose_weights(
         q_index, owner, (kernel, far_kernel), tuple(order), side, blocks_per_k
     )
-    own = (orbitals, swap(lax.optimization_barrier((orbitals, far_kernel))[0]))
-    arrived[2], weights = lax.optimization_barrier((arrived[2], weights))
-    arrived[1], beside, arrived[2] = lax.optimization_barrier((arrived[1], beside, arrived[2]))
+    own_far = swap(lax.optimization_barrier((orbitals, far_kernel))[0])
+    names = (*order[:-1], 0)
+    landed = lax.optimization_barrier(tuple(arrived[d] if d else beside for d in names) + (own_far, weights))
+    arrived = dict(zip(names, landed))
+    beside, weights = arrived[0], landed[-1]
+    own = (orbitals, landed[-2])
     beside = (beside, swap(beside))
-    partners = [own] + [(arrived[d], swap(arrived[d])) for d in order[1:]]
+    partners = [(arrived[d], swap(arrived[d])) for d in order[:-1]] + [own]
     sums = None
-    for at in range(0, lines, 4):
-        sums = apply_pairs(own, beside, partners[at : at + 4], weights, at, side, sums)
+    for at in range(0, lines, GROUP):
+        sums = apply_pairs(own, beside, partners[at : at + GROUP], weights, at // GROUP, side, sums)
     mine, far = sums
     near = swap(far)
     away = lax.ppermute(jnp.where(core == column, near, mine), "kb", across)

time: 31.3 us -> 29.3 us (0.936)
  waiting for transfers between devices: 12.1 us -> 10.9 us
  Pallas kernels: 5.34 us -> 4.5 us
    ppermute x3, waiting for transfers between devices: 5.55 us -> 4.66 us  [from_line(): lax.ppermute(x, 'kb', [(2 * a + c, 2 * (a ^ d) + c) for a in range(lines)...]
    pallas_call x1, Pallas kernels: 3.54 us -> 2.7 us  [apply_pairs(): pl.pallas_call(functools.partial(pair_kernel, side, at_group, sums is not...]
    ppermute x7, waiting for transfers between devices: 2.45 us -> 2.06 us  [swap(): return lax.ppermute(x, 'slab', [(0, 1), (1, 0)])]
    unnamed x18 -> x16, local copies, waits for them, and re-layouts: 2.41 us -> 2.4 us
  transfers between devices with their start and end apart: 12 -> 12, of which waited for: 7 -> 8; matrix products, arithmetic and copies ran while one was open for 0% -> 0% of each run, Pallas kernels for 4% -> 4%
where the time goes in v3:
time: 29.3 us; the launch traced here: 28.9 us
  waiting for transfers between devices  10.9 us (37%)
  starting transfers between devices  10.3 us (35%)
  Pallas kernels  4.5 us (15%)
  local copies, waits for them, and re-layouts  2.4 us (8%)
  between operations  0.71 us (2%)
    ppermute x3, starting transfers between devices, from_line(): lax.ppermute(x, 'kb', [(2 * a + c, 2 * (a ^ d) + c) for a in range(lines)...  5.24 us
    ppermute x3, waiting for transfers between devices, from_line(): lax.ppermute(x, 'kb', [(2 * a + c, 2 * (a ^ d) + c) for a in range(lines)...  4.66 us
    ppermute x1, waiting for transfers between devices, on_device(): away = lax.ppermute(jnp.where(core == column, near, mine), 'kb', across)  4.23 us
    pallas_call x1, Pallas kernels, apply_pairs(): pl.pallas_call(functools.partial(pair_kernel, side, at_group, sums is not...  2.7 us
    unnamed x16, local copies, waits for them, and re-layouts  2.4 us
    ppermute x7, waiting for transfers between devices, swap(): return lax.ppermute(x, 'slab', [(0, 1), (1, 0)])  2.06 us
    ppermute x7, starting transfers between devices, swap(): return lax.ppermute(x, 'slab', [(0, 1), (1, 0)])  1.92 us
    ppermute x1, starting transfers between devices, on_device(): away = lax.ppermute(jnp.where(core == column, near, mine), 'kb', across)  1.65 us
  transfers between devices with their start and end apart: 12, of which 8 were waited for; matrix products, arithmetic and copies ran while one was open for 0% of the time, Pallas kernels for 4%

profile of v3, /device:TPU:0, one launch (start us, length us, event | category | flops | bytes accessed | tf_op | source)
XLA Modules:
  0.0 28.9 jit_solution(7375640825321860452)
XLA Ops:
  0.6 0.5 %collective-permute-start.4 = (f32[8,32,512]{2,1,0:T(8,128)}, f32[8,32,512]{2,1,0:T(8,128)S(1)}, u32[]{:S(2)}, u32[]{:S(2)}) collective-permute-start(f32[8,32,512]{2,1,0:T(8,128)} %mine_ref.1), channel_id=1, source_target_pairs={{0,1},{1,0},{2,3},{3,2},{4,5},{5,4},{6,7},{7,6},{8,9},{9,8},{10,11... | collective-permute-start | bytes 1572872 | tf_op jit(solution)/shard_map/ppermute | solution.py:361
  1.1 3.7 %collective-permute-start = (f32[2,1,16,1024]{3,2,1,0:T(8,128)}, f32[2,1,16,1024]{3,2,1,0:T(8,128)S(1)}, u32[]{:S(2)}, u32[]{:S(2)}) collective-permute-start(f32[2,1,16,1024]{3,2,1,0:T(8,128)} %refs_8_.1), channel_id=1, source_target_pairs={{0,8},{2,10},{4,12},{6,14},{8,0},{10,2},{12,4},{14,6},{1,9},{3,11}... | collective-permute-start | bytes 393224 | tf_op jit(solution)/shard_map/ppermute | solution.py:364
  4.8 1.3 %collective-permute-start.1 = (f32[2,1,16,1024]{3,2,1,0:T(8,128)}, f32[2,1,16,1024]{3,2,1,0:T(8,128)S(1)}, u32[]{:S(2)}, u32[]{:S(2)}) collective-permute-start(f32[2,1,16,1024]{3,2,1,0:T(8,128)} %refs_8_.1), channel_id=1, source_target_pairs={{0,12},{2,14},{4,8},{6,10},{8,4},{10,6},{12,0},{14,2},{1,13},{3,15... | collective-permute-start | bytes 393224 | tf_op jit(solution)/shard_map/ppermute | solution.py:364
  6.2 0.2 collective-permute-start.2
  6.4 1.5 %collective-permute-start.3 = (f32[2,1,16,1024]{3,2,1,0:T(8,128)}, f32[2,1,16,1024]{3,2,1,0:T(8,128)S(1)}, u32[]{:S(2)}, u32[]{:S(2)}) collective-permute-start(f32[2,1,16,1024]{3,2,1,0:T(8,128)} %refs_8_.1), channel_id=1, source_target_pairs={{0,2},{2,0},{4,6},{6,4},{8,10},{10,8},{12,14},{14,12},{1,3},{3,1},... | collective-permute-start | bytes 393224 | tf_op jit(solution)/shard_map/ppermute | solution.py:370
  7.9 0.0 collective-permute-done.4.other_ref
  7.9 0.0 collective-permute-start.5
  7.9 0.0 copy-start
  7.9 1.0 %copy-done = f32[8,32,512]{2,1,0:T(8,128)S(1)} copy-done((f32[8,32,512]{2,1,0:T(8,128)S(1)}, f32[8,32,512]{2,1,0:T(8,128)}, u32[]{:S(2)}) %copy-start) | copy-done | bytes 524312
  9.0 0.0 copy-start.2
  9.0 0.7 %copy-done.2 = s32[8,8]{1,0:T(8,128)S(1)} copy-done((s32[8,8]{1,0:T(8,128)S(1)}, s32[8,8]{1,0:T(8,128)}, u32[]{:S(2)}) %copy-start.2) | copy-done | bytes 280
  9.6 0.0 copy-start.3
  9.7 0.7 %copy-done.3 = s32[8]{0:T(128)S(1)} copy-done((s32[8]{0:T(128)S(1)}, s32[8]{0:T(128)}, u32[]{:S(2)}) %copy-start.3) | copy-done | bytes 56
  10.3 0.0 copy-start.1
  10.3 0.0 copy-start.4
  10.3 0.0 copy-start.5
  10.3 0.0 copy-start.6
  10.3 0.0 copy-start.7
  10.3 1.1 %weights.1.refs_12_ = f32[1,1024,128]{2,1,0:T(8,128)S(1)} custom-call(s32[8,8]{1,0:T(8,128)S(1)} %copy-done.2, s32[8]{0:T(128)S(1)} %copy-done.3, f32[8,32,512]{2,1,0:T(8,128)S(1)} %copy-done, f32[8,32,512]{2,1,0:T(8,128)S(1)} %collective-permute-done.4.other_ref), custom_call_target="tpu_custom_call" | custom-call | flops 20000000000 | bytes 100000000 | tf_op jit(solution)/shard_map/weights/pallas_call | solution.py:280
  11.4 3.6 %collective-permute-done.refs_0_ = f32[2,1,16,1024]{3,2,1,0:T(8,128)S(1)} collective-permute-done((f32[2,1,16,1024]{3,2,1,0:T(8,128)}, f32[2,1,16,1024]{3,2,1,0:T(8,128)S(1)}, u32[]{:S(2)}, u32[]{:S(2)}) %collective-permute-start) | collective-permute-done | bytes 131104 | tf_op jit(solution)/shard_map/ppermute | solution.py:364
  15.0 0.0 collective-permute-done.1.refs_2_
  15.0 1.1 %collective-permute-done.2.refs_4_ = f32[2,1,16,1024]{3,2,1,0:T(8,128)S(1)} collective-permute-done((f32[2,1,16,1024]{3,2,1,0:T(8,128)}, f32[2,1,16,1024]{3,2,1,0:T(8,128)S(1)}, u32[]{:S(2)}, u32[]{:S(2)}) %collective-permute-start.2) | collective-permute-done | bytes 131104 | tf_op jit(solution)/shard_map/ppermute | solution.py:364
  16.1 0.0 collective-permute-done.3.refs_10_
  16.1 0.0 collective-permute-done.5.refs_7_.refs_9_
  16.1 0.0 collective-permute-start.6
  16.1 0.5 %collective-permute-start.7 = (f32[2,1,16,1024]{3,2,1,0:T(8,128)S(1)}, f32[2,1,16,1024]{3,2,1,0:T(8,128)S(1)}, u32[]{:S(2)}, u32[]{:S(2)}) collective-permute-start(f32[2,1,16,1024]{3,2,1,0:T(8,128)S(1)} %collective-permute-done.1.refs_2_), channel_id=1, source_target_pairs={{0,1},{1,0},{2,3},{3,2},{4,5},{5,4},{6,7},{7,6},{8,9},{9,8},{10,11... | collective-permute-start | bytes 393224 | tf_op jit(solution)/shard_map/ppermute | solution.py:361
  16.6 0.1 collective-permute-start.8
  16.7 0.4 %collective-permute-start.9 = (f32[2,1,16,1024]{3,2,1,0:T(8,128)S(1)}, f32[2,1,16,1024]{3,2,1,0:T(8,128)S(1)}, u32[]{:S(2)}, u32[]{:S(2)}) collective-permute-start(f32[2,1,16,1024]{3,2,1,0:T(8,128)S(1)} %collective-permute-done.3.refs_10_), channel_id=1, source_target_pairs={{0,1},{1,0},{2,3},{3,2},{4,5},{5,4},{6,7},{7,6},{8,9},{9,8},{10,11... | collective-permute-start | bytes 393224 | tf_op jit(solution)/shard_map/ppermute | solution.py:361
  17.1 0.3 %collective-permute-done.6.refs_1_ = f32[2,1,16,1024]{3,2,1,0:T(8,128)S(1)} collective-permute-done((f32[2,1,16,1024]{3,2,1,0:T(8,128)S(1)}, f32[2,1,16,1024]{3,2,1,0:T(8,128)S(1)}, u32[]{:S(2)}, u32[]{:S(2)}) %collective-permute-start.6) | collective-permute-done | bytes 131104 | tf_op jit(solution)/shard_map/ppermute | solution.py:361
  17.5 0.2 collective-permute-done.7.refs_3_
  17.6 0.3 %collective-permute-done.8.refs_5_ = f32[2,1,16,1024]{3,2,1,0:T(8,128)S(1)} collective-permute-done((f32[2,1,16,1024]{3,2,1,0:T(8,128)S(1)}, f32[2,1,16,1024]{3,2,1,0:T(8,128)S(1)}, u32[]{:S(2)}, u32[]{:S(2)}) %collective-permute-start.8) | collective-permute-done | bytes 131104 | tf_op jit(solution)/shard_map/ppermute | solution.py:361
  18.0 0.2 collective-permute-done.9.refs_11_
  18.2 0.0 copy-done.1
  18.2 0.0 copy-done.4
  18.2 0.0 copy-done.5
  18.2 0.0 copy-done.6
  18.2 0.0 copy-done.7
  18.2 2.7 %pairs.1 = (f32[264,128]{1,0:T(8,128)S(1)}, f32[264,128]{1,0:T(8,128)S(1)}) custom-call(f32[2,1,16,1024]{3,2,1,0:T(8,128)S(1)} %collective-permute-done.refs_0_, f32[2,1,16,1024]{3,2,1,0:T(8,128)S(1)} %collective-permute-done.6.refs_1_, f32[2,1,16,1024]{3,2,1,0:T(8,128)S(1)} %collective-permute-done.1.refs_2_, ...), custom_call_target="tpu_custom_call" | custom-call | flops 20000000000 | bytes 100000000 | tf_op jit(solution)/shard_map/pairs/pallas_call | solution.py:305
  20.9 0.4 %collective-permute-start.10 = (f32[264,128]{1,0:T(8,128)S(1)}, f32[264,128]{1,0:T(8,128)S(1)}, u32[]{:S(2)}, u32[]{:S(2)}) collective-permute-start(f32[264,128]{1,0:T(8,128)S(1)} %get-tuple-element.21), channel_id=1, source_target_pairs={{0,1},{1,0},{2,3},{3,2},{4,5},{5,4},{6,7},{7,6},{8,9},{9,8},{10,11... | collective-permute-start | bytes 405512 | tf_op jit(solution)/shard_map/ppermute | solution.py:361
  21.3 1.0 %collective-permute-done.10.near_ref = f32[264,128]{1,0:T(8,128)S(1)} collective-permute-done((f32[264,128]{1,0:T(8,128)S(1)}, f32[264,128]{1,0:T(8,128)S(1)}, u32[]{:S(2)}, u32[]{:S(2)}) %collective-permute-start.10) | collective-permute-done | bytes 135200 | tf_op jit(solution)/shard_map/ppermute | solution.py:361
  22.3 1.7 %collective-permute-start.11 = (f32[264,128]{1,0:T(8,128)S(1)}, f32[264,128]{1,0:T(8,128)S(1)}, u32[]{:S(2)}, u32[]{:S(2)}) collective-permute-start(f32[264,128]{1,0:T(8,128)S(1)} %broadcast_select_fusion), channel_id=1, source_target_pairs={{0,2},{2,0},{4,6},{6,4},{8,10},{10,8},{12,14},{14,12},{1,3},{3,1},... | collective-permute-start | bytes 405512 | tf_op jit(solution)/shard_map/ppermute | solution.py:388
  24.0 4.2 %collective-permute-done.11.away_ref = f32[264,128]{1,0:T(8,128)S(1)} collective-permute-done((f32[264,128]{1,0:T(8,128)S(1)}, f32[264,128]{1,0:T(8,128)S(1)}, u32[]{:S(2)}, u32[]{:S(2)}) %collective-permute-start.11) | collective-permute-done | bytes 135200 | tf_op jit(solution)/shard_map/ppermute | solution.py:388
  28.2 0.7 %join.1 = (f32[2,1,16,1024]{3,2,1,0:T(8,128)}, f32[1,1,2]{2,1,0:T(1,128)}) custom-call(f32[264,128]{1,0:T(8,128)S(1)} %get-tuple-element.20.own_ref, f32[264,128]{1,0:T(8,128)S(1)} %collective-permute-done.10.near_ref, f32[264,128]{1,0:T(8,128)S(1)} %collective-permute-done.11.away_ref), custom_call_target="tpu_custom_call" | custom-call | flops 20000000000 | bytes 100000000 | tf_op jit(solution)/shard_map/join/pallas_call | solution.py:325
  (1 shorter events, 0.0 us)
Async XLA Ops:
  0.6 7.3 %collective-permute-start.4 = (f32[8,32,512]{2,1,0:T(8,128)}, f32[8,32,512]{2,1,0:T(8,128)S(1)}, u32[]{:S(2)}, u32[]{:S(2)}) collective-permute-start(f32[8,32,512]{2,1,0:T(8,128)} %mine_ref.1), channel_id=1, source_target_pairs={{0,1},{1,0},{2,3},{3,2},{4,5},{5,4},{6,7},{7,6},{8,9},{9,8},{10,11... | collective-permute-start | bytes 1572872 | tf_op jit(solution)/shard_map/ppermute | solution.py:361
  1.1 13.9 %collective-permute-start = (f32[2,1,16,1024]{3,2,1,0:T(8,128)}, f32[2,1,16,1024]{3,2,1,0:T(8,128)S(1)}, u32[]{:S(2)}, u32[]{:S(2)}) collective-permute-start(f32[2,1,16,1024]{3,2,1,0:T(8,128)} %refs_8_.1), channel_id=1, source_target_pairs={{0,8},{2,10},{4,12},{6,14},{8,0},{10,2},{12,4},{14,6},{1,9},{3,11}... | collective-permute-start | bytes 393224 | tf_op jit(solution)/shard_map/ppermute | solution.py:364
  4.8 10.2 %collective-permute-start.1 = (f32[2,1,16,1024]{3,2,1,0:T(8,128)}, f32[2,1,16,1024]{3,2,1,0:T(8,128)S(1)}, u32[]{:S(2)}, u32[]{:S(2)}) collective-permute-start(f32[2,1,16,1024]{3,2,1,0:T(8,128)} %refs_8_.1), channel_id=1, source_target_pairs={{0,12},{2,14},{4,8},{6,10},{8,4},{10,6},{12,0},{14,2},{1,13},{3,15... | collective-permute-start | bytes 393224 | tf_op jit(solution)/shard_map/ppermute | solution.py:364
  6.2 9.9 %collective-permute-start.2 = (f32[2,1,16,1024]{3,2,1,0:T(8,128)}, f32[2,1,16,1024]{3,2,1,0:T(8,128)S(1)}, u32[]{:S(2)}, u32[]{:S(2)}) collective-permute-start(f32[2,1,16,1024]{3,2,1,0:T(8,128)} %refs_8_.1), channel_id=1, source_target_pairs={{0,4},{2,6},{4,0},{6,2},{8,12},{10,14},{12,8},{14,10},{1,5},{3,7},... | collective-permute-start | bytes 393224 | tf_op jit(solution)/shard_map/ppermute | solution.py:364
  6.4 9.7 %collective-permute-start.3 = (f32[2,1,16,1024]{3,2,1,0:T(8,128)}, f32[2,1,16,1024]{3,2,1,0:T(8,128)S(1)}, u32[]{:S(2)}, u32[]{:S(2)}) collective-permute-start(f32[2,1,16,1024]{3,2,1,0:T(8,128)} %refs_8_.1), channel_id=1, source_target_pairs={{0,2},{2,0},{4,6},{6,4},{8,10},{10,8},{12,14},{14,12},{1,3},{3,1},... | collective-permute-start | bytes 393224 | tf_op jit(solution)/shard_map/ppermute | solution.py:370
  7.9 8.2 %collective-permute-start.5 = (f32[2,1,16,1024]{3,2,1,0:T(8,128)}, f32[2,1,16,1024]{3,2,1,0:T(8,128)S(1)}, u32[]{:S(2)}, u32[]{:S(2)}) collective-permute-start(f32[2,1,16,1024]{3,2,1,0:T(8,128)} %refs_8_.1), channel_id=1, source_target_pairs={{0,1},{1,0},{2,3},{3,2},{4,5},{5,4},{6,7},{7,6},{8,9},{9,8},{10,11... | collective-permute-start | bytes 393224 | tf_op jit(solution)/shard_map/ppermute | solution.py:361
  7.9 1.0 %copy-start = (f32[8,32,512]{2,1,0:T(8,128)S(1)}, f32[8,32,512]{2,1,0:T(8,128)}, u32[]{:S(2)}) copy-start(f32[8,32,512]{2,1,0:T(8,128)} %mine_ref.1) | copy-start | bytes 1572868
  9.0 0.7 %copy-start.2 = (s32[8,8]{1,0:T(8,128)S(1)}, s32[8,8]{1,0:T(8,128)}, u32[]{:S(2)}) copy-start(s32[8,8]{1,0:T(8,128)} %q_ref.1) | copy-start | bytes 772
  9.6 0.7 %copy-start.3 = (s32[8]{0:T(128)S(1)}, s32[8]{0:T(128)}, u32[]{:S(2)}) copy-start(s32[8]{0:T(128)} %owner_ref.1) | copy-start | bytes 100
  10.3 7.9 %copy-start.1 = (f32[2,1,16,1024]{3,2,1,0:T(8,128)S(1)}, f32[2,1,16,1024]{3,2,1,0:T(8,128)}, u32[]{:S(2)}) copy-start(f32[2,1,16,1024]{3,2,1,0:T(8,128)} %refs_8_.1) | copy-start | bytes 393220
  10.3 7.9 %copy-start.4 = (bf16[2,256,256]{2,1,0:T(8,128)(2,1)S(1)}, bf16[2,256,256]{2,1,0:T(8,128)(2,1)}, u32[]{:S(2)}) copy-start(bf16[2,256,256]{2,1,0:T(8,128)(2,1)} %constant.29.clone.refs_13_) | copy-start | bytes 786436
  10.3 7.9 %copy-start.5 = (bf16[2,256,256]{2,1,0:T(8,128)(2,1)S(1)}, bf16[2,256,256]{2,1,0:T(8,128)(2,1)}, u32[]{:S(2)}) copy-start(bf16[2,256,256]{2,1,0:T(8,128)(2,1)} %constant.30.clone.refs_14_) | copy-start | bytes 786436
  10.3 7.9 %copy-start.6 = (f32[8,2,16,128]{3,2,1,0:T(8,128)S(1)}, f32[8,2,16,128]{3,2,1,0:T(8,128)}, u32[]{:S(2)}) copy-start(f32[8,2,16,128]{3,2,1,0:T(8,128)} %constant.31.clone.refs_15_) | copy-start | bytes 393220
  10.3 7.9 %copy-start.7 = (f32[16,2,8,128]{3,2,1,0:T(8,128)S(1)}, f32[16,2,8,128]{3,2,1,0:T(8,128)}, u32[]{:S(2)}) copy-start(f32[16,2,8,128]{3,2,1,0:T(8,128)} %constant.32.clone.refs_16_) | copy-start | bytes 393220
  16.1 1.4 %collective-permute-start.6 = (f32[2,1,16,1024]{3,2,1,0:T(8,128)S(1)}, f32[2,1,16,1024]{3,2,1,0:T(8,128)S(1)}, u32[]{:S(2)}, u32[]{:S(2)}) collective-permute-start(f32[2,1,16,1024]{3,2,1,0:T(8,128)S(1)} %collective-permute-done.refs_0_), channel_id=1, source_target_pairs={{0,1},{1,0},{2,3},{3,2},{4,5},{5,4},{6,7},{7,6},{8,9},{9,8},{10,11... | collective-permute-start | bytes 393224 | tf_op jit(solution)/shard_map/ppermute | solution.py:361
  16.1 1.5 %collective-permute-start.7 = (f32[2,1,16,1024]{3,2,1,0:T(8,128)S(1)}, f32[2,1,16,1024]{3,2,1,0:T(8,128)S(1)}, u32[]{:S(2)}, u32[]{:S(2)}) collective-permute-start(f32[2,1,16,1024]{3,2,1,0:T(8,128)S(1)} %collective-permute-done.1.refs_2_), channel_id=1, source_target_pairs={{0,1},{1,0},{2,3},{3,2},{4,5},{5,4},{6,7},{7,6},{8,9},{9,8},{10,11... | collective-permute-start | bytes 393224 | tf_op jit(solution)/shard_map/ppermute | solution.py:361
  16.6 1.3 %collective-permute-start.8 = (f32[2,1,16,1024]{3,2,1,0:T(8,128)S(1)}, f32[2,1,16,1024]{3,2,1,0:T(8,128)S(1)}, u32[]{:S(2)}, u32[]{:S(2)}) collective-permute-start(f32[2,1,16,1024]{3,2,1,0:T(8,128)S(1)} %collective-permute-done.2.refs_4_), channel_id=1, source_target_pairs={{0,1},{1,0},{2,3},{3,2},{4,5},{5,4},{6,7},{7,6},{8,9},{9,8},{10,11... | collective-permute-start | bytes 393224 | tf_op jit(solution)/shard_map/ppermute | solution.py:361
  16.7 1.5 %collective-permute-start.9 = (f32[2,1,16,1024]{3,2,1,0:T(8,128)S(1)}, f32[2,1,16,1024]{3,2,1,0:T(8,128)S(1)}, u32[]{:S(2)}, u32[]{:S(2)}) collective-permute-start(f32[2,1,16,1024]{3,2,1,0:T(8,128)S(1)} %collective-permute-done.3.refs_10_), channel_id=1, source_target_pairs={{0,1},{1,0},{2,3},{3,2},{4,5},{5,4},{6,7},{7,6},{8,9},{9,8},{10,11... | collective-permute-start | bytes 393224 | tf_op jit(solution)/shard_map/ppermute | solution.py:361
  20.9 1.4 %collective-permute-start.10 = (f32[264,128]{1,0:T(8,128)S(1)}, f32[264,128]{1,0:T(8,128)S(1)}, u32[]{:S(2)}, u32[]{:S(2)}) collective-permute-start(f32[264,128]{1,0:T(8,128)S(1)} %get-tuple-element.21), channel_id=1, source_target_pairs={{0,1},{1,0},{2,3},{3,2},{4,5},{5,4},{6,7},{7,6},{8,9},{9,8},{10,11... | collective-permute-start | bytes 405512 | tf_op jit(solution)/shard_map/ppermute | solution.py:361
  22.3 5.9 %collective-permute-start.11 = (f32[264,128]{1,0:T(8,128)S(1)}, f32[264,128]{1,0:T(8,128)S(1)}, u32[]{:S(2)}, u32[]{:S(2)}) collective-permute-start(f32[264,128]{1,0:T(8,128)S(1)} %broadcast_select_fusion), channel_id=1, source_target_pairs={{0,2},{2,0},{4,6},{6,4},{8,10},{10,8},{12,14},{14,12},{1,3},{3,1},... | collective-permute-start | bytes 405512 | tf_op jit(solution)/shard_map/ppermute | solution.py:388

commit v4 on v3

--- a/solution.py
+++ b/solution.py
@@ -10,6 +10,8 @@
 from jax.sharding import PartitionSpec as P
 
 NK = 8
+SUBLANES = 8
+STEP = 9
 GROUP = 4
 LANES = 128
 F32 = jnp.float32
@@ -32,8 +34,8 @@
 
 
 def turn_table(side):
-    phase = 2.0 * math.pi * np.outer(np.arange(side // 2), np.arange(2 * GROUP) // GROUP) / side
-    both = np.stack([np.cos(phase), np.sin(phase)], 1).astype(np.float32)
+    phase = 2.0 * math.pi * np.arange(side // 2) / side
+    both = np.stack([np.cos(phase), np.sin(phase)]).astype(np.float32)
     return np.ascontiguousarray(np.broadcast_to(both[..., None], (*both.shape, LANES)))
 
 
@@ -120,14 +122,14 @@
                 if shift:
                     piece = pltpu.roll(piece, shift, 1)
                 total = piece if total is None else jnp.where(lane == a, piece, total)
-            at = pl.ds(b * GROUP * side + pair % GROUP, side, stride=GROUP)
-            weight_ref[pair // GROUP, at, :] = total
-
-
-def pair_kernel(side, at_group, has_sum, *refs):
+            at = pl.ds(b // GROUP * GROUP * side + b % GROUP, side, stride=GROUP)
+            weight_ref[pair, at, :] = total
+
+
+def pair_kernel(side, count, first, has_sum, *refs):
     refs = list(refs)
     take = lambda n: [refs.pop(0) for _ in range(n)]
-    partners = [take(2) for _ in range(GROUP)]
+    partners = [take(2) for _ in range(count)]
     own, beside = take(2), take(2)
     (weight_ref,) = take(1)
     lane_f, lane_b, twist, turn = take(4)
@@ -143,99 +145,115 @@
     def parts(ref):
         return ref[0], ref[1]
 
-    sign = jnp.where(lax.broadcasted_iota(jnp.int32, (subs, LANES), 0) < GROUP, 1.0, -1.0)
-
-    def halves(value):
-        return pltpu.roll(value, GROUP, 0) + value * sign
-
     home = lax.axis_index("kb") % 2 == lax.axis_index("slab")
     for h in range(2):
         target[h] = jnp.where(home, own[h][:, 0], beside[h][:, 0])
 
-    for p in range(GROUP):
-        for h in range(2):
-            values = []
-            for t in range(tiles):
-                t_re, t_im = target[h, 0, :, lane_slice(t)], target[h, 1, :, lane_slice(t)]
-                p_re = partners[p][h][0, 0, :, lane_slice(t)]
-                p_im = partners[p][h][1, 0, :, lane_slice(t)]
-                values.append((p_re * t_re + p_im * t_im, p_re * t_im - p_im * t_re))
-            for b, (re, im) in enumerate(dft_list(values, -1)):
-                if b:
-                    cosine, sine = twist[b, 0], twist[b, 1]
-                    re, im = re * cosine + im * sine, im * cosine - re * sine
-                at = pl.ds(b * rows + h * GROUP + p, half, stride=subs)
-                x_re[at, :] = re
-                x_im[at, :] = im
-    def forward(b):
-        values = []
-        for x in range(half):
-            at = pl.ds(b * rows + x * subs, subs)
-            re, im = halves(x_re[at, :]), halves(x_im[at, :])
-            if x:
-                cosine, sine = turn[x, 0], turn[x, 1]
-                re, im = re * cosine + im * sine, im * cosine - re * sine
-            values.append((re, im))
+    groups = tiles // GROUP
+
+    def spread(p, b, x, parity):
+        start = ((p * groups + b // GROUP) * half + x) * STEP + parity * GROUP + b % GROUP
+        return pl.ds(start, SUBLANES, stride=STEP)
+
+    def packed(g, x):
+        return pl.ds((g * half + x) * STEP, subs)
+
+    def densities(p):
+        for x in range(0, half, SUBLANES):
+            block = pl.ds(x, SUBLANES)
+            both = []
+            for h in range(2):
+                values = []
+                for t in range(tiles):
+                    t_re, t_im = target[h, 0, block, lane_slice(t)], target[h, 1, block, lane_slice(t)]
+                    p_re = partners[p][h][0, 0, block, lane_slice(t)]
+                    p_im = partners[p][h][1, 0, block, lane_slice(t)]
+                    values.append((p_re * t_re + p_im * t_im, p_re * t_im - p_im * t_re))
+                both.append(dft_list(values, -1))
+            turn_re, turn_im = turn[0, block], turn[1, block]
+            for b in range(tiles):
+                (re_0, im_0), (re_1, im_1) = both[0][b], both[1][b]
+                re, im = re_0 - re_1, im_0 - im_1
+                even = re_0 + re_1, im_0 + im_1
+                odd = re * turn_re + im * turn_im, im * turn_re - re * turn_im
+                for parity, (re, im) in enumerate((even, odd)):
+                    if b:
+                        cosine, sine = twist[b, 0], twist[b, 1]
+                        re, im = re * cosine + im * sine, im * cosine - re * sine
+                    x_re[spread(p, b, x, parity), :] = re
+                    x_im[spread(p, b, x, parity), :] = im
+
+    def forward(g):
+        values = [(x_re[packed(g, x), :], x_im[packed(g, x), :]) for x in range(half)]
         values = dft_list(values, -1)
         for x in range(0, half, 2):
-            at = pl.ds(b * rows + x * subs, 2 * subs)
+            at = pl.ds(g * rows + x * subs, 2 * subs)
             for k in range(2):
                 high, low = split(jnp.concatenate([values[x][k], values[x + 1][k]], 0))
                 high_ref[at, lane_slice(k)] = high
                 low_ref[at, lane_slice(k)] = low
 
-    def middle(b):
-        at = pl.ds(b * rows, rows)
+    def middle(g):
+        at = pl.ds(g * rows, rows)
         spectrum = dot_parts((high_ref[at, :], low_ref[at, :]), parts(lane_f))
-        weights = weight_ref[at_group, at, :]
+        weights = weight_ref[first + g // groups, pl.ds(g % groups * rows, rows), :]
         weighted = split(spectrum * jnp.concatenate([weights, weights], 1))
         g_ref[at, :] = dot_parts(weighted, parts(lane_b))
 
-    def backward(b):
+    def backward(g):
         values = []
         for x in range(half):
-            at = pl.ds(b * rows + x * subs, subs)
+            at = pl.ds(g * rows + x * subs, subs)
             values.append((g_ref[at, lane_slice(0)], g_ref[at, lane_slice(1)]))
         for x, (re, im) in enumerate(dft_list(values, 1)):
-            if x:
-                cosine, sine = turn[x, 0], turn[x, 1]
-                re, im = re * cosine - im * sine, im * cosine + re * sine
-            at = pl.ds(b * rows + x * subs, subs)
-            x_re[at, :] = halves(re)
-            x_im[at, :] = halves(im)
-
-    for b in range(tiles):
-        forward(b)
-        middle(b)
-        backward(b)
-    gram_re = jnp.zeros((half, LANES), F32)
-    gram_im = jnp.zeros((half, LANES), F32)
-    for h in range(2):
-        total = [[0.0, 0.0] for _ in range(tiles)]
+            x_re[packed(g, x), :] = re
+            x_im[packed(g, x), :] = im
+
+    for p in range(count):
+        densities(p)
+        for g in range(p * groups, (p + 1) * groups):
+            forward(g)
+            middle(g)
+            backward(g)
+    gram_re = jnp.zeros((SUBLANES, LANES), F32)
+    gram_im = jnp.zeros((SUBLANES, LANES), F32)
+    for x in range(0, half, SUBLANES):
+        block = pl.ds(x, SUBLANES)
+        total = [[[0.0, 0.0] for _ in range(tiles)] for _ in range(2)]
         if has_sum:
+            for h in range(2):
+                for t in range(tiles):
+                    for k in range(2):
+                        total[h][t][k] = sums[h][pl.ds((k * tiles + t) * half + x, SUBLANES), :]
+        turn_re, turn_im = turn[0, block], turn[1, block]
+        for p in range(count):
+            both = [], []
+            for b in range(tiles):
+                pair = []
+                for parity in range(2):
+                    re, im = x_re[spread(p, b, x, parity), :], x_im[spread(p, b, x, parity), :]
+                    if b:
+                        cosine, sine = twist[b, 0], twist[b, 1]
+                        re, im = re * cosine - im * sine, im * cosine + re * sine
+                    pair.append((re, im))
+                re, im = pair[1]
+                re, im = re * turn_re - im * turn_im, im * turn_re + re * turn_im
+                both[0].append((pair[0][0] + re, pair[0][1] + im))
+                both[1].append((pair[0][0] - re, pair[0][1] - im))
+            for h in range(2):
+                for t, (re, im) in enumerate(dft_list(both[h], 1)):
+                    p_re = partners[p][h][0, 0, block, lane_slice(t)]
+                    p_im = partners[p][h][1, 0, block, lane_slice(t)]
+                    total[h][t][0] = total[h][t][0] + (p_re * re - p_im * im)
+                    total[h][t][1] = total[h][t][1] + (p_re * im + p_im * re)
+        for h in range(2):
             for t in range(tiles):
-                total[t] = [sums[h][pl.ds((k * tiles + t) * half, half), :] for k in range(2)]
-        for p in range(GROUP):
-            values = []
-            for b in range(tiles):
-                at = pl.ds(b * rows + h * GROUP + p, half, stride=subs)
-                re, im = x_re[at, :], x_im[at, :]
-                if b:
-                    cosine, sine = twist[b, 0], twist[b, 1]
-                    re, im = re * cosine - im * sine, im * cosine + re * sine
-                values.append((re, im))
-            for t, (re, im) in enumerate(dft_list(values, 1)):
-                p_re = partners[p][h][0, 0, :, lane_slice(t)]
-                p_im = partners[p][h][1, 0, :, lane_slice(t)]
-                total[t][0] = total[t][0] + (p_re * re - p_im * im)
-                total[t][1] = total[t][1] + (p_re * im + p_im * re)
-        for t in range(tiles):
-            re, im = total[t]
-            t_re, t_im = target[h, 0, :, lane_slice(t)], target[h, 1, :, lane_slice(t)]
-            gram_re += t_re * re + t_im * im
-            gram_im += t_re * im - t_im * re
-            outs[h][pl.ds(t * half, half), :] = re
-            outs[h][pl.ds((tiles + t) * half, half), :] = im
+                re, im = total[h][t]
+                t_re, t_im = target[h, 0, block, lane_slice(t)], target[h, 1, block, lane_slice(t)]
+                gram_re += t_re * re + t_im * im
+                gram_im += t_re * im - t_im * re
+                outs[h][pl.ds(t * half + x, SUBLANES), :] = re
+                outs[h][pl.ds((tiles + t) * half + x, SUBLANES), :] = im
     end = 2 * tiles * half
     scale = 1.0 / side**3
     sums_row = jnp.concatenate(
@@ -279,7 +297,7 @@
 def choose_weights(q_index, owner, kernels, order, side, blocks_per_k):
     return pl.pallas_call(
         functools.partial(weight_kernel, side, blocks_per_k, order),
-        out_shape=jax.ShapeDtypeStruct((len(order) // GROUP, GROUP * side**3 // LANES, LANES), F32),
+        out_shape=jax.ShapeDtypeStruct((len(order), side**3 // LANES, LANES), F32),
         in_specs=[SMEM, SMEM, VMEM, VMEM],
         out_specs=VMEM,
         compiler_params=params(),
@@ -288,29 +306,30 @@
     )(q_index, owner, *kernels)
 
 
-def apply_pairs(own, beside, partners, weights, at_group, side, sums=None):
+def apply_pairs(own, beside, partners, weights, first, side, sums=None):
+    count = len(partners)
     half = side // 2
     tiles = side * side // LANES
-    rows = tiles * half * 2 * GROUP
+    rows = count * side**3 // LANES
     lane = lane_table(side)
     tables = [
         jnp.asarray(bf16_parts(lane)),
         jnp.asarray(bf16_parts(lane.T)),
-        jnp.asarray(twist_table(side, half)),
+        jnp.asarray(twist_table(side, SUBLANES)),
         jnp.asarray(turn_table(side)),
     ]
     operands = [x for pair in partners for x in pair] + [*own, *beside, weights] + tables
     operands += list(sums) if sums is not None else []
     message = jax.ShapeDtypeStruct((2 * tiles * half + 8, LANES), F32)
     return pl.pallas_call(
-        functools.partial(pair_kernel, side, at_group, sums is not None),
+        functools.partial(pair_kernel, side, count, first, sums is not None),
         out_shape=(message, message),
         in_specs=[VMEM] * len(operands),
         out_specs=(VMEM, VMEM),
         scratch_shapes=[
             pltpu.VMEM((2, 2, half, side * side), F32),
-            pltpu.VMEM((rows, LANES), F32),
-            pltpu.VMEM((rows, LANES), F32),
+            pltpu.VMEM((rows // SUBLANES * STEP, LANES), F32),
+            pltpu.VMEM((rows // SUBLANES * STEP, LANES), F32),
             pltpu.VMEM((rows, 2 * LANES), BF16),
             pltpu.VMEM((rows, 2 * LANES), BF16),
             pltpu.VMEM((rows, 2 * LANES), F32),
@@ -365,24 +384,36 @@
             x, "kb", [(2 * a + c, 2 * (a ^ d) + c) for a in range(lines) for c in range(2)]
         )
 
-    order = [*range(2, lines), 1, 0]
-    arrived = {d: from_line(orbitals, d) for d in order[:-1]}
-    beside = lax.ppermute(orbitals, "kb", across)
+    order = [0, 1, *range(2, lines)]
+    first = [2, 1, 0]
+    last = [d for d in order if d and d not in first]
+    arrived = {d: from_line(orbitals, d) for d in order[1:]}
+    arrived[0] = lax.ppermute(orbitals, "kb", across)
     far_kernel = swap(kernel)
     weights = choose_weights(
         q_index, owner, (kernel, far_kernel), tuple(order), side, blocks_per_k
     )
     own_far = swap(lax.optimization_barrier((orbitals, far_kernel))[0])
-    names = (*order[:-1], 0)
-    landed = lax.optimization_barrier(tuple(arrived[d] if d else beside for d in names) + (own_far, weights))
-    arrived = dict(zip(names, landed))
-    beside, weights = arrived[0], landed[-1]
-    own = (orbitals, landed[-2])
-    beside = (beside, swap(beside))
-    partners = [(arrived[d], swap(arrived[d])) for d in order[:-1]] + [own]
+    landed = lax.optimization_barrier((*(arrived[d] for d in first), weights))
+    arrived.update(zip(first, landed))
+    weights = landed[-1]
+    far = {d: swap(arrived[d]) for d in first}
+    landed = lax.optimization_barrier(
+        (*(arrived[d] for d in last), *(far[d] for d in first), own_far)
+    )
+    arrived.update(zip(last, landed))
+    far.update(zip(first, landed[len(last) :]))
+    own = (orbitals, landed[-1])
+    far.update({d: swap(arrived[d]) for d in last})
+    beside = (arrived[0], far[0])
+    partners = [own] + [(arrived[d], far[d]) for d in order[1:]]
+    if lines <= 4:
+        groups = [(0, lines - 1), (lines - 1, lines)]
+    else:
+        groups = [(at, min(at + 4, lines)) for at in range(0, lines, 4)]
     sums = None
-    for at in range(0, lines, GROUP):
-        sums = apply_pairs(own, beside, partners[at : at + GROUP], weights, at // GROUP, side, sums)
+    for at, end in groups:
+        sums = apply_pairs(own, beside, partners[at:end], weights, at, side, sums)
     mine, far = sums
     near = swap(far)
     away = lax.ppermute(jnp.where(core == column, near, mine), "kb", across)

time: 29.3 us -> 27.4 us (0.935)
  waiting for transfers between devices: 10.9 us -> 8.6 us
  starting transfers between devices: 10.3 us -> 10.7 us
    ppermute x3, waiting for transfers between devices: 4.66 us -> 3.28 us  [from_line(): lax.ppermute(x, 'kb', [(2 * a + c, 2 * (a ^ d) + c) for a in range(lines)...]
    ppermute x7, waiting for transfers between devices: 2.06 us -> 1.01 us  [swap(): return lax.ppermute(x, 'slab', [(0, 1), (1, 0)])]
    pallas_call x1 -> x2, Pallas kernels: 2.7 us -> 2.72 us  [apply_pairs(): pl.pallas_call(functools.partial(pair_kernel, side, count, first, sums is...]
  transfers between devices with their start and end apart: 12 -> 12, of which waited for: 8 -> 4; matrix products, arithmetic and copies ran while one was open for 0% -> 0% of each run, Pallas kernels for 4% -> 11%
where the time goes in v4:
time: 27.4 us; the launch traced here: 27 us
  starting transfers between devices  10.7 us (39%)
  waiting for transfers between devices  8.6 us (31%)
  Pallas kernels  4.51 us (16%)
  local copies, waits for them, and re-layouts  2.4 us (9%)
  between operations  0.75 us (3%)
    ppermute x3, starting transfers between devices, from_line(): lax.ppermute(x, 'kb', [(2 * a + c, 2 * (a ^ d) + c) for a in range(lines)...  5.46 us
    ppermute x1, waiting for transfers between devices, on_device(): away = lax.ppermute(jnp.where(core == column, near, mine), 'kb', across)  4.32 us
    ppermute x3, waiting for transfers between devices, from_line(): lax.ppermute(x, 'kb', [(2 * a + c, 2 * (a ^ d) + c) for a in range(lines)...  3.28 us
    pallas_call x2, Pallas kernels, apply_pairs(): pl.pallas_call(functools.partial(pair_kernel, side, count, first, sums is...  2.72 us
    unnamed x16, local copies, waits for them, and re-layouts  2.4 us
    ppermute x7, starting transfers between devices, swap(): return lax.ppermute(x, 'slab', [(0, 1), (1, 0)])  2.14 us
    ppermute x1, starting transfers between devices, on_device(): away = lax.ppermute(jnp.where(core == column, near, mine), 'kb', across)  1.6 us
    ppermute x1, starting transfers between devices, on_device(): arrived[0] = lax.ppermute(orbitals, 'kb', across)  1.52 us
  transfers between devices with their start and end apart: 12, of which 4 were waited for; matrix products, arithmetic and copies ran while one was open for 0% of the time, Pallas kernels for 11%

profile of v4, /device:TPU:0, one launch (start us, length us, event | category | flops | bytes accessed | tf_op | source)
XLA Modules:
  0.0 27.0 jit_solution(4694839012627304001)
XLA Ops:
  0.6 0.5 %collective-permute-start.4 = (f32[8,32,512]{2,1,0:T(8,128)}, f32[8,32,512]{2,1,0:T(8,128)S(1)}, u32[]{:S(2)}, u32[]{:S(2)}) collective-permute-start(f32[8,32,512]{2,1,0:T(8,128)} %mine_ref.1), channel_id=1, source_target_pairs={{0,1},{1,0},{2,3},{3,2},{4,5},{5,4},{6,7},{7,6},{8,9},{9,8},{10,11... | collective-permute-start | bytes 1572872 | tf_op jit(solution)/shard_map/ppermute | solution.py:380
  1.1 3.7 %collective-permute-start.1 = (f32[2,1,16,1024]{3,2,1,0:T(8,128)}, f32[2,1,16,1024]{3,2,1,0:T(8,128)S(1)}, u32[]{:S(2)}, u32[]{:S(2)}) collective-permute-start(f32[2,1,16,1024]{3,2,1,0:T(8,128)} %refs_2_.1), channel_id=1, source_target_pairs={{0,8},{2,10},{4,12},{6,14},{8,0},{10,2},{12,4},{14,6},{1,9},{3,11}... | collective-permute-start | bytes 393224 | tf_op jit(solution)/shard_map/ppermute | solution.py:383
  4.8 1.6 %collective-permute-start.2 = (f32[2,1,16,1024]{3,2,1,0:T(8,128)}, f32[2,1,16,1024]{3,2,1,0:T(8,128)S(1)}, u32[]{:S(2)}, u32[]{:S(2)}) collective-permute-start(f32[2,1,16,1024]{3,2,1,0:T(8,128)} %refs_2_.1), channel_id=1, source_target_pairs={{0,4},{2,6},{4,0},{6,2},{8,12},{10,14},{12,8},{14,10},{1,5},{3,7},... | collective-permute-start | bytes 393224 | tf_op jit(solution)/shard_map/ppermute | solution.py:383
  6.4 1.5 %collective-permute-start.3 = (f32[2,1,16,1024]{3,2,1,0:T(8,128)}, f32[2,1,16,1024]{3,2,1,0:T(8,128)S(1)}, u32[]{:S(2)}, u32[]{:S(2)}) collective-permute-start(f32[2,1,16,1024]{3,2,1,0:T(8,128)} %refs_2_.1), channel_id=1, source_target_pairs={{0,2},{2,0},{4,6},{6,4},{8,10},{10,8},{12,14},{14,12},{1,3},{3,1},... | collective-permute-start | bytes 393224 | tf_op jit(solution)/shard_map/ppermute | solution.py:391
  7.9 0.2 collective-permute-start
  8.1 0.0 collective-permute-done.4.other_ref
  8.1 0.0 copy-start
  8.1 1.0 %copy-done = f32[8,32,512]{2,1,0:T(8,128)S(1)} copy-done((f32[8,32,512]{2,1,0:T(8,128)S(1)}, f32[8,32,512]{2,1,0:T(8,128)}, u32[]{:S(2)}) %copy-start) | copy-done | bytes 524312
  9.2 0.0 copy-start.2
  9.2 0.7 %copy-done.2 = s32[8,8]{1,0:T(8,128)S(1)} copy-done((s32[8,8]{1,0:T(8,128)S(1)}, s32[8,8]{1,0:T(8,128)}, u32[]{:S(2)}) %copy-start.2) | copy-done | bytes 280
  9.9 0.0 copy-start.3
  9.9 0.7 %copy-done.3 = s32[8]{0:T(128)S(1)} copy-done((s32[8]{0:T(128)S(1)}, s32[8]{0:T(128)}, u32[]{:S(2)}) %copy-start.3) | copy-done | bytes 56
  10.5 0.0 copy-start.1
  10.5 0.0 copy-start.4
  10.5 0.0 copy-start.5
  10.5 0.0 copy-start.6
  10.5 0.0 copy-start.7
  10.5 1.1 %weights.1.refs_10_.refs_6_ = f32[4,256,128]{2,1,0:T(8,128)S(1)} custom-call(s32[8,8]{1,0:T(8,128)S(1)} %copy-done.2, s32[8]{0:T(128)S(1)} %copy-done.3, f32[8,32,512]{2,1,0:T(8,128)S(1)} %copy-done, f32[8,32,512]{2,1,0:T(8,128)S(1)} %collective-permute-done.4.other_ref), custom_call_target="tpu_custom_call" | custom-call | flops 20000000000 | bytes 100000000 | tf_op jit(solution)/shard_map/weights/pallas_call | solution.py:298
  11.7 0.6 %collective-permute-done.1.refs_4_ = f32[2,1,16,1024]{3,2,1,0:T(8,128)S(1)} collective-permute-done((f32[2,1,16,1024]{3,2,1,0:T(8,128)}, f32[2,1,16,1024]{3,2,1,0:T(8,128)S(1)}, u32[]{:S(2)}, u32[]{:S(2)}) %collective-permute-start.1) | collective-permute-done | bytes 131104 | tf_op jit(solution)/shard_map/ppermute | solution.py:383
  12.2 0.0 collective-permute-done.2.refs_2_
  12.2 0.0 collective-permute-done.3.refs_8_.refs_4_
  12.2 0.0 collective-permute-start.7
  12.2 0.5 %collective-permute-start.5 = (f32[2,1,16,1024]{3,2,1,0:T(8,128)S(1)}, f32[2,1,16,1024]{3,2,1,0:T(8,128)S(1)}, u32[]{:S(2)}, u32[]{:S(2)}) collective-permute-start(f32[2,1,16,1024]{3,2,1,0:T(8,128)S(1)} %collective-permute-done.1.refs_4_), channel_id=1, source_target_pairs={{0,1},{1,0},{2,3},{3,2},{4,5},{5,4},{6,7},{7,6},{8,9},{9,8},{10,11... | collective-permute-start | bytes 393224 | tf_op jit(solution)/shard_map/ppermute | solution.py:380
  12.7 0.1 collective-permute-start.6
  12.8 0.0 copy-done.1
  12.8 0.4 %collective-permute-start.8 = (f32[2,1,16,1024]{3,2,1,0:T(8,128)S(1)}, f32[2,1,16,1024]{3,2,1,0:T(8,128)S(1)}, u32[]{:S(2)}, u32[]{:S(2)}) collective-permute-start(f32[2,1,16,1024]{3,2,1,0:T(8,128)S(1)} %copy-done.1), channel_id=1, source_target_pairs={{0,1},{1,0},{2,3},{3,2},{4,5},{5,4},{6,7},{7,6},{8,9},{9,8},{10,11... | collective-permute-start | bytes 393224 | tf_op jit(solution)/shard_map/ppermute | solution.py:380
  13.3 2.7 %collective-permute-done.refs_0_ = f32[2,1,16,1024]{3,2,1,0:T(8,128)S(1)} collective-permute-done((f32[2,1,16,1024]{3,2,1,0:T(8,128)}, f32[2,1,16,1024]{3,2,1,0:T(8,128)S(1)}, u32[]{:S(2)}, u32[]{:S(2)}) %collective-permute-start) | collective-permute-done | bytes 131104 | tf_op jit(solution)/shard_map/ppermute | solution.py:383
  16.0 0.0 collective-permute-done.7.refs_9_.refs_5_
  16.0 0.0 collective-permute-done.5.refs_5_
  16.0 0.0 collective-permute-done.6.refs_3_
  16.0 0.0 collective-permute-done.8.refs_1_.refs_7_.refs_3_
  16.0 0.1 collective-permute-start.9
  16.1 0.0 copy-done.4
  16.1 0.0 copy-done.5
  16.1 0.0 copy-done.6
  16.1 0.0 copy-done.7
  16.1 1.7 %pairs.2 = (f32[264,128]{1,0:T(8,128)S(1)}, f32[264,128]{1,0:T(8,128)S(1)}) custom-call(f32[2,1,16,1024]{3,2,1,0:T(8,128)S(1)} %copy-done.1, f32[2,1,16,1024]{3,2,1,0:T(8,128)S(1)} %collective-permute-done.8.refs_1_.refs_7_.refs_3_, f32[2,1,16,1024]{3,2,1,0:T(8,128)S(1)} %collective-permute-done.2.refs_2_, ...), custom_call_target="tpu_custom_call" | custom-call | flops 20000000000 | bytes 100000000 | tf_op jit(solution)/shard_map/pairs/pallas_call | solution.py:324
  17.9 0.0 collective-permute-done.9.refs_1_
  17.9 1.0 %pairs.3 = (f32[264,128]{1,0:T(8,128)S(1)}, f32[264,128]{1,0:T(8,128)S(1)}) custom-call(f32[2,1,16,1024]{3,2,1,0:T(8,128)S(1)} %collective-permute-done.refs_0_, f32[2,1,16,1024]{3,2,1,0:T(8,128)S(1)} %collective-permute-done.9.refs_1_, f32[2,1,16,1024]{3,2,1,0:T(8,128)S(1)} %copy-done.1, ...), custom_call_target="tpu_custom_call" | custom-call | flops 20000000000 | bytes 100000000 | tf_op jit(solution)/shard_map/pairs/pallas_call | solution.py:324
  18.8 0.5 %collective-permute-start.10 = (f32[264,128]{1,0:T(8,128)S(1)}, f32[264,128]{1,0:T(8,128)S(1)}, u32[]{:S(2)}, u32[]{:S(2)}) collective-permute-start(f32[264,128]{1,0:T(8,128)S(1)} %get-tuple-element.31), channel_id=1, source_target_pairs={{0,1},{1,0},{2,3},{3,2},{4,5},{5,4},{6,7},{7,6},{8,9},{9,8},{10,11... | collective-permute-start | bytes 405512 | tf_op jit(solution)/shard_map/ppermute | solution.py:380
  19.4 1.0 %collective-permute-done.10.near_ref = f32[264,128]{1,0:T(8,128)S(1)} collective-permute-done((f32[264,128]{1,0:T(8,128)S(1)}, f32[264,128]{1,0:T(8,128)S(1)}, u32[]{:S(2)}, u32[]{:S(2)}) %collective-permute-start.10) | collective-permute-done | bytes 135200 | tf_op jit(solution)/shard_map/ppermute | solution.py:380
  20.4 1.6 %collective-permute-start.11 = (f32[264,128]{1,0:T(8,128)S(1)}, f32[264,128]{1,0:T(8,128)S(1)}, u32[]{:S(2)}, u32[]{:S(2)}) collective-permute-start(f32[264,128]{1,0:T(8,128)S(1)} %broadcast_select_fusion), channel_id=1, source_target_pairs={{0,2},{2,0},{4,6},{6,4},{8,10},{10,8},{12,14},{14,12},{1,3},{3,1},... | collective-permute-start | bytes 405512 | tf_op jit(solution)/shard_map/ppermute | solution.py:419
  22.0 4.3 %collective-permute-done.11.away_ref = f32[264,128]{1,0:T(8,128)S(1)} collective-permute-done((f32[264,128]{1,0:T(8,128)S(1)}, f32[264,128]{1,0:T(8,128)S(1)}, u32[]{:S(2)}, u32[]{:S(2)}) %collective-permute-start.11) | collective-permute-done | bytes 135200 | tf_op jit(solution)/shard_map/ppermute | solution.py:419
  26.3 0.7 %join.1 = (f32[2,1,16,1024]{3,2,1,0:T(8,128)}, f32[1,1,2]{2,1,0:T(1,128)}) custom-call(f32[264,128]{1,0:T(8,128)S(1)} %get-tuple-element.30.own_ref, f32[264,128]{1,0:T(8,128)S(1)} %collective-permute-done.10.near_ref, f32[264,128]{1,0:T(8,128)S(1)} %collective-permute-done.11.away_ref), custom_call_target="tpu_custom_call" | custom-call | flops 20000000000 | bytes 100000000 | tf_op jit(solution)/shard_map/join/pallas_call | solution.py:344
  (1 shorter events, 0.0 us)
Async XLA Ops:
  0.6 7.5 %collective-permute-start.4 = (f32[8,32,512]{2,1,0:T(8,128)}, f32[8,32,512]{2,1,0:T(8,128)S(1)}, u32[]{:S(2)}, u32[]{:S(2)}) collective-permute-start(f32[8,32,512]{2,1,0:T(8,128)} %mine_ref.1), channel_id=1, source_target_pairs={{0,1},{1,0},{2,3},{3,2},{4,5},{5,4},{6,7},{7,6},{8,9},{9,8},{10,11... | collective-permute-start | bytes 1572872 | tf_op jit(solution)/shard_map/ppermute | solution.py:380
  1.1 11.1 %collective-permute-start.1 = (f32[2,1,16,1024]{3,2,1,0:T(8,128)}, f32[2,1,16,1024]{3,2,1,0:T(8,128)S(1)}, u32[]{:S(2)}, u32[]{:S(2)}) collective-permute-start(f32[2,1,16,1024]{3,2,1,0:T(8,128)} %refs_2_.1), channel_id=1, source_target_pairs={{0,8},{2,10},{4,12},{6,14},{8,0},{10,2},{12,4},{14,6},{1,9},{3,11}... | collective-permute-start | bytes 393224 | tf_op jit(solution)/shard_map/ppermute | solution.py:383
  4.8 7.4 %collective-permute-start.2 = (f32[2,1,16,1024]{3,2,1,0:T(8,128)}, f32[2,1,16,1024]{3,2,1,0:T(8,128)S(1)}, u32[]{:S(2)}, u32[]{:S(2)}) collective-permute-start(f32[2,1,16,1024]{3,2,1,0:T(8,128)} %refs_2_.1), channel_id=1, source_target_pairs={{0,4},{2,6},{4,0},{6,2},{8,12},{10,14},{12,8},{14,10},{1,5},{3,7},... | collective-permute-start | bytes 393224 | tf_op jit(solution)/shard_map/ppermute | solution.py:383
  6.4 5.8 %collective-permute-start.3 = (f32[2,1,16,1024]{3,2,1,0:T(8,128)}, f32[2,1,16,1024]{3,2,1,0:T(8,128)S(1)}, u32[]{:S(2)}, u32[]{:S(2)}) collective-permute-start(f32[2,1,16,1024]{3,2,1,0:T(8,128)} %refs_2_.1), channel_id=1, source_target_pairs={{0,2},{2,0},{4,6},{6,4},{8,10},{10,8},{12,14},{14,12},{1,3},{3,1},... | collective-permute-start | bytes 393224 | tf_op jit(solution)/shard_map/ppermute | solution.py:391
  7.9 8.1 %collective-permute-start = (f32[2,1,16,1024]{3,2,1,0:T(8,128)}, f32[2,1,16,1024]{3,2,1,0:T(8,128)S(1)}, u32[]{:S(2)}, u32[]{:S(2)}) collective-permute-start(f32[2,1,16,1024]{3,2,1,0:T(8,128)} %refs_2_.1), channel_id=1, source_target_pairs={{0,12},{2,14},{4,8},{6,10},{8,4},{10,6},{12,0},{14,2},{1,13},{3,15... | collective-permute-start | bytes 393224 | tf_op jit(solution)/shard_map/ppermute | solution.py:383
  8.1 1.0 %copy-start = (f32[8,32,512]{2,1,0:T(8,128)S(1)}, f32[8,32,512]{2,1,0:T(8,128)}, u32[]{:S(2)}) copy-start(f32[8,32,512]{2,1,0:T(8,128)} %mine_ref.1) | copy-start | bytes 1572868
  9.2 0.7 %copy-start.2 = (s32[8,8]{1,0:T(8,128)S(1)}, s32[8,8]{1,0:T(8,128)}, u32[]{:S(2)}) copy-start(s32[8,8]{1,0:T(8,128)} %q_ref.1) | copy-start | bytes 772
  9.9 0.7 %copy-start.3 = (s32[8]{0:T(128)S(1)}, s32[8]{0:T(128)}, u32[]{:S(2)}) copy-start(s32[8]{0:T(128)} %owner_ref.1) | copy-start | bytes 100
  10.5 2.3 %copy-start.1 = (f32[2,1,16,1024]{3,2,1,0:T(8,128)S(1)}, f32[2,1,16,1024]{3,2,1,0:T(8,128)}, u32[]{:S(2)}) copy-start(f32[2,1,16,1024]{3,2,1,0:T(8,128)} %refs_2_.1) | copy-start | bytes 393220
  10.5 5.5 %copy-start.4 = (bf16[2,256,256]{2,1,0:T(8,128)(2,1)S(1)}, bf16[2,256,256]{2,1,0:T(8,128)(2,1)}, u32[]{:S(2)}) copy-start(bf16[2,256,256]{2,1,0:T(8,128)(2,1)} %constant.29.clone.refs_11_.refs_7_) | copy-start | bytes 786436
  10.5 5.6 %copy-start.5 = (bf16[2,256,256]{2,1,0:T(8,128)(2,1)S(1)}, bf16[2,256,256]{2,1,0:T(8,128)(2,1)}, u32[]{:S(2)}) copy-start(bf16[2,256,256]{2,1,0:T(8,128)(2,1)} %constant.30.clone.refs_12_.refs_8_) | copy-start | bytes 786436
  10.5 5.6 %copy-start.6 = (f32[8,2,8,128]{3,2,1,0:T(8,128)S(1)}, f32[8,2,8,128]{3,2,1,0:T(8,128)}, u32[]{:S(2)}) copy-start(f32[8,2,8,128]{3,2,1,0:T(8,128)} %constant.31.clone.refs_13_.refs_9_) | copy-start | bytes 196612
  10.5 5.6 %copy-start.7 = (f32[2,16,128]{2,1,0:T(8,128)S(1)}, f32[2,16,128]{2,1,0:T(8,128)}, u32[]{:S(2)}) copy-start(f32[2,16,128]{2,1,0:T(8,128)} %constant.32.clone.refs_14_.refs_10_) | copy-start | bytes 49156
  12.2 3.7 %collective-permute-start.7 = (f32[2,1,16,1024]{3,2,1,0:T(8,128)S(1)}, f32[2,1,16,1024]{3,2,1,0:T(8,128)S(1)}, u32[]{:S(2)}, u32[]{:S(2)}) collective-permute-start(f32[2,1,16,1024]{3,2,1,0:T(8,128)S(1)} %collective-permute-done.3.refs_8_.refs_4_), channel_id=1, source_target_pairs={{0,1},{1,0},{2,3},{3,2},{4,5},{5,4},{6,7},{7,6},{8,9},{9,8},{10,11... | collective-permute-start | bytes 393224 | tf_op jit(solution)/shard_map/ppermute | solution.py:380
  12.2 3.7 %collective-permute-start.5 = (f32[2,1,16,1024]{3,2,1,0:T(8,128)S(1)}, f32[2,1,16,1024]{3,2,1,0:T(8,128)S(1)}, u32[]{:S(2)}, u32[]{:S(2)}) collective-permute-start(f32[2,1,16,1024]{3,2,1,0:T(8,128)S(1)} %collective-permute-done.1.refs_4_), channel_id=1, source_target_pairs={{0,1},{1,0},{2,3},{3,2},{4,5},{5,4},{6,7},{7,6},{8,9},{9,8},{10,11... | collective-permute-start | bytes 393224 | tf_op jit(solution)/shard_map/ppermute | solution.py:380
  12.7 3.2 %collective-permute-start.6 = (f32[2,1,16,1024]{3,2,1,0:T(8,128)S(1)}, f32[2,1,16,1024]{3,2,1,0:T(8,128)S(1)}, u32[]{:S(2)}, u32[]{:S(2)}) collective-permute-start(f32[2,1,16,1024]{3,2,1,0:T(8,128)S(1)} %collective-permute-done.2.refs_2_), channel_id=1, source_target_pairs={{0,1},{1,0},{2,3},{3,2},{4,5},{5,4},{6,7},{7,6},{8,9},{9,8},{10,11... | collective-permute-start | bytes 393224 | tf_op jit(solution)/shard_map/ppermute | solution.py:380
  12.8 3.2 %collective-permute-start.8 = (f32[2,1,16,1024]{3,2,1,0:T(8,128)S(1)}, f32[2,1,16,1024]{3,2,1,0:T(8,128)S(1)}, u32[]{:S(2)}, u32[]{:S(2)}) collective-permute-start(f32[2,1,16,1024]{3,2,1,0:T(8,128)S(1)} %copy-done.1), channel_id=1, source_target_pairs={{0,1},{1,0},{2,3},{3,2},{4,5},{5,4},{6,7},{7,6},{8,9},{9,8},{10,11... | collective-permute-start | bytes 393224 | tf_op jit(solution)/shard_map/ppermute | solution.py:380
  16.0 1.9 %collective-permute-start.9 = (f32[2,1,16,1024]{3,2,1,0:T(8,128)S(1)}, f32[2,1,16,1024]{3,2,1,0:T(8,128)S(1)}, u32[]{:S(2)}, u32[]{:S(2)}) collective-permute-start(f32[2,1,16,1024]{3,2,1,0:T(8,128)S(1)} %collective-permute-done.refs_0_), channel_id=1, source_target_pairs={{0,1},{1,0},{2,3},{3,2},{4,5},{5,4},{6,7},{7,6},{8,9},{9,8},{10,11... | collective-permute-start | bytes 393224 | tf_op jit(solution)/shard_map/ppermute | solution.py:380
  18.8 1.5 %collective-permute-start.10 = (f32[264,128]{1,0:T(8,128)S(1)}, f32[264,128]{1,0:T(8,128)S(1)}, u32[]{:S(2)}, u32[]{:S(2)}) collective-permute-start(f32[264,128]{1,0:T(8,128)S(1)} %get-tuple-element.31), channel_id=1, source_target_pairs={{0,1},{1,0},{2,3},{3,2},{4,5},{5,4},{6,7},{7,6},{8,9},{9,8},{10,11... | collective-permute-start | bytes 405512 | tf_op jit(solution)/shard_map/ppermute | solution.py:380
  20.4 5.9 %collective-permute-start.11 = (f32[264,128]{1,0:T(8,128)S(1)}, f32[264,128]{1,0:T(8,128)S(1)}, u32[]{:S(2)}, u32[]{:S(2)}) collective-permute-start(f32[264,128]{1,0:T(8,128)S(1)} %broadcast_select_fusion), channel_id=1, source_target_pairs={{0,2},{2,0},{4,6},{6,4},{8,10},{10,8},{12,14},{14,12},{1,3},{3,1},... | collective-permute-start | bytes 405512 | tf_op jit(solution)/shard_map/ppermute | solution.py:419

commit v5 on v4

--- a/solution.py
+++ b/solution.py
@@ -96,17 +96,19 @@
     return pl.ds(tile * LANES, LANES)
 
 
-def weight_kernel(side, blocks_per_k, order, q_ref, owner_ref, mine_ref, other_ref, weight_ref):
+def weight_kernel(side, blocks_per_k, order, late, q_ref, owner_ref, mine_ref, other_ref, weight_ref):
     tiles = side * side // LANES
     lows = LANES // side
     scale = -1.0 / (NK * side**3)
     place, core = lax.axis_index("kb"), lax.axis_index("slab")
     line, column = place // 2, place % 2
     first_core = core == 0
-    target_k = owner_ref[2 * line + core] // blocks_per_k
     lane = lax.broadcasted_iota(jnp.int32, (side, LANES), 1) // side
-    for pair, d in enumerate(order):
-        q = q_ref[target_k, owner_ref[2 * (line ^ d) + column] // blocks_per_k]
+    pairs = [(2 * line + core, 2 * (line ^ d) + column) for d in order]
+    if late is not None:
+        pairs.append((place, 2 * (line ^ late) + (column ^ core)))
+    for pair, (target_at, partner_at) in enumerate(pairs):
+        q = q_ref[owner_ref[target_at] // blocks_per_k, owner_ref[partner_at] // blocks_per_k]
         mine, other = mine_ref[q], other_ref[q]
         low_half = jnp.where(first_core, mine, other) * scale
         high_half = jnp.where(first_core, other, mine) * scale
@@ -126,15 +128,16 @@
             weight_ref[pair, at, :] = total
 
 
-def pair_kernel(side, count, first, has_sum, *refs):
+def pair_kernel(side, count, first, late, has_sum, *refs):
     refs = list(refs)
     take = lambda n: [refs.pop(0) for _ in range(n)]
-    partners = [take(2) for _ in range(count)]
-    own, beside = take(2), take(2)
+    partners = [take(1 if late else 2) for _ in range(count)]
+    own = take(2)
+    beside = None if late else take(2)
     (weight_ref,) = take(1)
     lane_f, lane_b, twist, turn = take(4)
     sums = take(2) if has_sum else None
-    outs = take(2)
+    outs = take(3 if late else 2)
     target, x_re, x_im, high_ref, low_ref, g_ref = take(6)
 
     tiles = side * side // LANES
@@ -145,9 +148,14 @@
     def parts(ref):
         return ref[0], ref[1]
 
-    home = lax.axis_index("kb") % 2 == lax.axis_index("slab")
-    for h in range(2):
-        target[h] = jnp.where(home, own[h][:, 0], beside[h][:, 0])
+    if late:
+        for h in range(2):
+            target[h] = own[h][:, 0]
+        partners = [[whole.at[0:2], whole.at[2:4]] for (whole,) in partners]
+    else:
+        home = lax.axis_index("kb") % 2 == lax.axis_index("slab")
+        for h in range(2):
+            target[h] = jnp.where(home, own[h][:, 0], beside[h][:, 0])
 
     groups = tiles // GROUP
 
@@ -253,7 +261,10 @@
                 gram_re += t_re * re + t_im * im
                 gram_im += t_re * im - t_im * re
                 outs[h][pl.ds(t * half + x, SUBLANES), :] = re
-                outs[h][pl.ds((tiles + t) * half + x, SUBLANES), :] = im
+                if late and h:
+                    outs[2][pl.ds(t * half + x, SUBLANES), :] = im
+                else:
+                    outs[h][pl.ds((tiles + t) * half + x, SUBLANES), :] = im
     end = 2 * tiles * half
     scale = 1.0 / side**3
     sums_row = jnp.concatenate(
@@ -263,22 +274,35 @@
         ],
         0,
     )
-    for h in range(2):
-        outs[h][pl.ds(end, 8), :] = sums_row
-
-
-def join_kernel(own_ref, near_ref, away_ref, applied_ref, gram_ref):
+    outs[0][pl.ds(end, 8), :] = sums_row
+    outs[1][pl.ds(end // 2 if late else end, 8), :] = sums_row
+
+
+def join_kernel(*refs):
+    *parts, applied_ref, gram_ref = refs
+    own, near, away_mine, away_near, *late = parts
     half = applied_ref.shape[2]
     tiles = applied_ref.shape[3] // LANES
     home = lax.axis_index("kb") % 2 == lax.axis_index("slab")
+
+    def total(k, at, size):
+        at_all = pl.ds(at if k == 0 else tiles * half + at, size)
+        found = jnp.where(home, own[at_all, :], near[at_all, :]) + jnp.where(
+            home, away_mine[at_all, :], away_near[at_all, :]
+        )
+        if late:
+            found += late[0][at_all, :] + late[1 + k][pl.ds(at, size), :]
+        return found
+
     for k in range(2):
         for t in range(tiles):
-            at = pl.ds((k * tiles + t) * half, half)
-            applied_ref[k, 0, :, lane_slice(t)] = (
-                jnp.where(home, own_ref[at, :], near_ref[at, :]) + away_ref[at, :]
-            )
-    at = pl.ds(2 * tiles * half, 8)
-    sums = jnp.where(home, own_ref[at, :], near_ref[at, :]) + away_ref[at, :]
+            applied_ref[k, 0, :, lane_slice(t)] = total(k, t * half, half)
+    end = pl.ds(2 * tiles * half, 8)
+    sums = jnp.where(home, own[end, :], near[end, :]) + jnp.where(
+        home, away_mine[end, :], away_near[end, :]
+    )
+    if late:
+        sums += late[0][end, :] + late[1][pl.ds(tiles * half, 8), :]
     gram_ref[0, 0, 0] = jnp.max(sums[0:1, :])
     gram_ref[0, 0, 1] = jnp.max(sums[4:5, :])
 
@@ -287,17 +311,18 @@
 SMEM = pl.BlockSpec(memory_space=pltpu.SMEM)
 
 
-COST = pl.CostEstimate(flops=2*10**10, bytes_accessed=10**8, transcendentals=0)
+COST = pl.CostEstimate(flops=1, bytes_accessed=1, transcendentals=0)
 
 
 def params():
     return pltpu.CompilerParams(vmem_limit_bytes=48 * 2**20)
 
 
-def choose_weights(q_index, owner, kernels, order, side, blocks_per_k):
+def choose_weights(q_index, owner, kernels, order, late, side, blocks_per_k):
+    count = len(order) + (late is not None)
     return pl.pallas_call(
-        functools.partial(weight_kernel, side, blocks_per_k, order),
-        out_shape=jax.ShapeDtypeStruct((len(order), side**3 // LANES, LANES), F32),
+        functools.partial(weight_kernel, side, blocks_per_k, order, late),
+        out_shape=jax.ShapeDtypeStruct((count, side**3 // LANES, LANES), F32),
         in_specs=[SMEM, SMEM, VMEM, VMEM],
         out_specs=VMEM,
         compiler_params=params(),
@@ -306,7 +331,7 @@
     )(q_index, owner, *kernels)
 
 
-def apply_pairs(own, beside, partners, weights, first, side, sums=None):
+def apply_pairs(own, beside, partners, weights, first, side, sums=None, late=False):
     count = len(partners)
     half = side // 2
     tiles = side * side // LANES
@@ -318,14 +343,17 @@
         jnp.asarray(twist_table(side, SUBLANES)),
         jnp.asarray(turn_table(side)),
     ]
-    operands = [x for pair in partners for x in pair] + [*own, *beside, weights] + tables
+    operands = [x for pair in partners for x in pair] + [*own, *beside, weights, *tables]
     operands += list(sums) if sums is not None else []
-    message = jax.ShapeDtypeStruct((2 * tiles * half + 8, LANES), F32)
+    shapes = [2 * tiles * half + 8] * 2
+    if late:
+        shapes[1:] = [tiles * half + 8, tiles * half]
+    messages = tuple(jax.ShapeDtypeStruct((n, LANES), F32) for n in shapes)
     return pl.pallas_call(
-        functools.partial(pair_kernel, side, count, first, sums is not None),
-        out_shape=(message, message),
+        functools.partial(pair_kernel, side, count, first, late, sums is not None),
+        out_shape=messages,
         in_specs=[VMEM] * len(operands),
-        out_specs=(VMEM, VMEM),
+        out_specs=(VMEM,) * len(messages),
         scratch_shapes=[
             pltpu.VMEM((2, 2, half, side * side), F32),
             pltpu.VMEM((rows // SUBLANES * STEP, LANES), F32),
@@ -340,16 +368,16 @@
     )(*operands)
 
 
-def join(own, near, away, shape):
+def join(parts, shape):
     applied, gram = pl.pallas_call(
         join_kernel,
         out_shape=(jax.ShapeDtypeStruct(shape, F32), jax.ShapeDtypeStruct((1, 1, 2), F32)),
-        in_specs=[VMEM, VMEM, VMEM],
+        in_specs=[VMEM] * len(parts),
         out_specs=(VMEM, SMEM),
         compiler_params=params(),
         cost_estimate=COST,
         name="join",
-    )(own, near, away)
+    )(*parts)
     return applied, gram.transpose(2, 0, 1)
 
 
@@ -384,40 +412,45 @@
             x, "kb", [(2 * a + c, 2 * (a ^ d) + c) for a in range(lines) for c in range(2)]
         )
 
-    order = [0, 1, *range(2, lines)]
-    first = [2, 1, 0]
-    last = [d for d in order if d and d not in first]
+    late = 3 if lines == 4 else None
+    order = [d for d in range(lines) if d != late]
+    first = [*order[2:], 1, 0]
+    own = (orbitals, swap(orbitals))
     arrived = {d: from_line(orbitals, d) for d in order[1:]}
     arrived[0] = lax.ppermute(orbitals, "kb", across)
-    far_kernel = swap(kernel)
     weights = choose_weights(
-        q_index, owner, (kernel, far_kernel), tuple(order), side, blocks_per_k
+        q_index, owner, (kernel, swap(kernel)), tuple(order), late, side, blocks_per_k
     )
-    own_far = swap(lax.optimization_barrier((orbitals, far_kernel))[0])
     landed = lax.optimization_barrier((*(arrived[d] for d in first), weights))
     arrived.update(zip(first, landed))
     weights = landed[-1]
     far = {d: swap(arrived[d]) for d in first}
-    landed = lax.optimization_barrier(
-        (*(arrived[d] for d in last), *(far[d] for d in first), own_far)
-    )
-    arrived.update(zip(last, landed))
-    far.update(zip(first, landed[len(last) :]))
-    own = (orbitals, landed[-1])
-    far.update({d: swap(arrived[d]) for d in last})
     beside = (arrived[0], far[0])
     partners = [own] + [(arrived[d], far[d]) for d in order[1:]]
-    if lines <= 4:
-        groups = [(0, lines - 1), (lines - 1, lines)]
-    else:
-        groups = [(at, min(at + 4, lines)) for at in range(0, lines, 4)]
     sums = None
-    for at, end in groups:
-        sums = apply_pairs(own, beside, partners[at:end], weights, at, side, sums)
-    mine, far = sums
-    near = swap(far)
-    away = lax.ppermute(jnp.where(core == column, near, mine), "kb", across)
-    applied, gram = join(mine, near, away, orbitals.shape)
+    for at in range(0, len(order), 4):
+        sums = apply_pairs(own, beside, partners[at : at + 4], weights, at, side, sums)
+    if late is not None:
+        steps = (2 * late, 2 * late + 1)
+        moves = [(2 * a + c, 2 * (a ^ steps[c]) + c) for a in range(n_kb) for c in range(2)]
+        last = lax.ppermute(jnp.concatenate(own), ("kb", "slab"), moves)
+        last, _ = lax.optimization_barrier((last, sums))
+    mine, other_rows = sums
+    crossed = [
+        (2 * a + core, 2 * (a ^ 1) + 1 - core) for a in range(n_kb) for core in range(2)
+    ]
+    parts = [
+        mine,
+        swap(other_rows),
+        lax.ppermute(mine, "kb", across),
+        lax.ppermute(other_rows, ("kb", "slab"), crossed),
+    ]
+    if late is not None:
+        late_mine, *late_rows = apply_pairs(
+            own, (), [(last,)], weights, len(order), side, late=True
+        )
+        parts += [late_mine, *(swap(x) for x in late_rows)]
+    applied, gram = join(parts, orbitals.shape)
     if blocks_per_k > 1:
         gram = block_gram(orbitals, applied, owner, blocks_per_k, side**3)
     return applied, gram

time: 27.4 us -> 26.4 us (0.964)
  the two profiles are of different devices: /device:TPU:0 before, /device:TPU:9 now
where the time goes in v5:
time: 26.4 us; the launch traced here: 26.2 us
  starting transfers between devices  10.1 us (38%)
  waiting for transfers between devices  8.59 us (33%)
  Pallas kernels  4.5 us (17%)
  local copies, waits for them, and re-layouts  1.38 us (5%)
  other arithmetic  0.95 us (4%)
  between operations  0.74 us (3%)
    ppermute x8, starting transfers between devices, swap(): return lax.ppermute(x, 'slab', [(0, 1), (1, 0)])  4.19 us
    ppermute x1, waiting for transfers between devices, on_device(): last = lax.ppermute(jnp.concatenate(own), ('kb', 'slab'), moves)  3.58 us
    pallas_call x2, Pallas kernels, apply_pairs(): pl.pallas_call(functools.partial(pair_kernel, side, count, first, late, s...  2.68 us
    ppermute x2, starting transfers between devices, from_line(): lax.ppermute(x, 'kb', [(2 * a + c, 2 * (a ^ d) + c) for a in range(lines)...  2.48 us
    ppermute x8, waiting for transfers between devices, swap(): return lax.ppermute(x, 'slab', [(0, 1), (1, 0)])  2.21 us
    ppermute x1, waiting for transfers between devices, on_device(): lax.ppermute(mine, 'kb', across)  1.61 us
    ppermute x1, starting transfers between devices, on_device(): lax.ppermute(other_rows, ('kb', 'slab'), crossed)  1.51 us
    unnamed x16, local copies, waits for them, and re-layouts  1.38 us
  transfers between devices with their start and end apart: 14, of which 7 were waited for; matrix products, arithmetic and copies ran while one was open for 4% of the time, Pallas kernels for 14%

profile of v5, /device:TPU:9, one launch (start us, length us, event | category | flops | bytes accessed | tf_op | source)
XLA Modules:
  0.0 26.2 jit_solution(6915686763168032732)
XLA Ops:
  0.6 0.0 copy-start.3
  0.6 0.7 %collective-permute-start.4 = (f32[8,32,512]{2,1,0:T(8,128)}, f32[8,32,512]{2,1,0:T(8,128)S(1)}, u32[]{:S(2)}, u32[]{:S(2)}) collective-permute-start(f32[8,32,512]{2,1,0:T(8,128)} %mine_ref.1), channel_id=1, source_target_pairs={{0,1},{1,0},{2,3},{3,2},{4,5},{5,4},{6,7},{7,6},{8,9},{9,8},{10,11... | collective-permute-start | bytes 1572872 | tf_op jit(solution)/shard_map/ppermute | solution.py:408
  1.4 0.1 collective-permute-start
  1.5 2.3 %collective-permute-start.1 = (f32[2,1,16,1024]{3,2,1,0:T(8,128)}, f32[2,1,16,1024]{3,2,1,0:T(8,128)S(1)}, u32[]{:S(2)}, u32[]{:S(2)}) collective-permute-start(f32[2,1,16,1024]{3,2,1,0:T(8,128)} %refs_1_.1), channel_id=1, source_target_pairs={{0,8},{2,10},{4,12},{6,14},{8,0},{10,2},{12,4},{14,6},{1,9},{3,11}... | collective-permute-start | bytes 393224 | tf_op jit(solution)/shard_map/ppermute | solution.py:411
  3.8 0.2 collective-permute-start.2
  3.9 1.2 %collective-permute-start.3 = (f32[2,1,16,1024]{3,2,1,0:T(8,128)}, f32[2,1,16,1024]{3,2,1,0:T(8,128)S(1)}, u32[]{:S(2)}, u32[]{:S(2)}) collective-permute-start(f32[2,1,16,1024]{3,2,1,0:T(8,128)} %refs_1_.1), channel_id=1, source_target_pairs={{0,2},{2,0},{4,6},{6,4},{8,10},{10,8},{12,14},{14,12},{1,3},{3,1},... | collective-permute-start | bytes 393224 | tf_op jit(solution)/shard_map/ppermute | solution.py:420
  5.2 0.0 collective-permute-done.refs_1_.refs_7_.refs_2_
  5.2 1.0 %pad_maximum_fusion = f32[4,1,16,1024]{3,2,1,0:T(8,128)S(1)} fusion(f32[2,1,16,1024]{3,2,1,0:T(8,128)S(1)} %collective-permute-done.refs_1_.refs_7_.refs_2_, f32[2,1,16,1024]{3,2,1,0:T(8,128)} %refs_1_.1), kind=kLoop, calls=%fused_computation | loop fusion | flops 65536 | bytes 524288 | tf_op jit(solution)/shard_map/concatenate | solution.py:436
  6.1 0.0 copy-start
  6.1 0.0 copy-start.1
  6.2 0.0 copy-start.2
  6.2 0.0 copy-start.4
  6.2 0.0 copy-start.5
  6.2 0.4 %collective-permute-start.11 = (f32[4,1,16,1024]{3,2,1,0:T(8,128)S(1)}, f32[4,1,16,1024]{3,2,1,0:T(8,128)S(1)}, u32[]{:S(2)}, u32[]{:S(2)}) collective-permute-start(f32[4,1,16,1024]{3,2,1,0:T(8,128)S(1)} %pad_maximum_fusion), channel_id=1, source_target_pairs={{0,12},{1,15},{2,14},{3,13},{4,8},{5,11},{6,10},{7,9},{8,4},{9,7},... | collective-permute-start | bytes 786440 | tf_op jit(solution)/shard_map/ppermute | solution.py:436
  6.6 0.0 collective-permute-done.4.other_ref
  6.6 0.0 copy-done.3
  6.6 0.7 %copy-done.6 = s32[8,8]{1,0:T(8,128)S(1)} copy-done((s32[8,8]{1,0:T(8,128)S(1)}, s32[8,8]{1,0:T(8,128)}, u32[]{:S(2)}) %copy-start.6) | copy-done | bytes 280
  7.3 0.0 copy-start.7
  7.3 0.7 %copy-done.7 = s32[8]{0:T(128)S(1)} copy-done((s32[8]{0:T(128)S(1)}, s32[8]{0:T(128)}, u32[]{:S(2)}) %copy-start.7) | copy-done | bytes 56
  8.0 1.1 %weights.1.refs_10_.refs_3_ = f32[4,256,128]{2,1,0:T(8,128)S(1)} custom-call(s32[8,8]{1,0:T(8,128)S(1)} %copy-done.6, s32[8]{0:T(128)S(1)} %copy-done.7, f32[8,32,512]{2,1,0:T(8,128)S(1)} %copy-done.3, f32[8,32,512]{2,1,0:T(8,128)S(1)} %collective-permute-done.4.other_ref), custom_call_target="tpu_custom_call" | custom-call | flops 1 | bytes 1 | tf_op jit(solution)/shard_map/weights/pallas_call | solution.py:323
  9.1 1.2 %collective-permute-done.1.refs_4_ = f32[2,1,16,1024]{3,2,1,0:T(8,128)S(1)} collective-permute-done((f32[2,1,16,1024]{3,2,1,0:T(8,128)}, f32[2,1,16,1024]{3,2,1,0:T(8,128)S(1)}, u32[]{:S(2)}, u32[]{:S(2)}) %collective-permute-start.1) | collective-permute-done | bytes 131104 | tf_op jit(solution)/shard_map/ppermute | solution.py:411
  10.3 0.0 collective-permute-done.2.refs_2_
  10.3 0.0 collective-permute-done.3.refs_8_
  10.3 2.0 %collective-permute-start.5 = (f32[2,1,16,1024]{3,2,1,0:T(8,128)S(1)}, f32[2,1,16,1024]{3,2,1,0:T(8,128)S(1)}, u32[]{:S(2)}, u32[]{:S(2)}) collective-permute-start(f32[2,1,16,1024]{3,2,1,0:T(8,128)S(1)} %collective-permute-done.2.refs_2_), channel_id=1, source_target_pairs={{0,1},{1,0},{2,3},{3,2},{4,5},{5,4},{6,7},{7,6},{8,9},{9,8},{10,11... | collective-permute-start | bytes 393224 | tf_op jit(solution)/shard_map/ppermute | solution.py:408
  12.3 0.0 collective-permute-start.6
  12.3 0.5 %collective-permute-start.7 = (f32[2,1,16,1024]{3,2,1,0:T(8,128)S(1)}, f32[2,1,16,1024]{3,2,1,0:T(8,128)S(1)}, u32[]{:S(2)}, u32[]{:S(2)}) collective-permute-start(f32[2,1,16,1024]{3,2,1,0:T(8,128)S(1)} %collective-permute-done.3.refs_8_), channel_id=1, source_target_pairs={{0,1},{1,0},{2,3},{3,2},{4,5},{5,4},{6,7},{7,6},{8,9},{9,8},{10,11... | collective-permute-start | bytes 393224 | tf_op jit(solution)/shard_map/ppermute | solution.py:408
  12.8 0.5 %collective-permute-done.5.refs_3_ = f32[2,1,16,1024]{3,2,1,0:T(8,128)S(1)} collective-permute-done((f32[2,1,16,1024]{3,2,1,0:T(8,128)S(1)}, f32[2,1,16,1024]{3,2,1,0:T(8,128)S(1)}, u32[]{:S(2)}, u32[]{:S(2)}) %collective-permute-start.5) | collective-permute-done | bytes 131104 | tf_op jit(solution)/shard_map/ppermute | solution.py:408
  13.3 0.4 %collective-permute-done.6.refs_5_ = f32[2,1,16,1024]{3,2,1,0:T(8,128)S(1)} collective-permute-done((f32[2,1,16,1024]{3,2,1,0:T(8,128)S(1)}, f32[2,1,16,1024]{3,2,1,0:T(8,128)S(1)}, u32[]{:S(2)}, u32[]{:S(2)}) %collective-permute-start.6) | collective-permute-done | bytes 131104 | tf_op jit(solution)/shard_map/ppermute | solution.py:408
  13.7 0.2 collective-permute-done.7.refs_9_
  13.9 0.0 copy-done
  13.9 0.0 copy-done.1
  13.9 0.0 copy-done.2
  13.9 0.0 copy-done.4
  13.9 0.0 copy-done.5
  13.9 1.7 %pairs.2 = (f32[264,128]{1,0:T(8,128)S(1)}, f32[264,128]{1,0:T(8,128)S(1)}) custom-call(f32[2,1,16,1024]{3,2,1,0:T(8,128)S(1)} %copy-done, f32[2,1,16,1024]{3,2,1,0:T(8,128)S(1)} %collective-permute-done.refs_1_.refs_7_.refs_2_, f32[2,1,16,1024]{3,2,1,0:T(8,128)S(1)} %collective-permute-done.2.refs_2_, ...), custom_call_target="tpu_custom_call" | custom-call | flops 1 | bytes 1 | tf_op jit(solution)/shard_map/pairs/pallas_call | solution.py:352
  15.6 1.5 %collective-permute-start.10 = (f32[264,128]{1,0:T(8,128)S(1)}, f32[264,128]{1,0:T(8,128)S(1)}, u32[]{:S(2)}, u32[]{:S(2)}) collective-permute-start(f32[264,128]{1,0:T(8,128)S(1)} %get-tuple-element.19), channel_id=1, source_target_pairs={{0,3},{1,2},{2,1},{3,0},{4,7},{5,6},{6,5},{7,4},{8,11},{9,10},{10,... | collective-permute-start | bytes 405512 | tf_op jit(solution)/shard_map/ppermute | solution.py:446
  17.1 0.2 collective-permute-start.8
  17.3 0.2 collective-permute-start.9
  17.6 3.6 %collective-permute-done.11.refs_0_ = f32[4,1,16,1024]{3,2,1,0:T(8,128)S(1)} collective-permute-done((f32[4,1,16,1024]{3,2,1,0:T(8,128)S(1)}, f32[4,1,16,1024]{3,2,1,0:T(8,128)S(1)}, u32[]{:S(2)}, u32[]{:S(2)}) %collective-permute-start.11) | collective-permute-done | bytes 262176 | tf_op jit(solution)/shard_map/ppermute | solution.py:436
  21.1 0.9 %pairs.3 = (f32[264,128]{1,0:T(8,128)S(1)}, f32[136,128]{1,0:T(8,128)S(1)}, f32[128,128]{1,0:T(8,128)S(1)}) custom-call(f32[4,1,16,1024]{3,2,1,0:T(8,128)S(1)} %collective-permute-done.11.refs_0_, f32[2,1,16,1024]{3,2,1,0:T(8,128)S(1)} %copy-done, f32[2,1,16,1024]{3,2,1,0:T(8,128)S(1)} %collective-permute-done.refs_1_.refs_7_.refs_2_, ...), custom_call_target="tpu_custom_call" | custom-call | flops 1 | bytes 1 | tf_op jit(solution)/shard_map/pairs/pallas_call | solution.py:352
  22.1 0.5 %collective-permute-start.12 = (f32[136,128]{1,0:T(8,128)S(1)}, f32[136,128]{1,0:T(8,128)S(1)}, u32[]{:S(2)}, u32[]{:S(2)}) collective-permute-start(f32[136,128]{1,0:T(8,128)S(1)} %get-tuple-element.22), channel_id=1, source_target_pairs={{0,1},{1,0},{2,3},{3,2},{4,5},{5,4},{6,7},{7,6},{8,9},{9,8},{10,11... | collective-permute-start | bytes 208904 | tf_op jit(solution)/shard_map/ppermute | solution.py:408
  22.6 0.1 collective-permute-start.13
  22.7 1.2 %collective-permute-done.13.refs_6_ = f32[128,128]{1,0:T(8,128)S(1)} collective-permute-done((f32[128,128]{1,0:T(8,128)S(1)}, f32[128,128]{1,0:T(8,128)S(1)}, u32[]{:S(2)}, u32[]{:S(2)}) %collective-permute-start.13) | collective-permute-done | bytes 65568 | tf_op jit(solution)/shard_map/ppermute | solution.py:408
  23.9 0.0 collective-permute-done.12.refs_5_
  23.9 0.0 collective-permute-done.10.refs_3_
  23.9 0.0 collective-permute-done.8.refs_1_
  23.9 1.6 %collective-permute-done.9.refs_2_ = f32[264,128]{1,0:T(8,128)S(1)} collective-permute-done((f32[264,128]{1,0:T(8,128)S(1)}, f32[264,128]{1,0:T(8,128)S(1)}, u32[]{:S(2)}, u32[]{:S(2)}) %collective-permute-start.9) | collective-permute-done | bytes 135200 | tf_op jit(solution)/shard_map/ppermute | solution.py:445
  25.5 0.7 %join.1 = (f32[2,1,16,1024]{3,2,1,0:T(8,128)}, f32[1,1,2]{2,1,0:T(1,128)}) custom-call(f32[264,128]{1,0:T(8,128)S(1)} %get-tuple-element.18.refs_0_, f32[264,128]{1,0:T(8,128)S(1)} %collective-permute-done.8.refs_1_, f32[264,128]{1,0:T(8,128)S(1)} %collective-permute-done.9.refs_2_, f32[264,128]{1,0:T(8,128)S(1)} %collective-permute-done.10.refs_3_, ...), custom_call_target="tpu_custom_call" | custom-call | flops 1 | bytes 1 | tf_op jit(solution)/shard_map/join/pallas_call | solution.py:372
  (1 shorter events, 0.0 us)
Async XLA Ops:
  0.6 6.0 %copy-start.3 = (f32[8,32,512]{2,1,0:T(8,128)S(1)}, f32[8,32,512]{2,1,0:T(8,128)}, u32[]{:S(2)}) copy-start(f32[8,32,512]{2,1,0:T(8,128)} %mine_ref.1) | copy-start | bytes 1572868
  0.6 6.0 %collective-permute-start.4 = (f32[8,32,512]{2,1,0:T(8,128)}, f32[8,32,512]{2,1,0:T(8,128)S(1)}, u32[]{:S(2)}, u32[]{:S(2)}) collective-permute-start(f32[8,32,512]{2,1,0:T(8,128)} %mine_ref.1), channel_id=1, source_target_pairs={{0,1},{1,0},{2,3},{3,2},{4,5},{5,4},{6,7},{7,6},{8,9},{9,8},{10,11... | collective-permute-start | bytes 1572872 | tf_op jit(solution)/shard_map/ppermute | solution.py:408
  1.4 3.8 %collective-permute-start = (f32[2,1,16,1024]{3,2,1,0:T(8,128)}, f32[2,1,16,1024]{3,2,1,0:T(8,128)S(1)}, u32[]{:S(2)}, u32[]{:S(2)}) collective-permute-start(f32[2,1,16,1024]{3,2,1,0:T(8,128)} %refs_1_.1), channel_id=1, source_target_pairs={{0,1},{1,0},{2,3},{3,2},{4,5},{5,4},{6,7},{7,6},{8,9},{9,8},{10,11... | collective-permute-start | bytes 393224 | tf_op jit(solution)/shard_map/ppermute | solution.py:408
  1.5 8.8 %collective-permute-start.1 = (f32[2,1,16,1024]{3,2,1,0:T(8,128)}, f32[2,1,16,1024]{3,2,1,0:T(8,128)S(1)}, u32[]{:S(2)}, u32[]{:S(2)}) collective-permute-start(f32[2,1,16,1024]{3,2,1,0:T(8,128)} %refs_1_.1), channel_id=1, source_target_pairs={{0,8},{2,10},{4,12},{6,14},{8,0},{10,2},{12,4},{14,6},{1,9},{3,11}... | collective-permute-start | bytes 393224 | tf_op jit(solution)/shard_map/ppermute | solution.py:411
  3.8 6.5 %collective-permute-start.2 = (f32[2,1,16,1024]{3,2,1,0:T(8,128)}, f32[2,1,16,1024]{3,2,1,0:T(8,128)S(1)}, u32[]{:S(2)}, u32[]{:S(2)}) collective-permute-start(f32[2,1,16,1024]{3,2,1,0:T(8,128)} %refs_1_.1), channel_id=1, source_target_pairs={{0,4},{2,6},{4,0},{6,2},{8,12},{10,14},{12,8},{14,10},{1,5},{3,7},... | collective-permute-start | bytes 393224 | tf_op jit(solution)/shard_map/ppermute | solution.py:411
  3.9 6.3 %collective-permute-start.3 = (f32[2,1,16,1024]{3,2,1,0:T(8,128)}, f32[2,1,16,1024]{3,2,1,0:T(8,128)S(1)}, u32[]{:S(2)}, u32[]{:S(2)}) collective-permute-start(f32[2,1,16,1024]{3,2,1,0:T(8,128)} %refs_1_.1), channel_id=1, source_target_pairs={{0,2},{2,0},{4,6},{6,4},{8,10},{10,8},{12,14},{14,12},{1,3},{3,1},... | collective-permute-start | bytes 393224 | tf_op jit(solution)/shard_map/ppermute | solution.py:420
  6.1 7.7 %copy-start = (f32[2,1,16,1024]{3,2,1,0:T(8,128)S(1)}, f32[2,1,16,1024]{3,2,1,0:T(8,128)}, u32[]{:S(2)}) copy-start(f32[2,1,16,1024]{3,2,1,0:T(8,128)} %refs_1_.1) | copy-start | bytes 393220
  6.1 7.7 %copy-start.1 = (bf16[2,256,256]{2,1,0:T(8,128)(2,1)S(1)}, bf16[2,256,256]{2,1,0:T(8,128)(2,1)}, u32[]{:S(2)}) copy-start(bf16[2,256,256]{2,1,0:T(8,128)(2,1)} %constant.8.clone.refs_11_.refs_4_) | copy-start | bytes 786436
  6.2 7.7 %copy-start.2 = (bf16[2,256,256]{2,1,0:T(8,128)(2,1)S(1)}, bf16[2,256,256]{2,1,0:T(8,128)(2,1)}, u32[]{:S(2)}) copy-start(bf16[2,256,256]{2,1,0:T(8,128)(2,1)} %constant.9.clone.refs_12_.refs_5_) | copy-start | bytes 786436
  6.2 7.7 %copy-start.4 = (f32[8,2,8,128]{3,2,1,0:T(8,128)S(1)}, f32[8,2,8,128]{3,2,1,0:T(8,128)}, u32[]{:S(2)}) copy-start(f32[8,2,8,128]{3,2,1,0:T(8,128)} %constant.10.clone.refs_13_.refs_6_) | copy-start | bytes 196612
  6.2 7.7 %copy-start.5 = (f32[2,16,128]{2,1,0:T(8,128)S(1)}, f32[2,16,128]{2,1,0:T(8,128)}, u32[]{:S(2)}) copy-start(f32[2,16,128]{2,1,0:T(8,128)} %constant.11.clone.refs_14_.refs_7_) | copy-start | bytes 49156
  6.2 14.9 %collective-permute-start.11 = (f32[4,1,16,1024]{3,2,1,0:T(8,128)S(1)}, f32[4,1,16,1024]{3,2,1,0:T(8,128)S(1)}, u32[]{:S(2)}, u32[]{:S(2)}) collective-permute-start(f32[4,1,16,1024]{3,2,1,0:T(8,128)S(1)} %pad_maximum_fusion), channel_id=1, source_target_pairs={{0,12},{1,15},{2,14},{3,13},{4,8},{5,11},{6,10},{7,9},{8,4},{9,7},... | collective-permute-start | bytes 786440 | tf_op jit(solution)/shard_map/ppermute | solution.py:436
  6.6 0.7 %copy-start.6 = (s32[8,8]{1,0:T(8,128)S(1)}, s32[8,8]{1,0:T(8,128)}, u32[]{:S(2)}) copy-start(s32[8,8]{1,0:T(8,128)} %q_ref.1) | copy-start | bytes 772
  7.3 0.7 %copy-start.7 = (s32[8]{0:T(128)S(1)}, s32[8]{0:T(128)}, u32[]{:S(2)}) copy-start(s32[8]{0:T(128)} %owner_ref.1) | copy-start | bytes 100
  10.3 3.0 %collective-permute-start.5 = (f32[2,1,16,1024]{3,2,1,0:T(8,128)S(1)}, f32[2,1,16,1024]{3,2,1,0:T(8,128)S(1)}, u32[]{:S(2)}, u32[]{:S(2)}) collective-permute-start(f32[2,1,16,1024]{3,2,1,0:T(8,128)S(1)} %collective-permute-done.2.refs_2_), channel_id=1, source_target_pairs={{0,1},{1,0},{2,3},{3,2},{4,5},{5,4},{6,7},{7,6},{8,9},{9,8},{10,11... | collective-permute-start | bytes 393224 | tf_op jit(solution)/shard_map/ppermute | solution.py:408
  12.3 1.3 %collective-permute-start.6 = (f32[2,1,16,1024]{3,2,1,0:T(8,128)S(1)}, f32[2,1,16,1024]{3,2,1,0:T(8,128)S(1)}, u32[]{:S(2)}, u32[]{:S(2)}) collective-permute-start(f32[2,1,16,1024]{3,2,1,0:T(8,128)S(1)} %collective-permute-done.1.refs_4_), channel_id=1, source_target_pairs={{0,1},{1,0},{2,3},{3,2},{4,5},{5,4},{6,7},{7,6},{8,9},{9,8},{10,11... | collective-permute-start | bytes 393224 | tf_op jit(solution)/shard_map/ppermute | solution.py:408
  12.3 1.5 %collective-permute-start.7 = (f32[2,1,16,1024]{3,2,1,0:T(8,128)S(1)}, f32[2,1,16,1024]{3,2,1,0:T(8,128)S(1)}, u32[]{:S(2)}, u32[]{:S(2)}) collective-permute-start(f32[2,1,16,1024]{3,2,1,0:T(8,128)S(1)} %collective-permute-done.3.refs_8_), channel_id=1, source_target_pairs={{0,1},{1,0},{2,3},{3,2},{4,5},{5,4},{6,7},{7,6},{8,9},{9,8},{10,11... | collective-permute-start | bytes 393224 | tf_op jit(solution)/shard_map/ppermute | solution.py:408
  15.6 8.3 %collective-permute-start.10 = (f32[264,128]{1,0:T(8,128)S(1)}, f32[264,128]{1,0:T(8,128)S(1)}, u32[]{:S(2)}, u32[]{:S(2)}) collective-permute-start(f32[264,128]{1,0:T(8,128)S(1)} %get-tuple-element.19), channel_id=1, source_target_pairs={{0,3},{1,2},{2,1},{3,0},{4,7},{5,6},{6,5},{7,4},{8,11},{9,10},{10,... | collective-permute-start | bytes 405512 | tf_op jit(solution)/shard_map/ppermute | solution.py:446
  17.1 6.8 %collective-permute-start.8 = (f32[264,128]{1,0:T(8,128)S(1)}, f32[264,128]{1,0:T(8,128)S(1)}, u32[]{:S(2)}, u32[]{:S(2)}) collective-permute-start(f32[264,128]{1,0:T(8,128)S(1)} %get-tuple-element.19), channel_id=1, source_target_pairs={{0,1},{1,0},{2,3},{3,2},{4,5},{5,4},{6,7},{7,6},{8,9},{9,8},{10,11... | collective-permute-start | bytes 405512 | tf_op jit(solution)/shard_map/ppermute | solution.py:408
  17.3 8.2 %collective-permute-start.9 = (f32[264,128]{1,0:T(8,128)S(1)}, f32[264,128]{1,0:T(8,128)S(1)}, u32[]{:S(2)}, u32[]{:S(2)}) collective-permute-start(f32[264,128]{1,0:T(8,128)S(1)} %get-tuple-element.18.refs_0_), channel_id=1, source_target_pairs={{0,2},{2,0},{4,6},{6,4},{8,10},{10,8},{12,14},{14,12},{1,3},{3,1},... | collective-permute-start | bytes 405512 | tf_op jit(solution)/shard_map/ppermute | solution.py:445
  22.1 1.8 %collective-permute-start.12 = (f32[136,128]{1,0:T(8,128)S(1)}, f32[136,128]{1,0:T(8,128)S(1)}, u32[]{:S(2)}, u32[]{:S(2)}) collective-permute-start(f32[136,128]{1,0:T(8,128)S(1)} %get-tuple-element.22), channel_id=1, source_target_pairs={{0,1},{1,0},{2,3},{3,2},{4,5},{5,4},{6,7},{7,6},{8,9},{9,8},{10,11... | collective-permute-start | bytes 208904 | tf_op jit(solution)/shard_map/ppermute | solution.py:408
  22.6 1.3 %collective-permute-start.13 = (f32[128,128]{1,0:T(8,128)S(1)}, f32[128,128]{1,0:T(8,128)S(1)}, u32[]{:S(2)}, u32[]{:S(2)}) collective-permute-start(f32[128,128]{1,0:T(8,128)S(1)} %get-tuple-element.23), channel_id=1, source_target_pairs={{0,1},{1,0},{2,3},{3,2},{4,5},{5,4},{6,7},{7,6},{8,9},{9,8},{10,11... | collective-permute-start | bytes 196616 | tf_op jit(solution)/shard_map/ppermute | solution.py:408

commit v6 on v5

--- a/solution.py
+++ b/solution.py
@@ -104,7 +104,8 @@
     line, column = place // 2, place % 2
     first_core = core == 0
     lane = lax.broadcasted_iota(jnp.int32, (side, LANES), 1) // side
-    pairs = [(2 * line + core, 2 * (line ^ d) + column) for d in order]
+    targets = (place, place ^ 1)
+    pairs = [(target, 2 * (line ^ d) + column) for target in targets for d in order]
     if late is not None:
         pairs.append((place, 2 * (line ^ late) + (column ^ core)))
     for pair, (target_at, partner_at) in enumerate(pairs):
@@ -128,54 +129,49 @@
             weight_ref[pair, at, :] = total
 
 
-def pair_kernel(side, count, first, late, has_sum, *refs):
+def pair_kernel(side, count, at_weights, late, has_sum, *refs):
     refs = list(refs)
     take = lambda n: [refs.pop(0) for _ in range(n)]
     partners = [take(1 if late else 2) for _ in range(count)]
-    own = take(2)
-    beside = None if late else take(2)
+    targets = [take(2) for _ in range(1 if late else 2)]
     (weight_ref,) = take(1)
     lane_f, lane_b, twist, turn = take(4)
     sums = take(2) if has_sum else None
-    outs = take(3 if late else 2)
-    target, x_re, x_im, high_ref, low_ref, g_ref = take(6)
+    before = take(2) if late else None
+    outs = take(3)
+    x_re, x_im, high_ref, low_ref, f_ref, back_high, back_low, g_ref = take(8)
+    if late:
+        partners = [[whole.at[0:2], whole.at[2:4]] for (whole,) in partners]
 
     tiles = side * side // LANES
     half = side // 2
     subs = 2 * GROUP
     rows = half * subs
+    groups = tiles // GROUP
+    halves = 2 if late else 1
 
     def parts(ref):
         return ref[0], ref[1]
 
-    if late:
-        for h in range(2):
-            target[h] = own[h][:, 0]
-        partners = [[whole.at[0:2], whole.at[2:4]] for (whole,) in partners]
-    else:
-        home = lax.axis_index("kb") % 2 == lax.axis_index("slab")
-        for h in range(2):
-            target[h] = jnp.where(home, own[h][:, 0], beside[h][:, 0])
-
-    groups = tiles // GROUP
-
-    def spread(p, b, x, parity):
-        start = ((p * groups + b // GROUP) * half + x) * STEP + parity * GROUP + b % GROUP
+    def field(band, h, block, t):
+        return band[h][0, 0, block, lane_slice(t)], band[h][1, 0, block, lane_slice(t)]
+
+    def spread(pair, b, x, parity):
+        start = ((pair * groups + b // GROUP) * half + x) * STEP + parity * GROUP + b % GROUP
         return pl.ds(start, SUBLANES, stride=STEP)
 
     def packed(g, x):
         return pl.ds((g * half + x) * STEP, subs)
 
-    def densities(p):
+    def densities(pair, target, partner):
         for x in range(0, half, SUBLANES):
             block = pl.ds(x, SUBLANES)
             both = []
             for h in range(2):
                 values = []
                 for t in range(tiles):
-                    t_re, t_im = target[h, 0, block, lane_slice(t)], target[h, 1, block, lane_slice(t)]
-                    p_re = partners[p][h][0, 0, block, lane_slice(t)]
-                    p_im = partners[p][h][1, 0, block, lane_slice(t)]
+                    t_re, t_im = field(target, h, block, t)
+                    p_re, p_im = field(partner, h, block, t)
                     values.append((p_re * t_re + p_im * t_im, p_re * t_im - p_im * t_re))
                 both.append(dft_list(values, -1))
             turn_re, turn_im = turn[0, block], turn[1, block]
@@ -188,10 +184,10 @@
                     if b:
                         cosine, sine = twist[b, 0], twist[b, 1]
                         re, im = re * cosine + im * sine, im * cosine - re * sine
-                    x_re[spread(p, b, x, parity), :] = re
-                    x_im[spread(p, b, x, parity), :] = im
-
-    def forward(g):
+                    x_re[spread(pair, b, x, parity), :] = re
+                    x_im[spread(pair, b, x, parity), :] = im
+
+    def transform(g, weights):
         values = [(x_re[packed(g, x), :], x_im[packed(g, x), :]) for x in range(half)]
         values = dft_list(values, -1)
         for x in range(0, half, 2):
@@ -200,111 +196,119 @@
                 high, low = split(jnp.concatenate([values[x][k], values[x + 1][k]], 0))
                 high_ref[at, lane_slice(k)] = high
                 low_ref[at, lane_slice(k)] = low
-
-    def middle(g):
         at = pl.ds(g * rows, rows)
         spectrum = dot_parts((high_ref[at, :], low_ref[at, :]), parts(lane_f))
-        weights = weight_ref[first + g // groups, pl.ds(g % groups * rows, rows), :]
-        weighted = split(spectrum * jnp.concatenate([weights, weights], 1))
-        g_ref[at, :] = dot_parts(weighted, parts(lane_b))
-
-    def backward(g):
+        f_ref[at, :] = spectrum * jnp.concatenate([weights, weights], 1)
         values = []
         for x in range(half):
             at = pl.ds(g * rows + x * subs, subs)
-            values.append((g_ref[at, lane_slice(0)], g_ref[at, lane_slice(1)]))
+            values.append((f_ref[at, lane_slice(0)], f_ref[at, lane_slice(1)]))
         for x, (re, im) in enumerate(dft_list(values, 1)):
             x_re[packed(g, x), :] = re
             x_im[packed(g, x), :] = im
 
-    for p in range(count):
-        densities(p)
-        for g in range(p * groups, (p + 1) * groups):
-            forward(g)
-            middle(g)
-            backward(g)
-    gram_re = jnp.zeros((SUBLANES, LANES), F32)
-    gram_im = jnp.zeros((SUBLANES, LANES), F32)
-    for x in range(0, half, SUBLANES):
-        block = pl.ds(x, SUBLANES)
-        total = [[[0.0, 0.0] for _ in range(tiles)] for _ in range(2)]
-        if has_sum:
-            for h in range(2):
+    def potentials(pair):
+        for b in range(tiles):
+            made = [[] for _ in range(halves)]
+            for x in range(0, half, SUBLANES):
+                block = pl.ds(x, SUBLANES)
+                turn_re, turn_im = turn[0, block], turn[1, block]
+                even_re, even_im = x_re[spread(pair, b, x, 0), :], x_im[spread(pair, b, x, 0), :]
+                re, im = x_re[spread(pair, b, x, 1), :], x_im[spread(pair, b, x, 1), :]
+                re, im = re * turn_re - im * turn_im, im * turn_re + re * turn_im
+                made[0].append((even_re + re, even_im + im))
+                if late:
+                    made[1].append((even_re - re, even_im - im))
+            for h in range(halves):
+                at = pl.ds(((pair * halves + h) * tiles + b) * half, half)
+                for k in range(2):
+                    high, low = split(jnp.concatenate([block[k] for block in made[h]], 0))
+                    back_high[at, lane_slice(k)] = high
+                    back_low[at, lane_slice(k)] = low
+        at = pl.ds(pair * halves * tiles * half, halves * tiles * half)
+        g_ref[at, :] = dot_parts((back_high[at, :], back_low[at, :]), parts(lane_b))
+
+    for c, target in enumerate(targets):
+        for p, partner in enumerate(partners):
+            pair = c * count + p
+            densities(pair, target, partner)
+            for g in range(groups):
+                weights = weight_ref[at_weights[c] + p, pl.ds(g * rows, rows), :]
+                transform(pair * groups + g, weights)
+            potentials(pair)
+    for c, target in enumerate(targets):
+        gram_re = jnp.zeros((SUBLANES, LANES), F32)
+        gram_im = jnp.zeros((SUBLANES, LANES), F32)
+        for h in range(halves):
+            for x in range(0, half, SUBLANES):
+                block = pl.ds(x, SUBLANES)
+                total = [[0.0, 0.0] for _ in range(tiles)]
+                if has_sum:
+                    for t in range(tiles):
+                        for k in range(2):
+                            total[t][k] = sums[c][pl.ds((k * tiles + t) * half + x, SUBLANES), :]
+                for p, partner in enumerate(partners):
+                    values = []
+                    for b in range(tiles):
+                        pair = c * count + p
+                        start = ((pair * halves + h) * tiles + b) * half + x
+                        at = pl.ds(start, SUBLANES)
+                        re, im = g_ref[at, lane_slice(0)], g_ref[at, lane_slice(1)]
+                        if b:
+                            cosine, sine = twist[b, 0], twist[b, 1]
+                            re, im = re * cosine - im * sine, im * cosine + re * sine
+                        values.append((re, im))
+                    for t, (re, im) in enumerate(dft_list(values, 1)):
+                        p_re, p_im = field(partner, h, block, t)
+                        total[t][0] = total[t][0] + (p_re * re - p_im * im)
+                        total[t][1] = total[t][1] + (p_re * im + p_im * re)
                 for t in range(tiles):
-                    for k in range(2):
-                        total[h][t][k] = sums[h][pl.ds((k * tiles + t) * half + x, SUBLANES), :]
-        turn_re, turn_im = turn[0, block], turn[1, block]
-        for p in range(count):
-            both = [], []
-            for b in range(tiles):
-                pair = []
-                for parity in range(2):
-                    re, im = x_re[spread(p, b, x, parity), :], x_im[spread(p, b, x, parity), :]
-                    if b:
-                        cosine, sine = twist[b, 0], twist[b, 1]
-                        re, im = re * cosine - im * sine, im * cosine + re * sine
-                    pair.append((re, im))
-                re, im = pair[1]
-                re, im = re * turn_re - im * turn_im, im * turn_re + re * turn_im
-                both[0].append((pair[0][0] + re, pair[0][1] + im))
-                both[1].append((pair[0][0] - re, pair[0][1] - im))
-            for h in range(2):
-                for t, (re, im) in enumerate(dft_list(both[h], 1)):
-                    p_re = partners[p][h][0, 0, block, lane_slice(t)]
-                    p_im = partners[p][h][1, 0, block, lane_slice(t)]
-                    total[h][t][0] = total[h][t][0] + (p_re * re - p_im * im)
-                    total[h][t][1] = total[h][t][1] + (p_re * im + p_im * re)
-        for h in range(2):
-            for t in range(tiles):
-                re, im = total[h][t]
-                t_re, t_im = target[h, 0, block, lane_slice(t)], target[h, 1, block, lane_slice(t)]
-                gram_re += t_re * re + t_im * im
-                gram_im += t_re * im - t_im * re
-                outs[h][pl.ds(t * half + x, SUBLANES), :] = re
-                if late and h:
-                    outs[2][pl.ds(t * half + x, SUBLANES), :] = im
-                else:
-                    outs[h][pl.ds((tiles + t) * half + x, SUBLANES), :] = im
-    end = 2 * tiles * half
-    scale = 1.0 / side**3
-    sums_row = jnp.concatenate(
-        [
-            jnp.full((4, LANES), jnp.sum(gram_re) * scale, F32),
-            jnp.full((4, LANES), jnp.sum(gram_im) * scale, F32),
-        ],
-        0,
-    )
-    outs[0][pl.ds(end, 8), :] = sums_row
-    outs[1][pl.ds(end // 2 if late else end, 8), :] = sums_row
+                    re, im = total[t]
+                    t_re, t_im = field(target, h, block, t)
+                    gram_re += t_re * re + t_im * im
+                    gram_im += t_re * im - t_im * re
+                    if late and h:
+                        outs[1][pl.ds(t * half + x, SUBLANES), :] = re
+                        outs[2][pl.ds(t * half + x, SUBLANES), :] = im
+                    else:
+                        outs[c][pl.ds(t * half + x, SUBLANES), :] = re
+                        outs[c][pl.ds((tiles + t) * half + x, SUBLANES), :] = im
+        end = 2 * tiles * half
+        scale = 1.0 / side**3
+        sums_row = jnp.concatenate(
+            [
+                jnp.full((4, LANES), jnp.sum(gram_re) * scale, F32),
+                jnp.full((4, LANES), jnp.sum(gram_im) * scale, F32),
+            ],
+            0,
+        )
+        if late:
+            sums_row += before[0][pl.ds(end, 8), :] + before[1][...]
+            outs[0][pl.ds(end, 8), :] = sums_row
+            outs[1][pl.ds(end // 2, 8), :] = sums_row
+        else:
+            outs[c][pl.ds(end, 8), :] = sums_row
+            if c:
+                outs[2][...] = sums_row
 
 
 def join_kernel(*refs):
-    *parts, applied_ref, gram_ref = refs
-    own, near, away_mine, away_near, *late = parts
+    home, away, *late, applied_ref, gram_ref = refs
     half = applied_ref.shape[2]
     tiles = applied_ref.shape[3] // LANES
-    home = lax.axis_index("kb") % 2 == lax.axis_index("slab")
-
-    def total(k, at, size):
-        at_all = pl.ds(at if k == 0 else tiles * half + at, size)
-        found = jnp.where(home, own[at_all, :], near[at_all, :]) + jnp.where(
-            home, away_mine[at_all, :], away_near[at_all, :]
-        )
-        if late:
-            found += late[0][at_all, :] + late[1 + k][pl.ds(at, size), :]
-        return found
-
     for k in range(2):
         for t in range(tiles):
-            applied_ref[k, 0, :, lane_slice(t)] = total(k, t * half, half)
-    end = pl.ds(2 * tiles * half, 8)
-    sums = jnp.where(home, own[end, :], near[end, :]) + jnp.where(
-        home, away_mine[end, :], away_near[end, :]
-    )
+            at = pl.ds((k * tiles + t) * half, half)
+            found = home[at, :] + away[at, :]
+            if late:
+                found += late[0][at, :] + late[1 + k][pl.ds(t * half, half), :]
+            applied_ref[k, 0, :, lane_slice(t)] = found
     if late:
-        sums += late[0][end, :] + late[1][pl.ds(tiles * half, 8), :]
-    gram_ref[0, 0, 0] = jnp.max(sums[0:1, :])
-    gram_ref[0, 0, 1] = jnp.max(sums[4:5, :])
+        gram = late[0][pl.ds(2 * tiles * half, 8), :] + late[1][pl.ds(tiles * half, 8), :]
+    else:
+        gram = home[pl.ds(2 * tiles * half, 8), :]
+    gram_ref[0, 0, 0] = jnp.max(gram[0:1, :])
+    gram_ref[0, 0, 1] = jnp.max(gram[4:5, :])
 
 
 VMEM = pl.BlockSpec(memory_space=pltpu.VMEM)
@@ -313,13 +317,15 @@
 
 COST = pl.CostEstimate(flops=1, bytes_accessed=1, transcendentals=0)
 
+LATE_COST = pl.CostEstimate(flops=2 * 10**9, bytes_accessed=4 * 2**20, transcendentals=0)
+
 
 def params():
     return pltpu.CompilerParams(vmem_limit_bytes=48 * 2**20)
 
 
 def choose_weights(q_index, owner, kernels, order, late, side, blocks_per_k):
-    count = len(order) + (late is not None)
+    count = 2 * len(order) + (late is not None)
     return pl.pallas_call(
         functools.partial(weight_kernel, side, blocks_per_k, order, late),
         out_shape=jax.ShapeDtypeStruct((count, side**3 // LANES, LANES), F32),
@@ -331,11 +337,13 @@
     )(q_index, owner, *kernels)
 
 
-def apply_pairs(own, beside, partners, weights, first, side, sums=None, late=False):
-    count = len(partners)
+def apply_pairs(targets, partners, weights, at_weights, side, sums=(), before=()):
+    count, late = len(partners), len(targets) == 1
     half = side // 2
     tiles = side * side // LANES
-    rows = count * side**3 // LANES
+    pairs = count * len(targets)
+    rows = pairs * side**3 // LANES
+    back = rows if late else rows // 2
     lane = lane_table(side)
     tables = [
         jnp.asarray(bf16_parts(lane)),
@@ -343,27 +351,28 @@
         jnp.asarray(twist_table(side, SUBLANES)),
         jnp.asarray(turn_table(side)),
     ]
-    operands = [x for pair in partners for x in pair] + [*own, *beside, weights, *tables]
-    operands += list(sums) if sums is not None else []
-    shapes = [2 * tiles * half + 8] * 2
-    if late:
-        shapes[1:] = [tiles * half + 8, tiles * half]
-    messages = tuple(jax.ShapeDtypeStruct((n, LANES), F32) for n in shapes)
+    operands = [x for pair in partners for x in pair] + [x for pair in targets for x in pair]
+    operands += [weights, *tables, *sums, *before]
+    size = 2 * tiles * half + 8
+    sizes = [size, tiles * half + 8, tiles * half] if late else [size, size, 8]
+    messages = tuple(jax.ShapeDtypeStruct((n, LANES), F32) for n in sizes)
     return pl.pallas_call(
-        functools.partial(pair_kernel, side, count, first, late, sums is not None),
+        functools.partial(pair_kernel, side, count, at_weights, late, len(sums) > 0),
         out_shape=messages,
         in_specs=[VMEM] * len(operands),
         out_specs=(VMEM,) * len(messages),
         scratch_shapes=[
-            pltpu.VMEM((2, 2, half, side * side), F32),
             pltpu.VMEM((rows // SUBLANES * STEP, LANES), F32),
             pltpu.VMEM((rows // SUBLANES * STEP, LANES), F32),
             pltpu.VMEM((rows, 2 * LANES), BF16),
             pltpu.VMEM((rows, 2 * LANES), BF16),
             pltpu.VMEM((rows, 2 * LANES), F32),
+            pltpu.VMEM((back, 2 * LANES), BF16),
+            pltpu.VMEM((back, 2 * LANES), BF16),
+            pltpu.VMEM((back, 2 * LANES), F32),
         ],
         compiler_params=params(),
-        cost_estimate=COST,
+        cost_estimate=LATE_COST if late else COST,
         name="pairs",
     )(*operands)
 
@@ -400,8 +409,6 @@
     n_kb = lax.axis_size("kb")
     lines = n_kb // 2
     blocks_per_k = n_kb // NK
-    place, core = lax.axis_index("kb"), lax.axis_index("slab")
-    column = place % 2
     across = [(a, a ^ 1) for a in range(n_kb)]
 
     def swap(x):
@@ -427,27 +434,24 @@
     far = {d: swap(arrived[d]) for d in first}
     beside = (arrived[0], far[0])
     partners = [own] + [(arrived[d], far[d]) for d in order[1:]]
-    sums = None
+    sums = ()
     for at in range(0, len(order), 4):
-        sums = apply_pairs(own, beside, partners[at : at + 4], weights, at, side, sums)
+        at_weights = (at, len(order) + at)
+        sums = apply_pairs(
+            (own, beside), partners[at : at + 4], weights, at_weights, side, sums[:2]
+        )
     if late is not None:
         steps = (2 * late, 2 * late + 1)
         moves = [(2 * a + c, 2 * (a ^ steps[c]) + c) for a in range(n_kb) for c in range(2)]
         last = lax.ppermute(jnp.concatenate(own), ("kb", "slab"), moves)
         last, _ = lax.optimization_barrier((last, sums))
-    mine, other_rows = sums
-    crossed = [
-        (2 * a + core, 2 * (a ^ 1) + 1 - core) for a in range(n_kb) for core in range(2)
-    ]
-    parts = [
-        mine,
-        swap(other_rows),
-        lax.ppermute(mine, "kb", across),
-        lax.ppermute(other_rows, ("kb", "slab"), crossed),
-    ]
+    home, away, away_sums = sums
+    parts = [home, lax.ppermute(away, "kb", across)]
     if late is not None:
+        crossed = [(2 * a + c, 2 * (a ^ 1) + 1 - c) for a in range(n_kb) for c in range(2)]
+        crossed_sums = lax.ppermute(away_sums, ("kb", "slab"), crossed)
         late_mine, *late_rows = apply_pairs(
-            own, (), [(last,)], weights, len(order), side, late=True
+            (own,), [(last,)], weights, (2 * len(order),), side, before=(home, crossed_sums)
         )
         parts += [late_mine, *(swap(x) for x in late_rows)]
     applied, gram = join(parts, orbitals.shape)

time: 26.4 us -> 26.1 us (0.989)
  the two profiles are of different devices: /device:TPU:9 before, /device:TPU:0 now
where the time goes in v6:
time: 26.1 us; the launch traced here: 25.9 us
  starting transfers between devices  11.3 us (43%)
  Pallas kernels  6.26 us (24%)
  waiting for transfers between devices  5.27 us (20%)
  local copies, waits for them, and re-layouts  1.38 us (5%)
  other arithmetic  0.95 us (4%)
  between operations  0.74 us (3%)
    ppermute x2, starting transfers between devices, from_line(): lax.ppermute(x, 'kb', [(2 * a + c, 2 * (a ^ d) + c) for a in range(lines)...  5.59 us
    pallas_call x2, Pallas kernels, apply_pairs(): pl.pallas_call(functools.partial(pair_kernel, side, count, at_weights, la...  4.16 us
    ppermute x7, waiting for transfers between devices, swap(): return lax.ppermute(x, 'slab', [(0, 1), (1, 0)])  2.15 us
    ppermute x1, waiting for transfers between devices, on_device(): parts = [home, lax.ppermute(away, 'kb', across)]  1.91 us
    ppermute x7, starting transfers between devices, swap(): return lax.ppermute(x, 'slab', [(0, 1), (1, 0)])  1.9 us
    ppermute x1, starting transfers between devices, on_device(): crossed_sums = lax.ppermute(away_sums, ('kb', 'slab'), crossed)  1.75 us
    ppermute x1, starting transfers between devices, on_device(): arrived[0] = lax.ppermute(orbitals, 'kb', across)  1.52 us
    pallas_call x1, Pallas kernels, choose_weights(): pl.pallas_call(functools.partial(weight_kernel, side, blocks_per_k, order...  1.4 us
  transfers between devices with their start and end apart: 13, of which 7 were waited for; matrix products, arithmetic and copies ran while one was open for 4% of the time, Pallas kernels for 21%

profile of v6, /device:TPU:0, one launch (start us, length us, event | category | flops | bytes accessed | tf_op | source)
XLA Modules:
  0.0 25.9 jit_solution(4229385798961264219)
XLA Ops:
  0.6 0.0 copy-start.1
  0.6 0.5 %collective-permute-start.4 = (f32[8,32,512]{2,1,0:T(8,128)}, f32[8,32,512]{2,1,0:T(8,128)S(1)}, u32[]{:S(2)}, u32[]{:S(2)}) collective-permute-start(f32[8,32,512]{2,1,0:T(8,128)} %mine_ref.1), channel_id=1, source_target_pairs={{0,1},{1,0},{2,3},{3,2},{4,5},{5,4},{6,7},{7,6},{8,9},{9,8},{10,11... | collective-permute-start | bytes 1572872 | tf_op jit(solution)/shard_map/ppermute | solution.py:415
  1.2 0.1 collective-permute-start
  1.2 4.0 %collective-permute-start.1 = (f32[2,1,16,1024]{3,2,1,0:T(8,128)}, f32[2,1,16,1024]{3,2,1,0:T(8,128)S(1)}, u32[]{:S(2)}, u32[]{:S(2)}) collective-permute-start(f32[2,1,16,1024]{3,2,1,0:T(8,128)} %refs_1_.1), channel_id=1, source_target_pairs={{0,8},{2,10},{4,12},{6,14},{8,0},{10,2},{12,4},{14,6},{1,9},{3,11}... | collective-permute-start | bytes 393224 | tf_op jit(solution)/shard_map/ppermute | solution.py:418
  5.3 1.6 %collective-permute-start.2 = (f32[2,1,16,1024]{3,2,1,0:T(8,128)}, f32[2,1,16,1024]{3,2,1,0:T(8,128)S(1)}, u32[]{:S(2)}, u32[]{:S(2)}) collective-permute-start(f32[2,1,16,1024]{3,2,1,0:T(8,128)} %refs_1_.1), channel_id=1, source_target_pairs={{0,4},{2,6},{4,0},{6,2},{8,12},{10,14},{12,8},{14,10},{1,5},{3,7},... | collective-permute-start | bytes 393224 | tf_op jit(solution)/shard_map/ppermute | solution.py:418
  6.8 1.5 %collective-permute-start.3 = (f32[2,1,16,1024]{3,2,1,0:T(8,128)}, f32[2,1,16,1024]{3,2,1,0:T(8,128)S(1)}, u32[]{:S(2)}, u32[]{:S(2)}) collective-permute-start(f32[2,1,16,1024]{3,2,1,0:T(8,128)} %refs_1_.1), channel_id=1, source_target_pairs={{0,2},{2,0},{4,6},{6,4},{8,10},{10,8},{12,14},{14,12},{1,3},{3,1},... | collective-permute-start | bytes 393224 | tf_op jit(solution)/shard_map/ppermute | solution.py:427
  8.3 0.0 collective-permute-done.refs_1_.refs_7_.refs_2_
  8.4 1.0 %pad_maximum_fusion = f32[4,1,16,1024]{3,2,1,0:T(8,128)S(1)} fusion(f32[2,1,16,1024]{3,2,1,0:T(8,128)S(1)} %collective-permute-done.refs_1_.refs_7_.refs_2_, f32[2,1,16,1024]{3,2,1,0:T(8,128)} %refs_1_.1), kind=kLoop, calls=%fused_computation | loop fusion | flops 65536 | bytes 524288 | tf_op jit(solution)/shard_map/concatenate | solution.py:446
  9.3 0.0 copy-start
  9.3 0.0 copy-start.2
  9.3 0.0 copy-start.3
  9.3 0.0 copy-start.4
  9.4 0.0 copy-start.5
  9.4 0.3 %collective-permute-start.9 = (f32[4,1,16,1024]{3,2,1,0:T(8,128)S(1)}, f32[4,1,16,1024]{3,2,1,0:T(8,128)S(1)}, u32[]{:S(2)}, u32[]{:S(2)}) collective-permute-start(f32[4,1,16,1024]{3,2,1,0:T(8,128)S(1)} %pad_maximum_fusion), channel_id=1, source_target_pairs={{0,12},{1,15},{2,14},{3,13},{4,8},{5,11},{6,10},{7,9},{8,4},{9,7},... | collective-permute-start | bytes 786440 | tf_op jit(solution)/shard_map/ppermute | solution.py:446
  9.7 0.0 collective-permute-done.4.other_ref
  9.7 0.0 copy-done.1
  9.7 0.0 copy-start.6
  9.7 0.7 %copy-done.6 = s32[8,8]{1,0:T(8,128)S(1)} copy-done((s32[8,8]{1,0:T(8,128)S(1)}, s32[8,8]{1,0:T(8,128)}, u32[]{:S(2)}) %copy-start.6) | copy-done | bytes 280
  10.4 0.0 copy-start.7
  10.4 0.7 %copy-done.7 = s32[8]{0:T(128)S(1)} copy-done((s32[8]{0:T(128)S(1)}, s32[8]{0:T(128)}, u32[]{:S(2)}) %copy-start.7) | copy-done | bytes 56
  11.0 1.4 %weights.1.refs_10_.refs_3_ = f32[7,256,128]{2,1,0:T(8,128)S(1)} custom-call(s32[8,8]{1,0:T(8,128)S(1)} %copy-done.6, s32[8]{0:T(128)S(1)} %copy-done.7, f32[8,32,512]{2,1,0:T(8,128)S(1)} %copy-done.1, f32[8,32,512]{2,1,0:T(8,128)S(1)} %collective-permute-done.4.other_ref), custom_call_target="tpu_custom_call" | custom-call | flops 1 | bytes 1 | tf_op jit(solution)/shard_map/weights/pallas_call | solution.py:329
  12.4 0.1 collective-permute-done.1.refs_4_
  12.6 0.0 collective-permute-done.2.refs_2_
  12.6 0.0 collective-permute-done.3.refs_8_
  12.6 0.2 collective-permute-start.5
  12.8 0.3 %collective-permute-start.6 = (f32[2,1,16,1024]{3,2,1,0:T(8,128)S(1)}, f32[2,1,16,1024]{3,2,1,0:T(8,128)S(1)}, u32[]{:S(2)}, u32[]{:S(2)}) collective-permute-start(f32[2,1,16,1024]{3,2,1,0:T(8,128)S(1)} %collective-permute-done.1.refs_4_), channel_id=1, source_target_pairs={{0,1},{1,0},{2,3},{3,2},{4,5},{5,4},{6,7},{7,6},{8,9},{9,8},{10,11... | collective-permute-start | bytes 393224 | tf_op jit(solution)/shard_map/ppermute | solution.py:415
  13.1 0.2 collective-permute-start.7
  13.3 0.6 %collective-permute-done.5.refs_3_ = f32[2,1,16,1024]{3,2,1,0:T(8,128)S(1)} collective-permute-done((f32[2,1,16,1024]{3,2,1,0:T(8,128)S(1)}, f32[2,1,16,1024]{3,2,1,0:T(8,128)S(1)}, u32[]{:S(2)}, u32[]{:S(2)}) %collective-permute-start.5) | collective-permute-done | bytes 131104 | tf_op jit(solution)/shard_map/ppermute | solution.py:415
  13.9 0.2 collective-permute-done.6.refs_5_
  14.1 0.3 %collective-permute-done.7.refs_9_ = f32[2,1,16,1024]{3,2,1,0:T(8,128)S(1)} collective-permute-done((f32[2,1,16,1024]{3,2,1,0:T(8,128)S(1)}, f32[2,1,16,1024]{3,2,1,0:T(8,128)S(1)}, u32[]{:S(2)}, u32[]{:S(2)}) %collective-permute-start.7) | collective-permute-done | bytes 131104 | tf_op jit(solution)/shard_map/ppermute | solution.py:415
  14.4 0.0 copy-done
  14.4 0.0 copy-done.2
  14.4 0.0 copy-done.3
  14.4 0.0 copy-done.4
  14.5 0.0 copy-done.5
  14.5 3.2 %pairs.2 = (f32[264,128]{1,0:T(8,128)S(1)}, f32[264,128]{1,0:T(8,128)S(1)}, f32[8,128]{1,0:T(8,128)S(1)}) custom-call(f32[2,1,16,1024]{3,2,1,0:T(8,128)S(1)} %copy-done, f32[2,1,16,1024]{3,2,1,0:T(8,128)S(1)} %collective-permute-done.refs_1_.refs_7_.refs_2_, f32[2,1,16,1024]{3,2,1,0:T(8,128)S(1)} %collective-permute-done.2.refs_2_, ...), custom_call_target="tpu_custom_call" | custom-call | flops 1 | bytes 1 | tf_op jit(solution)/shard_map/pairs/pallas_call | solution.py:359
  17.7 1.7 %collective-permute-start.10 = (f32[8,128]{1,0:T(8,128)S(1)}, f32[8,128]{1,0:T(8,128)S(1)}, u32[]{:S(2)}, u32[]{:S(2)}) collective-permute-start(f32[8,128]{1,0:T(8,128)S(1)} %get-tuple-element.21), channel_id=1, source_target_pairs={{0,3},{1,2},{2,1},{3,0},{4,7},{5,6},{6,5},{7,4},{8,11},{9,10},{10,... | collective-permute-start | bytes 12296 | tf_op jit(solution)/shard_map/ppermute | solution.py:452
  19.4 0.3 %collective-permute-start.8 = (f32[264,128]{1,0:T(8,128)S(1)}, f32[264,128]{1,0:T(8,128)S(1)}, u32[]{:S(2)}, u32[]{:S(2)}) collective-permute-start(f32[264,128]{1,0:T(8,128)S(1)} %get-tuple-element.20), channel_id=1, source_target_pairs={{0,2},{2,0},{4,6},{6,4},{8,10},{10,8},{12,14},{14,12},{1,3},{3,1},... | collective-permute-start | bytes 405512 | tf_op jit(solution)/shard_map/ppermute | solution.py:449
  19.7 0.0 collective-permute-done.9.refs_0_
  19.7 1.1 %collective-permute-done.10.refs_9_ = f32[8,128]{1,0:T(8,128)S(1)} collective-permute-done((f32[8,128]{1,0:T(8,128)S(1)}, f32[8,128]{1,0:T(8,128)S(1)}, u32[]{:S(2)}, u32[]{:S(2)}) %collective-permute-start.10) | collective-permute-done | bytes 4128 | tf_op jit(solution)/shard_map/ppermute | solution.py:452
  20.8 1.0 %pairs.3 = (f32[264,128]{1,0:T(8,128)S(1)}, f32[136,128]{1,0:T(8,128)S(1)}, f32[128,128]{1,0:T(8,128)S(1)}) custom-call(f32[4,1,16,1024]{3,2,1,0:T(8,128)S(1)} %collective-permute-done.9.refs_0_, f32[2,1,16,1024]{3,2,1,0:T(8,128)S(1)} %copy-done, f32[2,1,16,1024]{3,2,1,0:T(8,128)S(1)} %collective-permute-done.refs_1_.refs_7_.refs_2_, ...), custom_call_target="tpu_custom_call" | custom-call | flops 2000000000 | bytes 4194304 | tf_op jit(solution)/shard_map/pairs/pallas_call | solution.py:359
  21.7 0.3 %collective-permute-start.11 = (f32[136,128]{1,0:T(8,128)S(1)}, f32[136,128]{1,0:T(8,128)S(1)}, u32[]{:S(2)}, u32[]{:S(2)}) collective-permute-start(f32[136,128]{1,0:T(8,128)S(1)} %get-tuple-element.24), channel_id=1, source_target_pairs={{0,1},{1,0},{2,3},{3,2},{4,5},{5,4},{6,7},{7,6},{8,9},{9,8},{10,11... | collective-permute-start | bytes 208904 | tf_op jit(solution)/shard_map/ppermute | solution.py:415
  22.1 0.2 collective-permute-start.12
  22.3 1.0 %collective-permute-done.12.refs_4_ = f32[128,128]{1,0:T(8,128)S(1)} collective-permute-done((f32[128,128]{1,0:T(8,128)S(1)}, f32[128,128]{1,0:T(8,128)S(1)}, u32[]{:S(2)}, u32[]{:S(2)}) %collective-permute-start.12) | collective-permute-done | bytes 65568 | tf_op jit(solution)/shard_map/ppermute | solution.py:415
  23.3 0.0 collective-permute-done.11.refs_3_
  23.3 1.9 %collective-permute-done.8.refs_1_ = f32[264,128]{1,0:T(8,128)S(1)} collective-permute-done((f32[264,128]{1,0:T(8,128)S(1)}, f32[264,128]{1,0:T(8,128)S(1)}, u32[]{:S(2)}, u32[]{:S(2)}) %collective-permute-start.8) | collective-permute-done | bytes 135200 | tf_op jit(solution)/shard_map/ppermute | solution.py:449
  25.2 0.7 %join.1 = (f32[2,1,16,1024]{3,2,1,0:T(8,128)}, f32[1,1,2]{2,1,0:T(1,128)}) custom-call(f32[264,128]{1,0:T(8,128)S(1)} %get-tuple-element.19.refs_8_.refs_0_, f32[264,128]{1,0:T(8,128)S(1)} %collective-permute-done.8.refs_1_, f32[264,128]{1,0:T(8,128)S(1)} %get-tuple-element.23.refs_2_, f32[136,128]{1,0:T(8,128)S(1)} %collective-permute-done.11.refs_3_, ...), custom_call_target="tpu_custom_call" | custom-call | flops 1 | bytes 1 | tf_op jit(solution)/shard_map/join/pallas_call | solution.py:381
Async XLA Ops:
  0.6 9.0 %copy-start.1 = (f32[8,32,512]{2,1,0:T(8,128)S(1)}, f32[8,32,512]{2,1,0:T(8,128)}, u32[]{:S(2)}) copy-start(f32[8,32,512]{2,1,0:T(8,128)} %mine_ref.1) | copy-start | bytes 1572868
  0.6 9.0 %collective-permute-start.4 = (f32[8,32,512]{2,1,0:T(8,128)}, f32[8,32,512]{2,1,0:T(8,128)S(1)}, u32[]{:S(2)}, u32[]{:S(2)}) collective-permute-start(f32[8,32,512]{2,1,0:T(8,128)} %mine_ref.1), channel_id=1, source_target_pairs={{0,1},{1,0},{2,3},{3,2},{4,5},{5,4},{6,7},{7,6},{8,9},{9,8},{10,11... | collective-permute-start | bytes 1572872 | tf_op jit(solution)/shard_map/ppermute | solution.py:415
  1.2 7.2 %collective-permute-start = (f32[2,1,16,1024]{3,2,1,0:T(8,128)}, f32[2,1,16,1024]{3,2,1,0:T(8,128)S(1)}, u32[]{:S(2)}, u32[]{:S(2)}) collective-permute-start(f32[2,1,16,1024]{3,2,1,0:T(8,128)} %refs_1_.1), channel_id=1, source_target_pairs={{0,1},{1,0},{2,3},{3,2},{4,5},{5,4},{6,7},{7,6},{8,9},{9,8},{10,11... | collective-permute-start | bytes 393224 | tf_op jit(solution)/shard_map/ppermute | solution.py:415
  1.2 11.3 %collective-permute-start.1 = (f32[2,1,16,1024]{3,2,1,0:T(8,128)}, f32[2,1,16,1024]{3,2,1,0:T(8,128)S(1)}, u32[]{:S(2)}, u32[]{:S(2)}) collective-permute-start(f32[2,1,16,1024]{3,2,1,0:T(8,128)} %refs_1_.1), channel_id=1, source_target_pairs={{0,8},{2,10},{4,12},{6,14},{8,0},{10,2},{12,4},{14,6},{1,9},{3,11}... | collective-permute-start | bytes 393224 | tf_op jit(solution)/shard_map/ppermute | solution.py:418
  5.3 7.3 %collective-permute-start.2 = (f32[2,1,16,1024]{3,2,1,0:T(8,128)}, f32[2,1,16,1024]{3,2,1,0:T(8,128)S(1)}, u32[]{:S(2)}, u32[]{:S(2)}) collective-permute-start(f32[2,1,16,1024]{3,2,1,0:T(8,128)} %refs_1_.1), channel_id=1, source_target_pairs={{0,4},{2,6},{4,0},{6,2},{8,12},{10,14},{12,8},{14,10},{1,5},{3,7},... | collective-permute-start | bytes 393224 | tf_op jit(solution)/shard_map/ppermute | solution.py:418
  6.8 5.7 %collective-permute-start.3 = (f32[2,1,16,1024]{3,2,1,0:T(8,128)}, f32[2,1,16,1024]{3,2,1,0:T(8,128)S(1)}, u32[]{:S(2)}, u32[]{:S(2)}) collective-permute-start(f32[2,1,16,1024]{3,2,1,0:T(8,128)} %refs_1_.1), channel_id=1, source_target_pairs={{0,2},{2,0},{4,6},{6,4},{8,10},{10,8},{12,14},{14,12},{1,3},{3,1},... | collective-permute-start | bytes 393224 | tf_op jit(solution)/shard_map/ppermute | solution.py:427
  9.3 5.1 %copy-start = (f32[2,1,16,1024]{3,2,1,0:T(8,128)S(1)}, f32[2,1,16,1024]{3,2,1,0:T(8,128)}, u32[]{:S(2)}) copy-start(f32[2,1,16,1024]{3,2,1,0:T(8,128)} %refs_1_.1) | copy-start | bytes 393220
  9.3 5.1 %copy-start.2 = (bf16[2,256,256]{2,1,0:T(8,128)(2,1)S(1)}, bf16[2,256,256]{2,1,0:T(8,128)(2,1)}, u32[]{:S(2)}) copy-start(bf16[2,256,256]{2,1,0:T(8,128)(2,1)} %constant.8.clone.refs_11_.refs_4_) | copy-start | bytes 786436
  9.3 5.1 %copy-start.3 = (bf16[2,256,256]{2,1,0:T(8,128)(2,1)S(1)}, bf16[2,256,256]{2,1,0:T(8,128)(2,1)}, u32[]{:S(2)}) copy-start(bf16[2,256,256]{2,1,0:T(8,128)(2,1)} %constant.9.clone.refs_12_.refs_5_) | copy-start | bytes 786436
  9.3 5.1 %copy-start.4 = (f32[8,2,8,128]{3,2,1,0:T(8,128)S(1)}, f32[8,2,8,128]{3,2,1,0:T(8,128)}, u32[]{:S(2)}) copy-start(f32[8,2,8,128]{3,2,1,0:T(8,128)} %constant.10.clone.refs_13_.refs_6_) | copy-start | bytes 196612
  9.4 5.1 %copy-start.5 = (f32[2,16,128]{2,1,0:T(8,128)S(1)}, f32[2,16,128]{2,1,0:T(8,128)}, u32[]{:S(2)}) copy-start(f32[2,16,128]{2,1,0:T(8,128)} %constant.11.clone.refs_14_.refs_7_) | copy-start | bytes 49156
  9.4 10.3 %collective-permute-start.9 = (f32[4,1,16,1024]{3,2,1,0:T(8,128)S(1)}, f32[4,1,16,1024]{3,2,1,0:T(8,128)S(1)}, u32[]{:S(2)}, u32[]{:S(2)}) collective-permute-start(f32[4,1,16,1024]{3,2,1,0:T(8,128)S(1)} %pad_maximum_fusion), channel_id=1, source_target_pairs={{0,12},{1,15},{2,14},{3,13},{4,8},{5,11},{6,10},{7,9},{8,4},{9,7},... | collective-permute-start | bytes 786440 | tf_op jit(solution)/shard_map/ppermute | solution.py:446
  9.7 0.7 %copy-start.6 = (s32[8,8]{1,0:T(8,128)S(1)}, s32[8,8]{1,0:T(8,128)}, u32[]{:S(2)}) copy-start(s32[8,8]{1,0:T(8,128)} %q_ref.1) | copy-start | bytes 772
  10.4 0.7 %copy-start.7 = (s32[8]{0:T(128)S(1)}, s32[8]{0:T(128)}, u32[]{:S(2)}) copy-start(s32[8]{0:T(128)} %owner_ref.1) | copy-start | bytes 100
  12.6 1.4 %collective-permute-start.5 = (f32[2,1,16,1024]{3,2,1,0:T(8,128)S(1)}, f32[2,1,16,1024]{3,2,1,0:T(8,128)S(1)}, u32[]{:S(2)}, u32[]{:S(2)}) collective-permute-start(f32[2,1,16,1024]{3,2,1,0:T(8,128)S(1)} %collective-permute-done.2.refs_2_), channel_id=1, source_target_pairs={{0,1},{1,0},{2,3},{3,2},{4,5},{5,4},{6,7},{7,6},{8,9},{9,8},{10,11... | collective-permute-start | bytes 393224 | tf_op jit(solution)/shard_map/ppermute | solution.py:415
  12.8 1.3 %collective-permute-start.6 = (f32[2,1,16,1024]{3,2,1,0:T(8,128)S(1)}, f32[2,1,16,1024]{3,2,1,0:T(8,128)S(1)}, u32[]{:S(2)}, u32[]{:S(2)}) collective-permute-start(f32[2,1,16,1024]{3,2,1,0:T(8,128)S(1)} %collective-permute-done.1.refs_4_), channel_id=1, source_target_pairs={{0,1},{1,0},{2,3},{3,2},{4,5},{5,4},{6,7},{7,6},{8,9},{9,8},{10,11... | collective-permute-start | bytes 393224 | tf_op jit(solution)/shard_map/ppermute | solution.py:415
  13.1 1.3 %collective-permute-start.7 = (f32[2,1,16,1024]{3,2,1,0:T(8,128)S(1)}, f32[2,1,16,1024]{3,2,1,0:T(8,128)S(1)}, u32[]{:S(2)}, u32[]{:S(2)}) collective-permute-start(f32[2,1,16,1024]{3,2,1,0:T(8,128)S(1)} %collective-permute-done.3.refs_8_), channel_id=1, source_target_pairs={{0,1},{1,0},{2,3},{3,2},{4,5},{5,4},{6,7},{7,6},{8,9},{9,8},{10,11... | collective-permute-start | bytes 393224 | tf_op jit(solution)/shard_map/ppermute | solution.py:415
  17.7 3.1 %collective-permute-start.10 = (f32[8,128]{1,0:T(8,128)S(1)}, f32[8,128]{1,0:T(8,128)S(1)}, u32[]{:S(2)}, u32[]{:S(2)}) collective-permute-start(f32[8,128]{1,0:T(8,128)S(1)} %get-tuple-element.21), channel_id=1, source_target_pairs={{0,3},{1,2},{2,1},{3,0},{4,7},{5,6},{6,5},{7,4},{8,11},{9,10},{10,... | collective-permute-start | bytes 12296 | tf_op jit(solution)/shard_map/ppermute | solution.py:452
  19.4 5.8 %collective-permute-start.8 = (f32[264,128]{1,0:T(8,128)S(1)}, f32[264,128]{1,0:T(8,128)S(1)}, u32[]{:S(2)}, u32[]{:S(2)}) collective-permute-start(f32[264,128]{1,0:T(8,128)S(1)} %get-tuple-element.20), channel_id=1, source_target_pairs={{0,2},{2,0},{4,6},{6,4},{8,10},{10,8},{12,14},{14,12},{1,3},{3,1},... | collective-permute-start | bytes 405512 | tf_op jit(solution)/shard_map/ppermute | solution.py:449
  21.7 1.6 %collective-permute-start.11 = (f32[136,128]{1,0:T(8,128)S(1)}, f32[136,128]{1,0:T(8,128)S(1)}, u32[]{:S(2)}, u32[]{:S(2)}) collective-permute-start(f32[136,128]{1,0:T(8,128)S(1)} %get-tuple-element.24), channel_id=1, source_target_pairs={{0,1},{1,0},{2,3},{3,2},{4,5},{5,4},{6,7},{7,6},{8,9},{9,8},{10,11... | collective-permute-start | bytes 208904 | tf_op jit(solution)/shard_map/ppermute | solution.py:415
  22.1 1.3 %collective-permute-start.12 = (f32[128,128]{1,0:T(8,128)S(1)}, f32[128,128]{1,0:T(8,128)S(1)}, u32[]{:S(2)}, u32[]{:S(2)}) collective-permute-start(f32[128,128]{1,0:T(8,128)S(1)} %get-tuple-element.25), channel_id=1, source_target_pairs={{0,1},{1,0},{2,3},{3,2},{4,5},{5,4},{6,7},{7,6},{8,9},{9,8},{10,11... | collective-permute-start | bytes 196616 | tf_op jit(solution)/shard_map/ppermute | solution.py:415

commit v7 on v6

--- a/solution.py
+++ b/solution.py
@@ -228,14 +228,15 @@
         at = pl.ds(pair * halves * tiles * half, halves * tiles * half)
         g_ref[at, :] = dot_parts((back_high[at, :], back_low[at, :]), parts(lane_b))
 
-    for c, target in enumerate(targets):
-        for p, partner in enumerate(partners):
-            pair = c * count + p
-            densities(pair, target, partner)
-            for g in range(groups):
-                weights = weight_ref[at_weights[c] + p, pl.ds(g * rows, rows), :]
-                transform(pair * groups + g, weights)
-            potentials(pair)
+    pairs = [(c, p) for c in range(len(targets)) for p in range(count)]
+    for pair, (c, p) in enumerate(pairs):
+        densities(pair, targets[c], partners[p])
+    for pair, (c, p) in enumerate(pairs):
+        for g in range(groups):
+            weights = weight_ref[at_weights[c] + p, pl.ds(g * rows, rows), :]
+            transform(pair * groups + g, weights)
+    for pair in range(len(pairs)):
+        potentials(pair)
     for c, target in enumerate(targets):
         gram_re = jnp.zeros((SUBLANES, LANES), F32)
         gram_im = jnp.zeros((SUBLANES, LANES), F32)

time: 26.1 us -> 26.1 us (level); the launches traced: 25.9 us -> 25.6 us
  Pallas kernels: 6.26 us -> 5.91 us
    pallas_call x2, Pallas kernels: 4.16 us -> 3.81 us  [apply_pairs(): pl.pallas_call(functools.partial(pair_kernel, side, count, at_weights, la...]
  transfers between devices with their start and end apart: 13 -> 13, of which waited for: 7 -> 7; matrix products, arithmetic and copies ran while one was open for 4% -> 4% of each run, Pallas kernels for 21% -> 20%
where the time goes in v7:
time: 26.1 us; the launch traced here: 25.6 us
  starting transfers between devices  11.3 us (43%)
  Pallas kernels  5.91 us (23%)
  waiting for transfers between devices  5.27 us (20%)
  local copies, waits for them, and re-layouts  1.38 us (5%)
  other arithmetic  0.95 us (4%)
  between operations  0.74 us (3%)
    ppermute x2, starting transfers between devices, from_line(): lax.ppermute(x, 'kb', [(2 * a + c, 2 * (a ^ d) + c) for a in range(lines)...  5.59 us
    pallas_call x2, Pallas kernels, apply_pairs(): pl.pallas_call(functools.partial(pair_kernel, side, count, at_weights, la...  3.81 us
    ppermute x7, waiting for transfers between devices, swap(): return lax.ppermute(x, 'slab', [(0, 1), (1, 0)])  2.15 us
    ppermute x1, waiting for transfers between devices, on_device(): parts = [home, lax.ppermute(away, 'kb', across)]  1.9 us
    ppermute x7, starting transfers between devices, swap(): return lax.ppermute(x, 'slab', [(0, 1), (1, 0)])  1.9 us
    ppermute x1, starting transfers between devices, on_device(): crossed_sums = lax.ppermute(away_sums, ('kb', 'slab'), crossed)  1.75 us
    ppermute x1, starting transfers between devices, on_device(): arrived[0] = lax.ppermute(orbitals, 'kb', across)  1.52 us
    pallas_call x1, Pallas kernels, choose_weights(): pl.pallas_call(functools.partial(weight_kernel, side, blocks_per_k, order...  1.4 us
  transfers between devices with their start and end apart: 13, of which 7 were waited for; matrix products, arithmetic and copies ran while one was open for 4% of the time, Pallas kernels for 20%

profile of v7, /device:TPU:0, one launch (start us, length us, event | category | flops | bytes accessed | tf_op | source)
XLA Modules:
  0.0 25.6 jit_solution(6383027502353141232)
XLA Ops:
  0.6 0.0 copy-start.1
  0.6 0.5 %collective-permute-start.4 = (f32[8,32,512]{2,1,0:T(8,128)}, f32[8,32,512]{2,1,0:T(8,128)S(1)}, u32[]{:S(2)}, u32[]{:S(2)}) collective-permute-start(f32[8,32,512]{2,1,0:T(8,128)} %mine_ref.1), channel_id=1, source_target_pairs={{0,1},{1,0},{2,3},{3,2},{4,5},{5,4},{6,7},{7,6},{8,9},{9,8},{10,11... | collective-permute-start | bytes 1572872 | tf_op jit(solution)/shard_map/ppermute | solution.py:416
  1.2 0.1 collective-permute-start
  1.2 4.0 %collective-permute-start.1 = (f32[2,1,16,1024]{3,2,1,0:T(8,128)}, f32[2,1,16,1024]{3,2,1,0:T(8,128)S(1)}, u32[]{:S(2)}, u32[]{:S(2)}) collective-permute-start(f32[2,1,16,1024]{3,2,1,0:T(8,128)} %refs_1_.1), channel_id=1, source_target_pairs={{0,8},{2,10},{4,12},{6,14},{8,0},{10,2},{12,4},{14,6},{1,9},{3,11}... | collective-permute-start | bytes 393224 | tf_op jit(solution)/shard_map/ppermute | solution.py:419
  5.3 1.6 %collective-permute-start.2 = (f32[2,1,16,1024]{3,2,1,0:T(8,128)}, f32[2,1,16,1024]{3,2,1,0:T(8,128)S(1)}, u32[]{:S(2)}, u32[]{:S(2)}) collective-permute-start(f32[2,1,16,1024]{3,2,1,0:T(8,128)} %refs_1_.1), channel_id=1, source_target_pairs={{0,4},{2,6},{4,0},{6,2},{8,12},{10,14},{12,8},{14,10},{1,5},{3,7},... | collective-permute-start | bytes 393224 | tf_op jit(solution)/shard_map/ppermute | solution.py:419
  6.8 1.5 %collective-permute-start.3 = (f32[2,1,16,1024]{3,2,1,0:T(8,128)}, f32[2,1,16,1024]{3,2,1,0:T(8,128)S(1)}, u32[]{:S(2)}, u32[]{:S(2)}) collective-permute-start(f32[2,1,16,1024]{3,2,1,0:T(8,128)} %refs_1_.1), channel_id=1, source_target_pairs={{0,2},{2,0},{4,6},{6,4},{8,10},{10,8},{12,14},{14,12},{1,3},{3,1},... | collective-permute-start | bytes 393224 | tf_op jit(solution)/shard_map/ppermute | solution.py:428
  8.3 0.0 collective-permute-done.refs_1_.refs_7_.refs_2_
  8.4 1.0 %pad_maximum_fusion = f32[4,1,16,1024]{3,2,1,0:T(8,128)S(1)} fusion(f32[2,1,16,1024]{3,2,1,0:T(8,128)S(1)} %collective-permute-done.refs_1_.refs_7_.refs_2_, f32[2,1,16,1024]{3,2,1,0:T(8,128)} %refs_1_.1), kind=kLoop, calls=%fused_computation | loop fusion | flops 65536 | bytes 524288 | tf_op jit(solution)/shard_map/concatenate | solution.py:447
  9.3 0.0 copy-start
  9.3 0.0 copy-start.2
  9.3 0.0 copy-start.3
  9.3 0.0 copy-start.4
  9.4 0.0 copy-start.5
  9.4 0.3 %collective-permute-start.9 = (f32[4,1,16,1024]{3,2,1,0:T(8,128)S(1)}, f32[4,1,16,1024]{3,2,1,0:T(8,128)S(1)}, u32[]{:S(2)}, u32[]{:S(2)}) collective-permute-start(f32[4,1,16,1024]{3,2,1,0:T(8,128)S(1)} %pad_maximum_fusion), channel_id=1, source_target_pairs={{0,12},{1,15},{2,14},{3,13},{4,8},{5,11},{6,10},{7,9},{8,4},{9,7},... | collective-permute-start | bytes 786440 | tf_op jit(solution)/shard_map/ppermute | solution.py:447
  9.7 0.0 collective-permute-done.4.other_ref
  9.7 0.0 copy-done.1
  9.7 0.0 copy-start.6
  9.7 0.7 %copy-done.6 = s32[8,8]{1,0:T(8,128)S(1)} copy-done((s32[8,8]{1,0:T(8,128)S(1)}, s32[8,8]{1,0:T(8,128)}, u32[]{:S(2)}) %copy-start.6) | copy-done | bytes 280
  10.4 0.0 copy-start.7
  10.4 0.7 %copy-done.7 = s32[8]{0:T(128)S(1)} copy-done((s32[8]{0:T(128)S(1)}, s32[8]{0:T(128)}, u32[]{:S(2)}) %copy-start.7) | copy-done | bytes 56
  11.0 1.4 %weights.1.refs_10_.refs_3_ = f32[7,256,128]{2,1,0:T(8,128)S(1)} custom-call(s32[8,8]{1,0:T(8,128)S(1)} %copy-done.6, s32[8]{0:T(128)S(1)} %copy-done.7, f32[8,32,512]{2,1,0:T(8,128)S(1)} %copy-done.1, f32[8,32,512]{2,1,0:T(8,128)S(1)} %collective-permute-done.4.other_ref), custom_call_target="tpu_custom_call" | custom-call | flops 1 | bytes 1 | tf_op jit(solution)/shard_map/weights/pallas_call | solution.py:330
  12.4 0.1 collective-permute-done.1.refs_4_
  12.6 0.0 collective-permute-done.2.refs_2_
  12.6 0.0 collective-permute-done.3.refs_8_
  12.6 0.2 collective-permute-start.5
  12.8 0.3 %collective-permute-start.6 = (f32[2,1,16,1024]{3,2,1,0:T(8,128)S(1)}, f32[2,1,16,1024]{3,2,1,0:T(8,128)S(1)}, u32[]{:S(2)}, u32[]{:S(2)}) collective-permute-start(f32[2,1,16,1024]{3,2,1,0:T(8,128)S(1)} %collective-permute-done.1.refs_4_), channel_id=1, source_target_pairs={{0,1},{1,0},{2,3},{3,2},{4,5},{5,4},{6,7},{7,6},{8,9},{9,8},{10,11... | collective-permute-start | bytes 393224 | tf_op jit(solution)/shard_map/ppermute | solution.py:416
  13.1 0.2 collective-permute-start.7
  13.3 0.6 %collective-permute-done.5.refs_3_ = f32[2,1,16,1024]{3,2,1,0:T(8,128)S(1)} collective-permute-done((f32[2,1,16,1024]{3,2,1,0:T(8,128)S(1)}, f32[2,1,16,1024]{3,2,1,0:T(8,128)S(1)}, u32[]{:S(2)}, u32[]{:S(2)}) %collective-permute-start.5) | collective-permute-done | bytes 131104 | tf_op jit(solution)/shard_map/ppermute | solution.py:416
  13.9 0.2 collective-permute-done.6.refs_5_
  14.1 0.3 %collective-permute-done.7.refs_9_ = f32[2,1,16,1024]{3,2,1,0:T(8,128)S(1)} collective-permute-done((f32[2,1,16,1024]{3,2,1,0:T(8,128)S(1)}, f32[2,1,16,1024]{3,2,1,0:T(8,128)S(1)}, u32[]{:S(2)}, u32[]{:S(2)}) %collective-permute-start.7) | collective-permute-done | bytes 131104 | tf_op jit(solution)/shard_map/ppermute | solution.py:416
  14.4 0.0 copy-done
  14.4 0.0 copy-done.2
  14.4 0.0 copy-done.3
  14.4 0.0 copy-done.4
  14.5 0.0 copy-done.5
  14.5 2.9 %pairs.2 = (f32[264,128]{1,0:T(8,128)S(1)}, f32[264,128]{1,0:T(8,128)S(1)}, f32[8,128]{1,0:T(8,128)S(1)}) custom-call(f32[2,1,16,1024]{3,2,1,0:T(8,128)S(1)} %copy-done, f32[2,1,16,1024]{3,2,1,0:T(8,128)S(1)} %collective-permute-done.refs_1_.refs_7_.refs_2_, f32[2,1,16,1024]{3,2,1,0:T(8,128)S(1)} %collective-permute-done.2.refs_2_, ...), custom_call_target="tpu_custom_call" | custom-call | flops 1 | bytes 1 | tf_op jit(solution)/shard_map/pairs/pallas_call | solution.py:360
  17.3 1.7 %collective-permute-start.10 = (f32[8,128]{1,0:T(8,128)S(1)}, f32[8,128]{1,0:T(8,128)S(1)}, u32[]{:S(2)}, u32[]{:S(2)}) collective-permute-start(f32[8,128]{1,0:T(8,128)S(1)} %get-tuple-element.21), channel_id=1, source_target_pairs={{0,3},{1,2},{2,1},{3,0},{4,7},{5,6},{6,5},{7,4},{8,11},{9,10},{10,... | collective-permute-start | bytes 12296 | tf_op jit(solution)/shard_map/ppermute | solution.py:453
  19.1 0.3 %collective-permute-start.8 = (f32[264,128]{1,0:T(8,128)S(1)}, f32[264,128]{1,0:T(8,128)S(1)}, u32[]{:S(2)}, u32[]{:S(2)}) collective-permute-start(f32[264,128]{1,0:T(8,128)S(1)} %get-tuple-element.20), channel_id=1, source_target_pairs={{0,2},{2,0},{4,6},{6,4},{8,10},{10,8},{12,14},{14,12},{1,3},{3,1},... | collective-permute-start | bytes 405512 | tf_op jit(solution)/shard_map/ppermute | solution.py:450
  19.4 0.0 collective-permute-done.9.refs_0_
  19.4 1.1 %collective-permute-done.10.refs_9_ = f32[8,128]{1,0:T(8,128)S(1)} collective-permute-done((f32[8,128]{1,0:T(8,128)S(1)}, f32[8,128]{1,0:T(8,128)S(1)}, u32[]{:S(2)}, u32[]{:S(2)}) %collective-permute-start.10) | collective-permute-done | bytes 4128 | tf_op jit(solution)/shard_map/ppermute | solution.py:453
  20.4 1.0 %pairs.3 = (f32[264,128]{1,0:T(8,128)S(1)}, f32[136,128]{1,0:T(8,128)S(1)}, f32[128,128]{1,0:T(8,128)S(1)}) custom-call(f32[4,1,16,1024]{3,2,1,0:T(8,128)S(1)} %collective-permute-done.9.refs_0_, f32[2,1,16,1024]{3,2,1,0:T(8,128)S(1)} %copy-done, f32[2,1,16,1024]{3,2,1,0:T(8,128)S(1)} %collective-permute-done.refs_1_.refs_7_.refs_2_, ...), custom_call_target="tpu_custom_call" | custom-call | flops 2000000000 | bytes 4194304 | tf_op jit(solution)/shard_map/pairs/pallas_call | solution.py:360
  21.4 0.3 %collective-permute-start.11 = (f32[136,128]{1,0:T(8,128)S(1)}, f32[136,128]{1,0:T(8,128)S(1)}, u32[]{:S(2)}, u32[]{:S(2)}) collective-permute-start(f32[136,128]{1,0:T(8,128)S(1)} %get-tuple-element.24), channel_id=1, source_target_pairs={{0,1},{1,0},{2,3},{3,2},{4,5},{5,4},{6,7},{7,6},{8,9},{9,8},{10,11... | collective-permute-start | bytes 208904 | tf_op jit(solution)/shard_map/ppermute | solution.py:416
  21.7 0.2 collective-permute-start.12
  22.0 1.0 %collective-permute-done.12.refs_4_ = f32[128,128]{1,0:T(8,128)S(1)} collective-permute-done((f32[128,128]{1,0:T(8,128)S(1)}, f32[128,128]{1,0:T(8,128)S(1)}, u32[]{:S(2)}, u32[]{:S(2)}) %collective-permute-start.12) | collective-permute-done | bytes 65568 | tf_op jit(solution)/shard_map/ppermute | solution.py:416
  23.0 0.0 collective-permute-done.11.refs_3_
  23.0 1.9 %collective-permute-done.8.refs_1_ = f32[264,128]{1,0:T(8,128)S(1)} collective-permute-done((f32[264,128]{1,0:T(8,128)S(1)}, f32[264,128]{1,0:T(8,128)S(1)}, u32[]{:S(2)}, u32[]{:S(2)}) %collective-permute-start.8) | collective-permute-done | bytes 135200 | tf_op jit(solution)/shard_map/ppermute | solution.py:450
  24.9 0.7 %join.1 = (f32[2,1,16,1024]{3,2,1,0:T(8,128)}, f32[1,1,2]{2,1,0:T(1,128)}) custom-call(f32[264,128]{1,0:T(8,128)S(1)} %get-tuple-element.19.refs_8_.refs_0_, f32[264,128]{1,0:T(8,128)S(1)} %collective-permute-done.8.refs_1_, f32[264,128]{1,0:T(8,128)S(1)} %get-tuple-element.23.refs_2_, f32[136,128]{1,0:T(8,128)S(1)} %collective-permute-done.11.refs_3_, ...), custom_call_target="tpu_custom_call" | custom-call | flops 1 | bytes 1 | tf_op jit(solution)/shard_map/join/pallas_call | solution.py:382
Async XLA Ops:
  0.6 9.0 %copy-start.1 = (f32[8,32,512]{2,1,0:T(8,128)S(1)}, f32[8,32,512]{2,1,0:T(8,128)}, u32[]{:S(2)}) copy-start(f32[8,32,512]{2,1,0:T(8,128)} %mine_ref.1) | copy-start | bytes 1572868
  0.6 9.0 %collective-permute-start.4 = (f32[8,32,512]{2,1,0:T(8,128)}, f32[8,32,512]{2,1,0:T(8,128)S(1)}, u32[]{:S(2)}, u32[]{:S(2)}) collective-permute-start(f32[8,32,512]{2,1,0:T(8,128)} %mine_ref.1), channel_id=1, source_target_pairs={{0,1},{1,0},{2,3},{3,2},{4,5},{5,4},{6,7},{7,6},{8,9},{9,8},{10,11... | collective-permute-start | bytes 1572872 | tf_op jit(solution)/shard_map/ppermute | solution.py:416
  1.2 7.2 %collective-permute-start = (f32[2,1,16,1024]{3,2,1,0:T(8,128)}, f32[2,1,16,1024]{3,2,1,0:T(8,128)S(1)}, u32[]{:S(2)}, u32[]{:S(2)}) collective-permute-start(f32[2,1,16,1024]{3,2,1,0:T(8,128)} %refs_1_.1), channel_id=1, source_target_pairs={{0,1},{1,0},{2,3},{3,2},{4,5},{5,4},{6,7},{7,6},{8,9},{9,8},{10,11... | collective-permute-start | bytes 393224 | tf_op jit(solution)/shard_map/ppermute | solution.py:416
  1.2 11.3 %collective-permute-start.1 = (f32[2,1,16,1024]{3,2,1,0:T(8,128)}, f32[2,1,16,1024]{3,2,1,0:T(8,128)S(1)}, u32[]{:S(2)}, u32[]{:S(2)}) collective-permute-start(f32[2,1,16,1024]{3,2,1,0:T(8,128)} %refs_1_.1), channel_id=1, source_target_pairs={{0,8},{2,10},{4,12},{6,14},{8,0},{10,2},{12,4},{14,6},{1,9},{3,11}... | collective-permute-start | bytes 393224 | tf_op jit(solution)/shard_map/ppermute | solution.py:419
  5.3 7.3 %collective-permute-start.2 = (f32[2,1,16,1024]{3,2,1,0:T(8,128)}, f32[2,1,16,1024]{3,2,1,0:T(8,128)S(1)}, u32[]{:S(2)}, u32[]{:S(2)}) collective-permute-start(f32[2,1,16,1024]{3,2,1,0:T(8,128)} %refs_1_.1), channel_id=1, source_target_pairs={{0,4},{2,6},{4,0},{6,2},{8,12},{10,14},{12,8},{14,10},{1,5},{3,7},... | collective-permute-start | bytes 393224 | tf_op jit(solution)/shard_map/ppermute | solution.py:419
  6.8 5.7 %collective-permute-start.3 = (f32[2,1,16,1024]{3,2,1,0:T(8,128)}, f32[2,1,16,1024]{3,2,1,0:T(8,128)S(1)}, u32[]{:S(2)}, u32[]{:S(2)}) collective-permute-start(f32[2,1,16,1024]{3,2,1,0:T(8,128)} %refs_1_.1), channel_id=1, source_target_pairs={{0,2},{2,0},{4,6},{6,4},{8,10},{10,8},{12,14},{14,12},{1,3},{3,1},... | collective-permute-start | bytes 393224 | tf_op jit(solution)/shard_map/ppermute | solution.py:428
  9.3 5.1 %copy-start = (f32[2,1,16,1024]{3,2,1,0:T(8,128)S(1)}, f32[2,1,16,1024]{3,2,1,0:T(8,128)}, u32[]{:S(2)}) copy-start(f32[2,1,16,1024]{3,2,1,0:T(8,128)} %refs_1_.1) | copy-start | bytes 393220
  9.3 5.1 %copy-start.2 = (bf16[2,256,256]{2,1,0:T(8,128)(2,1)S(1)}, bf16[2,256,256]{2,1,0:T(8,128)(2,1)}, u32[]{:S(2)}) copy-start(bf16[2,256,256]{2,1,0:T(8,128)(2,1)} %constant.8.clone.refs_11_.refs_4_) | copy-start | bytes 786436
  9.3 5.1 %copy-start.3 = (bf16[2,256,256]{2,1,0:T(8,128)(2,1)S(1)}, bf16[2,256,256]{2,1,0:T(8,128)(2,1)}, u32[]{:S(2)}) copy-start(bf16[2,256,256]{2,1,0:T(8,128)(2,1)} %constant.9.clone.refs_12_.refs_5_) | copy-start | bytes 786436
  9.3 5.1 %copy-start.4 = (f32[8,2,8,128]{3,2,1,0:T(8,128)S(1)}, f32[8,2,8,128]{3,2,1,0:T(8,128)}, u32[]{:S(2)}) copy-start(f32[8,2,8,128]{3,2,1,0:T(8,128)} %constant.10.clone.refs_13_.refs_6_) | copy-start | bytes 196612
  9.4 5.1 %copy-start.5 = (f32[2,16,128]{2,1,0:T(8,128)S(1)}, f32[2,16,128]{2,1,0:T(8,128)}, u32[]{:S(2)}) copy-start(f32[2,16,128]{2,1,0:T(8,128)} %constant.11.clone.refs_14_.refs_7_) | copy-start | bytes 49156
  9.4 10.0 %collective-permute-start.9 = (f32[4,1,16,1024]{3,2,1,0:T(8,128)S(1)}, f32[4,1,16,1024]{3,2,1,0:T(8,128)S(1)}, u32[]{:S(2)}, u32[]{:S(2)}) collective-permute-start(f32[4,1,16,1024]{3,2,1,0:T(8,128)S(1)} %pad_maximum_fusion), channel_id=1, source_target_pairs={{0,12},{1,15},{2,14},{3,13},{4,8},{5,11},{6,10},{7,9},{8,4},{9,7},... | collective-permute-start | bytes 786440 | tf_op jit(solution)/shard_map/ppermute | solution.py:447
  9.7 0.7 %copy-start.6 = (s32[8,8]{1,0:T(8,128)S(1)}, s32[8,8]{1,0:T(8,128)}, u32[]{:S(2)}) copy-start(s32[8,8]{1,0:T(8,128)} %q_ref.1) | copy-start | bytes 772
  10.4 0.7 %copy-start.7 = (s32[8]{0:T(128)S(1)}, s32[8]{0:T(128)}, u32[]{:S(2)}) copy-start(s32[8]{0:T(128)} %owner_ref.1) | copy-start | bytes 100
  12.6 1.4 %collective-permute-start.5 = (f32[2,1,16,1024]{3,2,1,0:T(8,128)S(1)}, f32[2,1,16,1024]{3,2,1,0:T(8,128)S(1)}, u32[]{:S(2)}, u32[]{:S(2)}) collective-permute-start(f32[2,1,16,1024]{3,2,1,0:T(8,128)S(1)} %collective-permute-done.2.refs_2_), channel_id=1, source_target_pairs={{0,1},{1,0},{2,3},{3,2},{4,5},{5,4},{6,7},{7,6},{8,9},{9,8},{10,11... | collective-permute-start | bytes 393224 | tf_op jit(solution)/shard_map/ppermute | solution.py:416
  12.8 1.3 %collective-permute-start.6 = (f32[2,1,16,1024]{3,2,1,0:T(8,128)S(1)}, f32[2,1,16,1024]{3,2,1,0:T(8,128)S(1)}, u32[]{:S(2)}, u32[]{:S(2)}) collective-permute-start(f32[2,1,16,1024]{3,2,1,0:T(8,128)S(1)} %collective-permute-done.1.refs_4_), channel_id=1, source_target_pairs={{0,1},{1,0},{2,3},{3,2},{4,5},{5,4},{6,7},{7,6},{8,9},{9,8},{10,11... | collective-permute-start | bytes 393224 | tf_op jit(solution)/shard_map/ppermute | solution.py:416
  13.1 1.3 %collective-permute-start.7 = (f32[2,1,16,1024]{3,2,1,0:T(8,128)S(1)}, f32[2,1,16,1024]{3,2,1,0:T(8,128)S(1)}, u32[]{:S(2)}, u32[]{:S(2)}) collective-permute-start(f32[2,1,16,1024]{3,2,1,0:T(8,128)S(1)} %collective-permute-done.3.refs_8_), channel_id=1, source_target_pairs={{0,1},{1,0},{2,3},{3,2},{4,5},{5,4},{6,7},{7,6},{8,9},{9,8},{10,11... | collective-permute-start | bytes 393224 | tf_op jit(solution)/shard_map/ppermute | solution.py:416
  17.3 3.1 %collective-permute-start.10 = (f32[8,128]{1,0:T(8,128)S(1)}, f32[8,128]{1,0:T(8,128)S(1)}, u32[]{:S(2)}, u32[]{:S(2)}) collective-permute-start(f32[8,128]{1,0:T(8,128)S(1)} %get-tuple-element.21), channel_id=1, source_target_pairs={{0,3},{1,2},{2,1},{3,0},{4,7},{5,6},{6,5},{7,4},{8,11},{9,10},{10,... | collective-permute-start | bytes 12296 | tf_op jit(solution)/shard_map/ppermute | solution.py:453
  19.1 5.8 %collective-permute-start.8 = (f32[264,128]{1,0:T(8,128)S(1)}, f32[264,128]{1,0:T(8,128)S(1)}, u32[]{:S(2)}, u32[]{:S(2)}) collective-permute-start(f32[264,128]{1,0:T(8,128)S(1)} %get-tuple-element.20), channel_id=1, source_target_pairs={{0,2},{2,0},{4,6},{6,4},{8,10},{10,8},{12,14},{14,12},{1,3},{3,1},... | collective-permute-start | bytes 405512 | tf_op jit(solution)/shard_map/ppermute | solution.py:450
  21.4 1.6 %collective-permute-start.11 = (f32[136,128]{1,0:T(8,128)S(1)}, f32[136,128]{1,0:T(8,128)S(1)}, u32[]{:S(2)}, u32[]{:S(2)}) collective-permute-start(f32[136,128]{1,0:T(8,128)S(1)} %get-tuple-element.24), channel_id=1, source_target_pairs={{0,1},{1,0},{2,3},{3,2},{4,5},{5,4},{6,7},{7,6},{8,9},{9,8},{10,11... | collective-permute-start | bytes 208904 | tf_op jit(solution)/shard_map/ppermute | solution.py:416
  21.7 1.3 %collective-permute-start.12 = (f32[128,128]{1,0:T(8,128)S(1)}, f32[128,128]{1,0:T(8,128)S(1)}, u32[]{:S(2)}, u32[]{:S(2)}) collective-permute-start(f32[128,128]{1,0:T(8,128)S(1)} %get-tuple-element.25), channel_id=1, source_target_pairs={{0,1},{1,0},{2,3},{3,2},{4,5},{5,4},{6,7},{7,6},{8,9},{9,8},{10,11... | collective-permute-start | bytes 196616 | tf_op jit(solution)/shard_map/ppermute | solution.py:416

commit v8 on v7

--- a/solution.py
+++ b/solution.py
@@ -11,6 +11,7 @@
 
 NK = 8
 SUBLANES = 8
+MARGIN = 24
 STEP = 9
 GROUP = 4
 LANES = 128
@@ -138,7 +139,7 @@
     lane_f, lane_b, twist, turn = take(4)
     sums = take(2) if has_sum else None
     before = take(2) if late else None
-    outs = take(3)
+    outs = take(2 if late else 3)
     x_re, x_im, high_ref, low_ref, f_ref, back_high, back_low, g_ref = take(8)
     if late:
         partners = [[whole.at[0:2], whole.at[2:4]] for (whole,) in partners]
@@ -268,12 +269,8 @@
                     t_re, t_im = field(target, h, block, t)
                     gram_re += t_re * re + t_im * im
                     gram_im += t_re * im - t_im * re
-                    if late and h:
-                        outs[1][pl.ds(t * half + x, SUBLANES), :] = re
-                        outs[2][pl.ds(t * half + x, SUBLANES), :] = im
-                    else:
-                        outs[c][pl.ds(t * half + x, SUBLANES), :] = re
-                        outs[c][pl.ds((tiles + t) * half + x, SUBLANES), :] = im
+                    outs[h + c][pl.ds(t * half + x, SUBLANES), :] = re
+                    outs[h + c][pl.ds((tiles + t) * half + x, SUBLANES), :] = im
         end = 2 * tiles * half
         scale = 1.0 / side**3
         sums_row = jnp.concatenate(
@@ -286,10 +283,11 @@
         if late:
             sums_row += before[0][pl.ds(end, 8), :] + before[1][...]
             outs[0][pl.ds(end, 8), :] = sums_row
-            outs[1][pl.ds(end // 2, 8), :] = sums_row
+            outs[1][pl.ds(end, 8), :] = sums_row
         else:
             outs[c][pl.ds(end, 8), :] = sums_row
             if c:
+                outs[1][pl.ds(end + 8, MARGIN), :] = jnp.zeros((MARGIN, LANES), F32)
                 outs[2][...] = sums_row
 
 
@@ -302,10 +300,10 @@
             at = pl.ds((k * tiles + t) * half, half)
             found = home[at, :] + away[at, :]
             if late:
-                found += late[0][at, :] + late[1 + k][pl.ds(t * half, half), :]
+                found += late[0][at, :] + late[1][at, :]
             applied_ref[k, 0, :, lane_slice(t)] = found
     if late:
-        gram = late[0][pl.ds(2 * tiles * half, 8), :] + late[1][pl.ds(tiles * half, 8), :]
+        gram = late[0][pl.ds(2 * tiles * half, 8), :] + late[1][pl.ds(2 * tiles * half, 8), :]
     else:
         gram = home[pl.ds(2 * tiles * half, 8), :]
     gram_ref[0, 0, 0] = jnp.max(gram[0:1, :])
@@ -355,7 +353,7 @@
     operands = [x for pair in partners for x in pair] + [x for pair in targets for x in pair]
     operands += [weights, *tables, *sums, *before]
     size = 2 * tiles * half + 8
-    sizes = [size, tiles * half + 8, tiles * half] if late else [size, size, 8]
+    sizes = [size, size] if late else [size, size + MARGIN, 8]
     messages = tuple(jax.ShapeDtypeStruct((n, LANES), F32) for n in sizes)
     return pl.pallas_call(
         functools.partial(pair_kernel, side, count, at_weights, late, len(sums) > 0),

time: 26.1 us -> 26 us (level); the launches traced: 25.6 us -> 25.8 us
  waiting for transfers between devices: 5.27 us -> 5.78 us
    ppermute x1, waiting for transfers between devices: 1.9 us -> 2.34 us  [on_device(): parts = [home, lax.ppermute(away, 'kb', across)]]
    ppermute x7 -> x6, starting transfers between devices: 1.9 us -> 1.65 us  [swap(): return lax.ppermute(x, 'slab', [(0, 1), (1, 0)])]
    ppermute x7 -> x6, waiting for transfers between devices: 2.15 us -> 2.23 us  [swap(): return lax.ppermute(x, 'slab', [(0, 1), (1, 0)])]
  transfers between devices with their start and end apart: 13 -> 12, of which waited for: 7 -> 7; matrix products, arithmetic and copies ran while one was open for 4% -> 4% of each run, Pallas kernels for 20% -> 20%
where the time goes in v8:
time: 26 us; the launch traced here: 25.8 us
  starting transfers between devices  11.1 us (43%)
  Pallas kernels  5.89 us (23%)
  waiting for transfers between devices  5.78 us (22%)
  local copies, waits for them, and re-layouts  1.38 us (5%)
  other arithmetic  0.95 us (4%)
  between operations  0.74 us (3%)
    ppermute x2, starting transfers between devices, from_line(): lax.ppermute(x, 'kb', [(2 * a + c, 2 * (a ^ d) + c) for a in range(lines)...  5.59 us
    pallas_call x2, Pallas kernels, apply_pairs(): pl.pallas_call(functools.partial(pair_kernel, side, count, at_weights, la...  3.79 us
    ppermute x1, waiting for transfers between devices, on_device(): parts = [home, lax.ppermute(away, 'kb', across)]  2.34 us
    ppermute x6, waiting for transfers between devices, swap(): return lax.ppermute(x, 'slab', [(0, 1), (1, 0)])  2.23 us
    ppermute x1, starting transfers between devices, on_device(): crossed_sums = lax.ppermute(away_sums, ('kb', 'slab'), crossed)  1.75 us
    ppermute x6, starting transfers between devices, swap(): return lax.ppermute(x, 'slab', [(0, 1), (1, 0)])  1.65 us
    ppermute x1, starting transfers between devices, on_device(): arrived[0] = lax.ppermute(orbitals, 'kb', across)  1.52 us
    pallas_call x1, Pallas kernels, choose_weights(): pl.pallas_call(functools.partial(weight_kernel, side, blocks_per_k, order...  1.4 us
  transfers between devices with their start and end apart: 12, of which 7 were waited for; matrix products, arithmetic and copies ran while one was open for 4% of the time, Pallas kernels for 20%

profile of v8, /device:TPU:0, one launch (start us, length us, event | category | flops | bytes accessed | tf_op | source)
XLA Modules:
  0.0 25.8 jit_solution(7623573204033618441)
XLA Ops:
  0.6 0.0 copy-start.1
  0.6 0.5 %collective-permute-start.4 = (f32[8,32,512]{2,1,0:T(8,128)}, f32[8,32,512]{2,1,0:T(8,128)S(1)}, u32[]{:S(2)}, u32[]{:S(2)}) collective-permute-start(f32[8,32,512]{2,1,0:T(8,128)} %mine_ref.1), channel_id=1, source_target_pairs={{0,1},{1,0},{2,3},{3,2},{4,5},{5,4},{6,7},{7,6},{8,9},{9,8},{10,11... | collective-permute-start | bytes 1572872 | tf_op jit(solution)/shard_map/ppermute | solution.py:414
  1.2 0.1 collective-permute-start
  1.2 4.0 %collective-permute-start.1 = (f32[2,1,16,1024]{3,2,1,0:T(8,128)}, f32[2,1,16,1024]{3,2,1,0:T(8,128)S(1)}, u32[]{:S(2)}, u32[]{:S(2)}) collective-permute-start(f32[2,1,16,1024]{3,2,1,0:T(8,128)} %refs_1_.1), channel_id=1, source_target_pairs={{0,8},{2,10},{4,12},{6,14},{8,0},{10,2},{12,4},{14,6},{1,9},{3,11}... | collective-permute-start | bytes 393224 | tf_op jit(solution)/shard_map/ppermute | solution.py:417
  5.3 1.6 %collective-permute-start.2 = (f32[2,1,16,1024]{3,2,1,0:T(8,128)}, f32[2,1,16,1024]{3,2,1,0:T(8,128)S(1)}, u32[]{:S(2)}, u32[]{:S(2)}) collective-permute-start(f32[2,1,16,1024]{3,2,1,0:T(8,128)} %refs_1_.1), channel_id=1, source_target_pairs={{0,4},{2,6},{4,0},{6,2},{8,12},{10,14},{12,8},{14,10},{1,5},{3,7},... | collective-permute-start | bytes 393224 | tf_op jit(solution)/shard_map/ppermute | solution.py:417
  6.8 1.5 %collective-permute-start.3 = (f32[2,1,16,1024]{3,2,1,0:T(8,128)}, f32[2,1,16,1024]{3,2,1,0:T(8,128)S(1)}, u32[]{:S(2)}, u32[]{:S(2)}) collective-permute-start(f32[2,1,16,1024]{3,2,1,0:T(8,128)} %refs_1_.1), channel_id=1, source_target_pairs={{0,2},{2,0},{4,6},{6,4},{8,10},{10,8},{12,14},{14,12},{1,3},{3,1},... | collective-permute-start | bytes 393224 | tf_op jit(solution)/shard_map/ppermute | solution.py:426
  8.3 0.0 collective-permute-done.refs_1_.refs_7_.refs_2_
  8.4 1.0 %pad_maximum_fusion = f32[4,1,16,1024]{3,2,1,0:T(8,128)S(1)} fusion(f32[2,1,16,1024]{3,2,1,0:T(8,128)S(1)} %collective-permute-done.refs_1_.refs_7_.refs_2_, f32[2,1,16,1024]{3,2,1,0:T(8,128)} %refs_1_.1), kind=kLoop, calls=%fused_computation | loop fusion | flops 65536 | bytes 524288 | tf_op jit(solution)/shard_map/concatenate | solution.py:445
  9.3 0.0 copy-start
  9.3 0.0 copy-start.2
  9.3 0.0 copy-start.3
  9.3 0.0 copy-start.4
  9.4 0.0 copy-start.5
  9.4 0.3 %collective-permute-start.9 = (f32[4,1,16,1024]{3,2,1,0:T(8,128)S(1)}, f32[4,1,16,1024]{3,2,1,0:T(8,128)S(1)}, u32[]{:S(2)}, u32[]{:S(2)}) collective-permute-start(f32[4,1,16,1024]{3,2,1,0:T(8,128)S(1)} %pad_maximum_fusion), channel_id=1, source_target_pairs={{0,12},{1,15},{2,14},{3,13},{4,8},{5,11},{6,10},{7,9},{8,4},{9,7},... | collective-permute-start | bytes 786440 | tf_op jit(solution)/shard_map/ppermute | solution.py:445
  9.7 0.0 collective-permute-done.4.other_ref
  9.7 0.0 copy-done.1
  9.7 0.0 copy-start.6
  9.7 0.7 %copy-done.6 = s32[8,8]{1,0:T(8,128)S(1)} copy-done((s32[8,8]{1,0:T(8,128)S(1)}, s32[8,8]{1,0:T(8,128)}, u32[]{:S(2)}) %copy-start.6) | copy-done | bytes 280
  10.4 0.0 copy-start.7
  10.4 0.7 %copy-done.7 = s32[8]{0:T(128)S(1)} copy-done((s32[8]{0:T(128)S(1)}, s32[8]{0:T(128)}, u32[]{:S(2)}) %copy-start.7) | copy-done | bytes 56
  11.0 1.4 %weights.1.refs_10_.refs_3_ = f32[7,256,128]{2,1,0:T(8,128)S(1)} custom-call(s32[8,8]{1,0:T(8,128)S(1)} %copy-done.6, s32[8]{0:T(128)S(1)} %copy-done.7, f32[8,32,512]{2,1,0:T(8,128)S(1)} %copy-done.1, f32[8,32,512]{2,1,0:T(8,128)S(1)} %collective-permute-done.4.other_ref), custom_call_target="tpu_custom_call" | custom-call | flops 1 | bytes 1 | tf_op jit(solution)/shard_map/weights/pallas_call | solution.py:328
  12.4 0.1 collective-permute-done.1.refs_4_
  12.6 0.0 collective-permute-done.2.refs_2_
  12.6 0.0 collective-permute-done.3.refs_8_
  12.6 0.2 collective-permute-start.5
  12.8 0.3 %collective-permute-start.6 = (f32[2,1,16,1024]{3,2,1,0:T(8,128)S(1)}, f32[2,1,16,1024]{3,2,1,0:T(8,128)S(1)}, u32[]{:S(2)}, u32[]{:S(2)}) collective-permute-start(f32[2,1,16,1024]{3,2,1,0:T(8,128)S(1)} %collective-permute-done.1.refs_4_), channel_id=1, source_target_pairs={{0,1},{1,0},{2,3},{3,2},{4,5},{5,4},{6,7},{7,6},{8,9},{9,8},{10,11... | collective-permute-start | bytes 393224 | tf_op jit(solution)/shard_map/ppermute | solution.py:414
  13.1 0.2 collective-permute-start.7
  13.3 0.6 %collective-permute-done.5.refs_3_ = f32[2,1,16,1024]{3,2,1,0:T(8,128)S(1)} collective-permute-done((f32[2,1,16,1024]{3,2,1,0:T(8,128)S(1)}, f32[2,1,16,1024]{3,2,1,0:T(8,128)S(1)}, u32[]{:S(2)}, u32[]{:S(2)}) %collective-permute-start.5) | collective-permute-done | bytes 131104 | tf_op jit(solution)/shard_map/ppermute | solution.py:414
  13.9 0.2 collective-permute-done.6.refs_5_
  14.1 0.3 %collective-permute-done.7.refs_9_ = f32[2,1,16,1024]{3,2,1,0:T(8,128)S(1)} collective-permute-done((f32[2,1,16,1024]{3,2,1,0:T(8,128)S(1)}, f32[2,1,16,1024]{3,2,1,0:T(8,128)S(1)}, u32[]{:S(2)}, u32[]{:S(2)}) %collective-permute-start.7) | collective-permute-done | bytes 131104 | tf_op jit(solution)/shard_map/ppermute | solution.py:414
  14.4 0.0 copy-done
  14.4 0.0 copy-done.2
  14.4 0.0 copy-done.3
  14.4 0.0 copy-done.4
  14.5 0.0 copy-done.5
  14.5 2.8 %pairs.2 = (f32[264,128]{1,0:T(8,128)S(1)}, f32[288,128]{1,0:T(8,128)S(1)}, f32[8,128]{1,0:T(8,128)S(1)}) custom-call(f32[2,1,16,1024]{3,2,1,0:T(8,128)S(1)} %copy-done, f32[2,1,16,1024]{3,2,1,0:T(8,128)S(1)} %collective-permute-done.refs_1_.refs_7_.refs_2_, f32[2,1,16,1024]{3,2,1,0:T(8,128)S(1)} %collective-permute-done.2.refs_2_, ...), custom_call_target="tpu_custom_call" | custom-call | flops 1 | bytes 1 | tf_op jit(solution)/shard_map/pairs/pallas_call | solution.py:358
  17.3 1.7 %collective-permute-start.10 = (f32[8,128]{1,0:T(8,128)S(1)}, f32[8,128]{1,0:T(8,128)S(1)}, u32[]{:S(2)}, u32[]{:S(2)}) collective-permute-start(f32[8,128]{1,0:T(8,128)S(1)} %get-tuple-element.20), channel_id=1, source_target_pairs={{0,3},{1,2},{2,1},{3,0},{4,7},{5,6},{6,5},{7,4},{8,11},{9,10},{10,... | collective-permute-start | bytes 12296 | tf_op jit(solution)/shard_map/ppermute | solution.py:451
  19.0 0.3 %collective-permute-start.8 = (f32[288,128]{1,0:T(8,128)S(1)}, f32[288,128]{1,0:T(8,128)S(1)}, u32[]{:S(2)}, u32[]{:S(2)}) collective-permute-start(f32[288,128]{1,0:T(8,128)S(1)} %get-tuple-element.19), channel_id=1, source_target_pairs={{0,2},{2,0},{4,6},{6,4},{8,10},{10,8},{12,14},{14,12},{1,3},{3,1},... | collective-permute-start | bytes 442376 | tf_op jit(solution)/shard_map/ppermute | solution.py:448
  19.3 0.0 collective-permute-done.9.refs_0_
  19.3 1.1 %collective-permute-done.10.refs_9_ = f32[8,128]{1,0:T(8,128)S(1)} collective-permute-done((f32[8,128]{1,0:T(8,128)S(1)}, f32[8,128]{1,0:T(8,128)S(1)}, u32[]{:S(2)}, u32[]{:S(2)}) %collective-permute-start.10) | collective-permute-done | bytes 4128 | tf_op jit(solution)/shard_map/ppermute | solution.py:451
  20.4 1.0 %pairs.3 = (f32[264,128]{1,0:T(8,128)S(1)}, f32[264,128]{1,0:T(8,128)S(1)}) custom-call(f32[4,1,16,1024]{3,2,1,0:T(8,128)S(1)} %collective-permute-done.9.refs_0_, f32[2,1,16,1024]{3,2,1,0:T(8,128)S(1)} %copy-done, f32[2,1,16,1024]{3,2,1,0:T(8,128)S(1)} %collective-permute-done.refs_1_.refs_7_.refs_2_, f32[7,256,128]{2,1,0:T(8,128)S(1)} %weights.1.refs_10_.refs_3_, ...), custom_call_target="tpu_custom_call" | custom-call | flops 2000000000 | bytes 4194304 | tf_op jit(solution)/shard_map/pairs/pallas_call | solution.py:358
  21.4 0.3 %collective-permute-start.11 = (f32[264,128]{1,0:T(8,128)S(1)}, f32[264,128]{1,0:T(8,128)S(1)}, u32[]{:S(2)}, u32[]{:S(2)}) collective-permute-start(f32[264,128]{1,0:T(8,128)S(1)} %get-tuple-element.23), channel_id=1, source_target_pairs={{0,1},{1,0},{2,3},{3,2},{4,5},{5,4},{6,7},{7,6},{8,9},{9,8},{10,11... | collective-permute-start | bytes 405512 | tf_op jit(solution)/shard_map/ppermute | solution.py:414
  21.7 1.1 %collective-permute-done.11.refs_3_ = f32[264,128]{1,0:T(8,128)S(1)} collective-permute-done((f32[264,128]{1,0:T(8,128)S(1)}, f32[264,128]{1,0:T(8,128)S(1)}, u32[]{:S(2)}, u32[]{:S(2)}) %collective-permute-start.11) | collective-permute-done | bytes 135200 | tf_op jit(solution)/shard_map/ppermute | solution.py:414
  22.8 2.3 %collective-permute-done.8.refs_1_ = f32[288,128]{1,0:T(8,128)S(1)} collective-permute-done((f32[288,128]{1,0:T(8,128)S(1)}, f32[288,128]{1,0:T(8,128)S(1)}, u32[]{:S(2)}, u32[]{:S(2)}) %collective-permute-start.8) | collective-permute-done | bytes 147488 | tf_op jit(solution)/shard_map/ppermute | solution.py:448
  25.1 0.7 %join.1 = (f32[2,1,16,1024]{3,2,1,0:T(8,128)}, f32[1,1,2]{2,1,0:T(1,128)}) custom-call(f32[264,128]{1,0:T(8,128)S(1)} %get-tuple-element.18.refs_8_.refs_0_, f32[288,128]{1,0:T(8,128)S(1)} %collective-permute-done.8.refs_1_, f32[264,128]{1,0:T(8,128)S(1)} %get-tuple-element.22.refs_2_, f32[264,128]{1,0:T(8,128)S(1)} %collective-permute-done.11.refs_3_), custom_call_target="tpu_custom_call" | custom-call | flops 1 | bytes 1 | tf_op jit(solution)/shard_map/join/pallas_call | solution.py:380
Async XLA Ops:
  0.6 9.0 %copy-start.1 = (f32[8,32,512]{2,1,0:T(8,128)S(1)}, f32[8,32,512]{2,1,0:T(8,128)}, u32[]{:S(2)}) copy-start(f32[8,32,512]{2,1,0:T(8,128)} %mine_ref.1) | copy-start | bytes 1572868
  0.6 9.0 %collective-permute-start.4 = (f32[8,32,512]{2,1,0:T(8,128)}, f32[8,32,512]{2,1,0:T(8,128)S(1)}, u32[]{:S(2)}, u32[]{:S(2)}) collective-permute-start(f32[8,32,512]{2,1,0:T(8,128)} %mine_ref.1), channel_id=1, source_target_pairs={{0,1},{1,0},{2,3},{3,2},{4,5},{5,4},{6,7},{7,6},{8,9},{9,8},{10,11... | collective-permute-start | bytes 1572872 | tf_op jit(solution)/shard_map/ppermute | solution.py:414
  1.2 7.2 %collective-permute-start = (f32[2,1,16,1024]{3,2,1,0:T(8,128)}, f32[2,1,16,1024]{3,2,1,0:T(8,128)S(1)}, u32[]{:S(2)}, u32[]{:S(2)}) collective-permute-start(f32[2,1,16,1024]{3,2,1,0:T(8,128)} %refs_1_.1), channel_id=1, source_target_pairs={{0,1},{1,0},{2,3},{3,2},{4,5},{5,4},{6,7},{7,6},{8,9},{9,8},{10,11... | collective-permute-start | bytes 393224 | tf_op jit(solution)/shard_map/ppermute | solution.py:414
  1.2 11.3 %collective-permute-start.1 = (f32[2,1,16,1024]{3,2,1,0:T(8,128)}, f32[2,1,16,1024]{3,2,1,0:T(8,128)S(1)}, u32[]{:S(2)}, u32[]{:S(2)}) collective-permute-start(f32[2,1,16,1024]{3,2,1,0:T(8,128)} %refs_1_.1), channel_id=1, source_target_pairs={{0,8},{2,10},{4,12},{6,14},{8,0},{10,2},{12,4},{14,6},{1,9},{3,11}... | collective-permute-start | bytes 393224 | tf_op jit(solution)/shard_map/ppermute | solution.py:417
  5.3 7.3 %collective-permute-start.2 = (f32[2,1,16,1024]{3,2,1,0:T(8,128)}, f32[2,1,16,1024]{3,2,1,0:T(8,128)S(1)}, u32[]{:S(2)}, u32[]{:S(2)}) collective-permute-start(f32[2,1,16,1024]{3,2,1,0:T(8,128)} %refs_1_.1), channel_id=1, source_target_pairs={{0,4},{2,6},{4,0},{6,2},{8,12},{10,14},{12,8},{14,10},{1,5},{3,7},... | collective-permute-start | bytes 393224 | tf_op jit(solution)/shard_map/ppermute | solution.py:417
  6.8 5.7 %collective-permute-start.3 = (f32[2,1,16,1024]{3,2,1,0:T(8,128)}, f32[2,1,16,1024]{3,2,1,0:T(8,128)S(1)}, u32[]{:S(2)}, u32[]{:S(2)}) collective-permute-start(f32[2,1,16,1024]{3,2,1,0:T(8,128)} %refs_1_.1), channel_id=1, source_target_pairs={{0,2},{2,0},{4,6},{6,4},{8,10},{10,8},{12,14},{14,12},{1,3},{3,1},... | collective-permute-start | bytes 393224 | tf_op jit(solution)/shard_map/ppermute | solution.py:426
  9.3 5.1 %copy-start = (f32[2,1,16,1024]{3,2,1,0:T(8,128)S(1)}, f32[2,1,16,1024]{3,2,1,0:T(8,128)}, u32[]{:S(2)}) copy-start(f32[2,1,16,1024]{3,2,1,0:T(8,128)} %refs_1_.1) | copy-start | bytes 393220
  9.3 5.1 %copy-start.2 = (bf16[2,256,256]{2,1,0:T(8,128)(2,1)S(1)}, bf16[2,256,256]{2,1,0:T(8,128)(2,1)}, u32[]{:S(2)}) copy-start(bf16[2,256,256]{2,1,0:T(8,128)(2,1)} %constant.8.clone.refs_11_.refs_4_) | copy-start | bytes 786436
  9.3 5.1 %copy-start.3 = (bf16[2,256,256]{2,1,0:T(8,128)(2,1)S(1)}, bf16[2,256,256]{2,1,0:T(8,128)(2,1)}, u32[]{:S(2)}) copy-start(bf16[2,256,256]{2,1,0:T(8,128)(2,1)} %constant.9.clone.refs_12_.refs_5_) | copy-start | bytes 786436
  9.3 5.1 %copy-start.4 = (f32[8,2,8,128]{3,2,1,0:T(8,128)S(1)}, f32[8,2,8,128]{3,2,1,0:T(8,128)}, u32[]{:S(2)}) copy-start(f32[8,2,8,128]{3,2,1,0:T(8,128)} %constant.10.clone.refs_13_.refs_6_) | copy-start | bytes 196612
  9.4 5.1 %copy-start.5 = (f32[2,16,128]{2,1,0:T(8,128)S(1)}, f32[2,16,128]{2,1,0:T(8,128)}, u32[]{:S(2)}) copy-start(f32[2,16,128]{2,1,0:T(8,128)} %constant.11.clone.refs_14_.refs_7_) | copy-start | bytes 49156
  9.4 10.0 %collective-permute-start.9 = (f32[4,1,16,1024]{3,2,1,0:T(8,128)S(1)}, f32[4,1,16,1024]{3,2,1,0:T(8,128)S(1)}, u32[]{:S(2)}, u32[]{:S(2)}) collective-permute-start(f32[4,1,16,1024]{3,2,1,0:T(8,128)S(1)} %pad_maximum_fusion), channel_id=1, source_target_pairs={{0,12},{1,15},{2,14},{3,13},{4,8},{5,11},{6,10},{7,9},{8,4},{9,7},... | collective-permute-start | bytes 786440 | tf_op jit(solution)/shard_map/ppermute | solution.py:445
  9.7 0.7 %copy-start.6 = (s32[8,8]{1,0:T(8,128)S(1)}, s32[8,8]{1,0:T(8,128)}, u32[]{:S(2)}) copy-start(s32[8,8]{1,0:T(8,128)} %q_ref.1) | copy-start | bytes 772
  10.4 0.7 %copy-start.7 = (s32[8]{0:T(128)S(1)}, s32[8]{0:T(128)}, u32[]{:S(2)}) copy-start(s32[8]{0:T(128)} %owner_ref.1) | copy-start | bytes 100
  12.6 1.4 %collective-permute-start.5 = (f32[2,1,16,1024]{3,2,1,0:T(8,128)S(1)}, f32[2,1,16,1024]{3,2,1,0:T(8,128)S(1)}, u32[]{:S(2)}, u32[]{:S(2)}) collective-permute-start(f32[2,1,16,1024]{3,2,1,0:T(8,128)S(1)} %collective-permute-done.2.refs_2_), channel_id=1, source_target_pairs={{0,1},{1,0},{2,3},{3,2},{4,5},{5,4},{6,7},{7,6},{8,9},{9,8},{10,11... | collective-permute-start | bytes 393224 | tf_op jit(solution)/shard_map/ppermute | solution.py:414
  12.8 1.3 %collective-permute-start.6 = (f32[2,1,16,1024]{3,2,1,0:T(8,128)S(1)}, f32[2,1,16,1024]{3,2,1,0:T(8,128)S(1)}, u32[]{:S(2)}, u32[]{:S(2)}) collective-permute-start(f32[2,1,16,1024]{3,2,1,0:T(8,128)S(1)} %collective-permute-done.1.refs_4_), channel_id=1, source_target_pairs={{0,1},{1,0},{2,3},{3,2},{4,5},{5,4},{6,7},{7,6},{8,9},{9,8},{10,11... | collective-permute-start | bytes 393224 | tf_op jit(solution)/shard_map/ppermute | solution.py:414
  13.1 1.3 %collective-permute-start.7 = (f32[2,1,16,1024]{3,2,1,0:T(8,128)S(1)}, f32[2,1,16,1024]{3,2,1,0:T(8,128)S(1)}, u32[]{:S(2)}, u32[]{:S(2)}) collective-permute-start(f32[2,1,16,1024]{3,2,1,0:T(8,128)S(1)} %collective-permute-done.3.refs_8_), channel_id=1, source_target_pairs={{0,1},{1,0},{2,3},{3,2},{4,5},{5,4},{6,7},{7,6},{8,9},{9,8},{10,11... | collective-permute-start | bytes 393224 | tf_op jit(solution)/shard_map/ppermute | solution.py:414
  17.3 3.1 %collective-permute-start.10 = (f32[8,128]{1,0:T(8,128)S(1)}, f32[8,128]{1,0:T(8,128)S(1)}, u32[]{:S(2)}, u32[]{:S(2)}) collective-permute-start(f32[8,128]{1,0:T(8,128)S(1)} %get-tuple-element.20), channel_id=1, source_target_pairs={{0,3},{1,2},{2,1},{3,0},{4,7},{5,6},{6,5},{7,4},{8,11},{9,10},{10,... | collective-permute-start | bytes 12296 | tf_op jit(solution)/shard_map/ppermute | solution.py:451
  19.0 6.1 %collective-permute-start.8 = (f32[288,128]{1,0:T(8,128)S(1)}, f32[288,128]{1,0:T(8,128)S(1)}, u32[]{:S(2)}, u32[]{:S(2)}) collective-permute-start(f32[288,128]{1,0:T(8,128)S(1)} %get-tuple-element.19), channel_id=1, source_target_pairs={{0,2},{2,0},{4,6},{6,4},{8,10},{10,8},{12,14},{14,12},{1,3},{3,1},... | collective-permute-start | bytes 442376 | tf_op jit(solution)/shard_map/ppermute | solution.py:448
  21.4 1.4 %collective-permute-start.11 = (f32[264,128]{1,0:T(8,128)S(1)}, f32[264,128]{1,0:T(8,128)S(1)}, u32[]{:S(2)}, u32[]{:S(2)}) collective-permute-start(f32[264,128]{1,0:T(8,128)S(1)} %get-tuple-element.23), channel_id=1, source_target_pairs={{0,1},{1,0},{2,3},{3,2},{4,5},{5,4},{6,7},{7,6},{8,9},{9,8},{10,11... | collective-permute-start | bytes 405512 | tf_op jit(solution)/shard_map/ppermute | solution.py:414
